TPU v7x, 32 devices: a whole 2x2x4 slice. The times are simulated.
32 devices in a mesh: dp: 16 (over z, y, x), ctx: 2 (over core).
Axes of the slice: x: 2, y: 2, z: 4, core: 2. Of those that a mesh axis runs over, the one named last changes fastest.
Arguments:
- queries: bfloat16 [16, 256, 128], P('dp', 'ctx'), may hold values from -6 to 6
- key_vectors: bfloat16 [16, 256, 128], P('dp', 'ctx'), may hold values from -6 to 6
- value_vectors: bfloat16 [16, 256, 128], P('dp', 'ctx'), may hold values from -6 to 6
- log_decay: float32 [16, 256, 128], P('dp', 'ctx'), may hold values from -2 to 0, as said below
- out_weight: bfloat16 [5120, 128], replicated, may hold values from -0.5 to 0.5
- cotangent: bfloat16 [16, 256, 5120], P('dp', 'ctx'), may hold values from -0.3984375 to 0.3984375
Outputs:
- grad_queries: bfloat16 [16, 256, 128], P('dp', 'ctx')
- grad_keys: bfloat16 [16, 256, 128], P('dp', 'ctx')
- grad_values: bfloat16 [16, 256, 128], P('dp', 'ctx')
- grad_decay: float32 [16, 256, 128], P('dp', 'ctx')
- grad_weight: float32 [5120, 128], P('dp')
Inputs may be any that keep to these rules, and one draw needn't show every extreme that they name: `log_decay`: every entry is negative.
All inputs are finite; a program needn't handle non-finite values.
Results may differ from a plain program's by a relative error of at most 0.0029.
Values sent between devices are 32-bit elements; how exact they have to be, the bound alone decides.
No kernel may reach another device: no remote copies, remote signals or barrier semaphores. Data moves between devices by JAX's collectives and lax.ppermute only.
A program may use at most 64 MiB of HBM per device.

v0:
```python
import jax
import jax.numpy as jnp
from jax import lax
from jax.sharding import PartitionSpec as P

DK = 128
HEADS = 1
BLK = 128


EPSILON = 1e-05
PRECISE = lax.Precision.HIGHEST


def shifted(value, axis, steps):
    count = lax.axis_size(axis)
    leading, last = (max(0, -steps), min(count, count - steps))
    return lax.ppermute(value, axis, [(source, source + steps) for source in range(leading, last)])


def body(queries, key_vectors, value_vectors, log_decay, out_weight, cotangent):
    length = queries.shape[1]
    blocks = length // BLK
    shaped = (blocks, BLK, HEADS, DK)
    query_blk = queries.reshape(shaped).astype(jnp.float32)
    key_blk = key_vectors.reshape(shaped).astype(jnp.float32)
    value_blk = value_vectors.reshape(shaped).astype(jnp.float32)
    decay_blk = log_decay.reshape(shaped)
    lower = jnp.tril(jnp.ones((BLK, BLK), jnp.float32))
    cumul = jnp.einsum("ij,njhc->nihc", lower, decay_blk, precision=PRECISE)
    totals = cumul[:, -1]
    rising = jnp.exp(cumul)
    falling = jnp.exp(-cumul)
    to_end = jnp.exp(totals[:, None] - cumul)
    query_scaled = query_blk * rising
    key_scaled = key_blk * falling
    key_to_end = key_blk * to_end
    scores = jnp.einsum("nihc,njhc->nhij", query_scaled, key_scaled, precision=PRECISE) * lower
    within = jnp.einsum("nhij,njhe->nihe", scores, value_blk, precision=PRECISE)
    block_states = jnp.einsum("njhc,njhe->nhce", key_to_end, value_blk, precision=PRECISE)

    def advance(carry, inputs):
        block_decay, block_state = inputs
        return (jnp.exp(block_decay)[..., None] * carry + block_state, carry)

    zero_state = jnp.zeros((HEADS, DK, DK), jnp.float32)
    local_state, zero_entries = lax.scan(advance, zero_state, (totals, block_states))
    before = jnp.cumsum(totals, axis=0) - totals
    device_decay = jnp.sum(totals, axis=0)
    after = device_decay - before - totals
    steps_count = lax.axis_size("ctx") - 1

    def pass_state(turn_index, incoming):
        return shifted(local_state + jnp.exp(device_decay)[..., None] * incoming, "ctx", 1)

    state_in = lax.fori_loop(0, steps_count, pass_state, zero_state)
    entries = zero_entries + jnp.exp(before)[..., None] * state_in
    across = jnp.einsum("nihc,nhce->nihe", query_scaled, entries, precision=PRECISE)
    output = within + across
    scale_inv = lax.rsqrt(jnp.mean(output * output, axis=-1, keepdims=True) + EPSILON)
    normed = output * scale_inv
    rounded = normed.reshape(length, HEADS * DK).astype(jnp.bfloat16)
    upstream = cotangent.reshape(length, cotangent.shape[2])
    row_share = lax.psum_scatter(
        jnp.einsum("td,tk->dk", upstream, rounded, preferred_element_type=jnp.float32),
        "dp",
        scatter_dimension=0,
        tiled=True,
    )
    grad_weight = lax.psum(row_share, "ctx")
    grad_normed = jnp.dot(upstream, out_weight, preferred_element_type=jnp.float32).reshape(shaped)
    grad_output = scale_inv * (
        grad_normed - normed * jnp.mean(grad_normed * normed, axis=-1, keepdims=True)
    )
    pairs = jnp.einsum("nihe,njhe->nhij", grad_output, value_blk, precision=PRECISE) * lower
    grad_query = rising * (
        jnp.einsum("nhij,njhc->nihc", pairs, key_scaled, precision=PRECISE)
        + jnp.einsum("nihe,nhce->nihc", grad_output, entries, precision=PRECISE)
    )
    block_grads = jnp.einsum("nihc,nihe->nhce", query_scaled, grad_output, precision=PRECISE)

    def retreat(carry, inputs):
        block_decay, block_grad = inputs
        return (block_grad + jnp.exp(block_decay)[..., None] * carry, carry)

    local_grad, zero_after = lax.scan(retreat, zero_state, (totals, block_grads), reverse=True)
    grad_key_zero = falling * jnp.einsum(
        "nhij,nihc->njhc", pairs, query_scaled, precision=PRECISE
    ) + to_end * jnp.einsum("nhce,njhe->njhc", zero_after, value_blk, precision=PRECISE)
    grad_value_zero = jnp.einsum(
        "nhij,nihe->njhe", scores, grad_output, precision=PRECISE
    ) + jnp.einsum("njhc,nhce->njhe", key_to_end, zero_after, precision=PRECISE)
    gate_zero = query_blk * grad_query - key_blk * grad_key_zero
    sigma_zero = jnp.sum(gate_zero, axis=(0, 1))

    def pass_grad(turn_index, carried):
        grad_in, later_sum = carried
        own_sum = sigma_zero - jnp.sum(grad_in * local_state, axis=-1)
        return shifted(
            (local_grad + jnp.exp(device_decay)[..., None] * grad_in, own_sum + later_sum),
            "ctx",
            -1,
        )

    grad_in, later_sum = lax.fori_loop(
        0, steps_count, pass_grad, (zero_state, jnp.zeros_like(sigma_zero))
    )
    reach = to_end * jnp.exp(after)[:, None]
    grad_key = grad_key_zero + reach * jnp.einsum(
        "hce,njhe->njhc", grad_in, value_blk, precision=PRECISE
    )
    grad_value = grad_value_zero + jnp.einsum(
        "njhc,hce->njhe", key_blk * reach, grad_in, precision=PRECISE
    )
    gate_full = query_blk * grad_query - key_blk * grad_key
    within_suffix = jnp.einsum("ij,njhc->nihc", jnp.transpose(lower), gate_full, precision=PRECISE)
    block_totals = jnp.sum(gate_full, axis=1)
    later_blocks = jnp.sum(block_totals, axis=0) - jnp.cumsum(block_totals, axis=0)
    grad_gate = within_suffix + later_blocks[:, None] + later_sum
    flat = (1, length, HEADS * DK)
    return (
        grad_query.reshape(flat).astype(jnp.bfloat16),
        grad_key.reshape(flat).astype(jnp.bfloat16),
        grad_value.reshape(flat).astype(jnp.bfloat16),
        grad_gate.reshape(flat),
        grad_weight,
    )


def solution(mesh):
    placed = (
        P("dp", "ctx", None),
        P("dp", "ctx", None),
        P("dp", "ctx", None),
        P("dp", "ctx", None),
        P(),
        P("dp", "ctx", None),
    )
    return jax.shard_map(
        body,
        mesh=mesh,
        in_specs=placed,
        out_specs=(
            P("dp", "ctx", None),
            P("dp", "ctx", None),
            P("dp", "ctx", None),
            P("dp", "ctx", None),
            P("dp", None),
        ),
        check_vma=False,
    )
```

profile of v0, /device:TPU:0, one launch (start us, length us, event | category | flops | bytes accessed | tf_op | source)
XLA Modules:
  0.0 130.8 jit_solution(8455345206534923816)
XLA Ops:
  7.2 0.0 copy-start
  7.2 0.0 reduce-scatter.4.cloned.1.call-start
  7.2 1.1 convolution_bitcast_fusion.8
  8.4 1.1 multiply_reduce_fusion
  9.5 2.4 %collective-permute-start = (f32[1,128,128]{2,1,0:T(8,128)S(1)}, f32[1,128,128]{2,1,0:T(8,128)S(1)}, u32[]{:S(2)}, u32[]{:S(2)}) collective-permute-start(f32[1,128,128]{2,1,0:T(8,128)S(1)} %get-tuple-element.74), channel_id=1, source_target_pairs={{0,1},{2,3},{4,5},{6,7},{8,9},{10,11},{12,13},{14,15},{16,17},{18,... | collective-permute-start | bytes 196616 | tf_op jit(solution)/shard_map/while/body/eval_jaxpr/ppermute | solution.py:18
  11.9 1.1 convolution_multiply_fusion.1
  12.9 1.0 convolution_bitcast_fusion.7
  13.9 0.0 collective-permute-done
  13.9 1.1 multiply_reduce_fusion.2
  15.1 0.0 copy-done
  15.1 2.0 %convolution_bitcast_fusion = f32[5120,128]{0,1:T(8,128)} fusion(bf16[1,128,5120]{2,1,0:T(8,128)(2,1)S(1)} %copy-done, f32[1,1,128,128]{3,2,1,0:T(8,128)S(1)} %get-tuple-element.89, f32[128]{0:T(128)S(1)} %add_rsqrt_fusion), kind=kOutput, calls=%fused_computation | convolution fusion | flops 167804928 | bytes 3998208 | tf_op jit(solution)/shard_map/td,tk->dk/dot_general | solution.py:65
  17.1 3.2 %copy.20 = f32[5120,128]{1,0:T(8,128)} copy(f32[5120,128]{0,1:T(8,128)} %convolution_bitcast_fusion) | data formatting | bytes 5242880
  20.4 0.0 copy-start.1
  20.4 0.0 copy-start.4
  20.4 0.0 copy-start.2
  20.4 0.0 reduce-scatter.4.cloned.1.call-update
  20.4 0.0 all-reduce.2.cloned.1.call-start
  20.4 0.7 copy-done.1
  21.1 0.1 multiply_reduce_fusion.1
  21.2 0.0 copy-done.4
  21.2 0.2 fusion.12
  21.4 0.3 copy-done.2
  21.7 0.0 copy-start.3
  21.7 0.6 fusion.39
  22.4 0.1 copy-done.3
  22.5 0.3 fusion.4
  22.8 1.3 collective-permute-start.1
  24.1 0.3 convolution_multiply_fusion
  24.3 0.2 fusion.47
  24.5 0.3 fusion.6
  24.8 0.3 fusion.19
  25.2 0.2 fusion.16
  25.4 0.5 collective-permute-done.1
  25.9 0.2 fusion.14
  26.1 0.7 fusion.87
  26.8 1.3 collective-permute-start.2
  28.1 76.6 %reduce-scatter.4.cloned.1.call-done = f32[320,128]{1,0:T(8,128)} async-done(((f32[5120,128]{1,0:T(8,128)}), f32[320,128]{1,0:T(8,128)}) %reduce-scatter.4.cloned.1.call-update) | async-done | bytes 163856
  104.7 1.7 %copy.21 = f32[320,128]{0,1:T(8,128)} copy(f32[320,128]{1,0:T(8,128)} %reduce-scatter.4.cloned.1.call-done) | data formatting | bytes 327680
  106.4 0.0 all-reduce.2.cloned.1.call-update
  106.5 0.3 fusion.21
  106.8 0.7 copy.16
  107.5 0.0 collective-permute-done.2
  107.5 0.3 add_bitcast_fusion
  107.8 0.7 copy.17
  108.5 13.8 %all-reduce.2.cloned.1.call-done = f32[320,128]{0,1:T(8,128)} async-done(((f32[320,128]{0,1:T(8,128)}), f32[320,128]{0,1:T(8,128)}) %all-reduce.2.cloned.1.call-update) | async-done | bytes 163856 | tf_op jit(solution)/shard_map/psum | solution.py:70
  122.3 1.7 %copy.18 = f32[320,128]{1,0:T(8,128)} copy(f32[320,128]{0,1:T(8,128)} %all-reduce.2.cloned.1.call-done) | data formatting | bytes 327680
  (7 shorter events, 0.1 us)
Async XLA Ops:
  7.2 7.9 %copy-start = (bf16[1,128,5120]{2,1,0:T(8,128)(2,1)S(1)}, bf16[1,128,5120]{2,1,0:T(8,128)(2,1)}, u32[]{:S(2)}) copy-start(bf16[1,128,5120]{2,1,0:T(8,128)(2,1)} %param.11) | copy-start | bytes 3932164
  7.2 97.5 %reduce-scatter.4.cloned.1.call-start = ((), (), s32[]{:S(2)}) async-start(), calls=%async_computation.2 | async-start | bytes 2785280
  9.5 4.4 %collective-permute-start = (f32[1,128,128]{2,1,0:T(8,128)S(1)}, f32[1,128,128]{2,1,0:T(8,128)S(1)}, u32[]{:S(2)}, u32[]{:S(2)}) collective-permute-start(f32[1,128,128]{2,1,0:T(8,128)S(1)} %get-tuple-element.74), channel_id=1, source_target_pairs={{0,1},{2,3},{4,5},{6,7},{8,9},{10,11},{12,13},{14,15},{16,17},{18,... | collective-permute-start | bytes 196616 | tf_op jit(solution)/shard_map/while/body/eval_jaxpr/ppermute | solution.py:18
  20.4 0.8 copy-start.1
  20.4 0.9 copy-start.4
  20.4 1.4 %copy-start.2 = (bf16[5120,128]{1,0:T(8,128)(2,1)S(1)}, bf16[5120,128]{1,0:T(8,128)(2,1)}, u32[]{:S(2)}) copy-start(bf16[5120,128]{1,0:T(8,128)(2,1)} %param.10) | copy-start | bytes 3932164
  20.4 101.9 %all-reduce.2.cloned.1.call-start = ((), (), s32[]{:S(2)}) async-start(), calls=%async_computation.1 | async-start | bytes 393216 | tf_op jit(solution)/shard_map/psum | solution.py:70
  21.7 0.8 copy-start.3
  22.8 3.1 %collective-permute-start.1 = (f32[1,128,128]{2,1,0:T(8,128)S(1)}, f32[1,128,128]{2,1,0:T(8,128)S(1)}, u32[]{:S(2)}, u32[]{:S(2)}) collective-permute-start(f32[1,128,128]{2,1,0:T(8,128)S(1)} %fusion.4), channel_id=1, source_target_pairs={{1,0},{3,2},{5,4},{7,6},{9,8},{11,10},{13,12},{15,14},{17,16},{19,... | collective-permute-start | bytes 196616 | tf_op jit(solution)/shard_map/while/body/eval_jaxpr/ppermute | solution.py:18
  26.8 80.7 %collective-permute-start.2 = (f32[1,128]{1,0:T(1,128)S(1)}, f32[1,128]{1,0:T(1,128)S(1)}, u32[]{:S(2)}, u32[]{:S(2)}) collective-permute-start(f32[1,128]{1,0:T(1,128)S(1)} %subtract_bitcast_fusion), channel_id=1, source_target_pairs={{1,0},{3,2},{5,4},{7,6},{9,8},{11,10},{13,12},{15,14},{17,16},{19,... | collective-permute-start | bytes 1544 | tf_op jit(solution)/shard_map/while/body/eval_jaxpr/ppermute | solution.py:18
Sparse Core Ops, SparseCore 0:
  20.5 84.1 reduce-scatter.3
  107.0 15.2 all-reduce.1
where the time goes:
time: 131 us
  waiting for transfers between devices  91 us (69%)
  between operations  14.2 us (11%)
  matrix products  10.6 us (8%)
  local copies, waits for them, and re-layouts  9.2 us (7%)
  starting transfers between devices  5.01 us (4%)
    unnamed x3, waiting for transfers between devices  76.7 us
    psum x1, waiting for transfers between devices, body(): grad_weight = lax.psum(row_share, 'ctx')  13.8 us
    unnamed x15, local copies, waits for them, and re-layouts  9.2 us
    ppermute x3, starting transfers between devices, shifted(): lax.ppermute(value, axis, [(source, source + steps) for source in range(l...  4.93 us
  transfers between devices with their start and end apart: 5, of which 3 were waited for; matrix products, arithmetic and copies ran while one was open for 7% of the time, Pallas kernels for 0%

commit v1 on v0

v1 whole, which is shorter than its diff:
```python
import functools

import jax
import jax.numpy as jnp
from jax import lax
from jax.experimental import pallas as pl
from jax.experimental.pallas import tpu as pltpu
from jax.sharding import PartitionSpec as P

EPSILON = 1e-05
VMEM_BYTES = 24 * 1024 * 1024
F32 = jnp.float32
BF16 = jnp.bfloat16
BOTH = ("dp", "ctx")


def split(value, parts):
    pieces = []
    for index in range(parts):
        piece = value.astype(BF16)
        pieces.append(piece)
        if index + 1 < parts:
            value = value - piece.astype(F32)
    return pieces


def product(left, right, left_axis, right_axis):
    dims = (((left_axis,), (right_axis,)), ((), ()))
    most = max(len(left), len(right))
    total = None
    for order in reversed(range(most)):
        for i, l in enumerate(left):
            j = order - i
            if 0 <= j < len(right):
                term = lax.dot_general(l, right[j], dims, preferred_element_type=F32)
                total = term if total is None else total + term
    return total


def lower_mask(length):
    rows = lax.broadcasted_iota(jnp.int32, (length, length), 0)
    columns = lax.broadcasted_iota(jnp.int32, (length, length), 1)
    return rows >= columns


def cumulate(decay):
    lower = lower_mask(decay.shape[0]).astype(F32).astype(BF16)
    return product([lower], split(decay, 3), 1, 0)


def state_kernel(key_ref, value_ref, decay_ref, state_ref):
    cumul = cumulate(decay_ref[0])
    to_end = jnp.exp(cumul[-1:] - cumul)
    key_to_end = key_ref[0].astype(F32) * to_end
    state_ref[...] = product(split(key_to_end, 2), [value_ref[0]], 0, 0)


def within_kernel(query_ref, key_ref, value_ref, decay_ref, within_ref, scores_ref, cumul_ref):
    cumul = cumulate(decay_ref[0])
    cumul_ref[...] = cumul
    query_scaled = query_ref[0].astype(F32) * jnp.exp(cumul)
    key_scaled = key_ref[0].astype(F32) * jnp.exp(-cumul)
    scores = product(split(query_scaled, 2), split(key_scaled, 2), 1, 1)
    scores = jnp.where(lower_mask(cumul.shape[0]), scores, 0.0)
    scores_ref[...] = scores
    within_ref[...] = product(split(scores, 2), [value_ref[0]], 1, 0)


def normed_kernel(query_ref, cumul_ref, within_ref, state_ref, normed_ref, scale_ref, rounded_ref):
    query_scaled = query_ref[0].astype(F32) * jnp.exp(cumul_ref[...])
    output = within_ref[...] + product(split(query_scaled, 2), split(state_ref[...], 2), 1, 0)
    scale_inv = lax.rsqrt(jnp.mean(output * output, axis=-1, keepdims=True) + EPSILON)
    normed = output * scale_inv
    normed_ref[...] = normed
    scale_ref[...] = jnp.broadcast_to(scale_inv, normed.shape)
    rounded_ref[...] = normed.astype(BF16).astype(F32)


def grads_kernel(
    query_ref, key_ref, value_ref, cumul_ref, scores_ref, state_ref, normed_ref, scale_ref,
    upstream_ref, weight_ref,
    grad_query_ref, grad_key_ref, grad_value_ref, gate_ref, sent_ref,
):
    query = query_ref[0].astype(F32)
    key = key_ref[0].astype(F32)
    value = value_ref[0]
    cumul = cumul_ref[...]
    rising = jnp.exp(cumul)
    falling = jnp.exp(-cumul)
    normed = normed_ref[...]
    grad_normed = jnp.dot(upstream_ref[0], weight_ref[...], preferred_element_type=F32)
    grad_output = scale_ref[...] * (
        grad_normed - normed * jnp.mean(grad_normed * normed, axis=-1, keepdims=True)
    )
    grad_output = split(grad_output, 2)
    query_scaled = split(query * rising, 2)
    key_scaled = split(key * falling, 2)
    pairs = product(grad_output, [value], 1, 1)
    pairs = split(jnp.where(lower_mask(cumul.shape[0]), pairs, 0.0), 2)
    grad_query = rising * (
        product(pairs, key_scaled, 1, 0) + product(grad_output, split(state_ref[...], 2), 1, 1)
    )
    grad_query_ref[0] = grad_query.astype(BF16)
    grad_key = falling * product(pairs, query_scaled, 0, 0)
    grad_key_ref[...] = grad_key
    grad_value_ref[...] = product(split(scores_ref[...], 2), grad_output, 0, 0)
    gate = query * grad_query - key * grad_key
    gate_ref[...] = gate
    width = query.shape[1]
    sent_ref[:width] = product(query_scaled, grad_output, 0, 0)
    sent_ref[width:] = jnp.broadcast_to(
        jnp.sum(gate, axis=0, keepdims=True), (sent_ref.shape[0] - width, width)
    )


def finish_kernel(
    key_ref, value_ref, cumul_ref, grad_key_ref, grad_value_ref, gate_ref, later_ref,
    key_out_ref, value_out_ref, decay_out_ref,
):
    key = key_ref[0].astype(F32)
    cumul = cumul_ref[...]
    width = key.shape[1]
    to_end = jnp.exp(cumul[-1:] - cumul)
    grad_in = split(later_ref[:width], 2)
    extra = to_end * product([value_ref[0]], grad_in, 1, 1)
    key_out_ref[0] = (grad_key_ref[...] + extra).astype(BF16)
    grad_value = grad_value_ref[...] + product(split(key * to_end, 2), grad_in, 1, 0)
    value_out_ref[0] = grad_value.astype(BF16)
    gate = gate_ref[...] - key * extra
    lower = lower_mask(cumul.shape[0]).astype(F32).astype(BF16)
    decay_out_ref[0] = product([lower], split(gate, 3), 0, 0) + later_ref[width:width + 1]


def local_call(kernel, shapes, *operands, name, flops, scratch=()):
    outs = [jax.ShapeDtypeStruct(shape, dtype) for shape, dtype in shapes]
    moved = sum(array.size * array.dtype.itemsize for array in [*operands, *outs])
    return pl.pallas_call(
        kernel,
        out_shape=outs,
        scratch_shapes=list(scratch),
        compiler_params=pltpu.CompilerParams(vmem_limit_bytes=VMEM_BYTES),
        cost_estimate=pl.CostEstimate(flops=flops, bytes_accessed=moved, transcendentals=0),
        name=name,
    )(*operands)


def swap(value):
    return lax.ppermute(value, "ctx", [(0, 1), (1, 0)])


def halving_plan(count, rows):
    bits = count.bit_length() - 1
    last = rows // 3 // 16 * 16
    rest = list(range(3, bits))
    return [
        (rows - last, ([0, 1, 2] + rest, [1, 0, 2] + rest)),
        (last, ([2, 0, 1] + rest, [2, 1, 0] + rest)),
    ]


def relative(place, order):
    top = len(order) - 1
    return sum(((place >> (top - step)) & 1) << bit for step, bit in enumerate(order))


def turn_kernel(count, plan, upstream_ref, state_ref, own_ref, send_ref, turned):
    del state_ref

    me, core = lax.axis_index("dp"), lax.axis_index("ctx")
    lanes = 128
    for start in range(0, turned.shape[0], lanes):
        block = upstream_ref[0, :, start:start + lanes].astype(F32)
        turned[start:start + lanes] = jnp.transpose(block)
    share = turned.shape[0] // count
    half = share // 2
    at = offset = 0
    for rows, orders in plan:
        for place in range(count):
            masks = [relative(place, order) for order in orders]
            for target, ref in ((core, own_ref), (1 - core, send_ref)):
                owner = me ^ (masks[0] + target * (masks[1] - masks[0]))
                begin = pl.multiple_of(owner * share + target * half + offset, 16)
                ref[at:at + rows] = turned[pl.ds(begin, rows)].astype(ref.dtype)
            at += rows
        offset += rows


def share_kernel(own_ref, received_ref, rounded_ref, other_ref, *outs):
    rounded = jnp.concatenate([rounded_ref[...], other_ref[...]], axis=0).astype(BF16)
    at = 0
    for out in outs:
        rows = out.shape[0]
        left = jnp.concatenate(
            [own_ref[at:at + rows], received_ref[at:at + rows].astype(BF16)], axis=1
        )
        out[...] = jnp.dot(left, rounded, preferred_element_type=F32)
        at += rows


def exchanged(value, count, bits):
    pairs = [
        (device * 2 + core, (device ^ (1 << bits[core])) * 2 + core)
        for device in range(count)
        for core in range(2)
    ]
    return lax.ppermute(value, BOTH, pairs)


def halving(chunks, plan, count, beside):
    beside = dict(beside)
    stages = len(plan[0][1][0])
    joined = 3
    for stage in range(joined):
        arrived = [
            exchanged(sent, count, [order[stage] for order in orders])
            for (_, sent), (_, orders) in zip(chunks, plan)
        ]
        if stage in beside:
            arrived[-1], beside[stage] = lax.optimization_barrier((arrived[-1], beside[stage]))
        chunks = [
            (kept[: len(kept) // 2] + new[: len(kept) // 2], kept[len(kept) // 2:] + new[len(kept) // 2:])
            if stage + 1 < stages
            else (kept + new, None)
            for (kept, _), new in zip(chunks, arrived)
        ]
    kept = [chunk[0] for chunk in chunks]
    sent = [chunk[1] for chunk in chunks]
    for stage in range(joined, stages):
        sizes = [len(part) for part in sent]
        new = exchanged(jnp.concatenate(sent), count, [stage] * 2)
        starts = [sum(sizes[:index]) for index in range(len(sizes))]
        sums = [part + new[at:at + size] for part, at, size in zip(kept, starts, sizes)]
        kept = [part[: len(part) // 2] if stage + 1 < stages else part for part in sums]
        sent = [part[len(part) // 2:] for part in sums]
    return jnp.concatenate(kept), beside


def shifted(value, axis, steps):
    count = lax.axis_size(axis)
    leading, last = (max(0, -steps), min(count, count - steps))
    return lax.ppermute(value, axis, [(source, source + steps) for source in range(leading, last)])


def body(queries, key_vectors, value_vectors, log_decay, out_weight, cotangent):
    length, width = queries.shape[1:]
    model = cotangent.shape[2]
    shards, count = lax.axis_size("ctx"), lax.axis_size("dp")
    square = (length, width)
    flops = 8 * length * width * model
    rows = model // count // 2
    paired = shards == 2 and count >= 8 and count & (count - 1) == 0 and rows % 16 == 0

    (local_state,) = local_call(
        state_kernel, [((width, width), F32)], key_vectors, value_vectors, log_decay, name="state", flops=flops // 2
    )
    state_in = shifted(local_state, "ctx", 1)
    if paired:
        plan = halving_plan(count, rows)
        own, send = local_call(
            functools.partial(turn_kernel, count, plan),
            [((rows * count, length), BF16), ((rows * count, length), F32)],
            cotangent, local_state,
            name="turn", flops=flops // 2,
            scratch=[pltpu.VMEM((model, length), F32)],
        )
        received = swap(send)
    within, scores, cumul = local_call(
        within_kernel,
        [(square, F32), ((length, length), F32), (square, F32)],
        queries, key_vectors, value_vectors, log_decay,
        name="within", flops=flops // 2,
    )
    device_decay = jnp.exp(cumul[-1])[:, None]
    for _ in range(shards - 2):
        state_in = shifted(local_state + device_decay * state_in, "ctx", 1)
    normed, scale_inv, rounded = local_call(
        normed_kernel, [(square, F32)] * 3, queries, cumul, within, state_in, name="normed", flops=flops // 4
    )
    grad_query, grad_key_zero, grad_value_zero, gate, sent = local_call(
        grads_kernel,
        [
            (queries.shape, BF16), (square, F32), (square, F32), (square, F32),
            ((width + 8, width), F32),
        ],
        queries, key_vectors, value_vectors, cumul, scores, state_in, normed, scale_inv,
        cotangent, out_weight,
        name="grads", flops=2 * flops,
    )
    later = shifted(sent, "ctx", -1)
    for _ in range(shards - 2):
        grad_in = later[:width]
        own_sum = sent[width:] - jnp.sum(grad_in * local_state, axis=-1)[None]
        later = shifted(
            jnp.concatenate([sent[:width] + device_decay * grad_in, own_sum + later[width:]]),
            "ctx",
            -1,
        )
    grad_key, grad_value, grad_decay = local_call(
        finish_kernel,
        [(queries.shape, BF16), (queries.shape, BF16), (queries.shape, F32)],
        key_vectors, value_vectors, cumul, grad_key_zero, grad_value_zero, gate, later,
        name="finish", flops=flops,
    )
    if paired:
        sizes = [count // 2 * part for part, _ in plan for _ in range(2)]
        pieces = local_call(
            share_kernel,
            [((size, width), F32) for size in sizes],
            own, received, rounded, swap(rounded),
            name="shares", flops=flops // 2,
        )
        mine, beside = halving(
            list(zip(pieces[::2], pieces[1::2])), plan, count, {0: grad_query, 1: grad_decay}
        )
        grad_query, grad_decay = beside[0], beside[1]
        theirs = swap(mine)
        first = lax.axis_index("ctx") == 0
        grad_weight = jnp.concatenate(
            [jnp.where(first, mine, theirs), jnp.where(first, theirs, mine)], axis=0
        )
    else:
        share = jnp.einsum(
            "td,tk->dk", cotangent[0], rounded.astype(BF16), preferred_element_type=F32
        )
        share = lax.psum_scatter(share, "dp", scatter_dimension=0, tiled=True)
        grad_weight = lax.psum(share, "ctx")

    return grad_query, grad_key, grad_value, grad_decay, grad_weight


def solution(mesh):
    placed = (
        P("dp", "ctx", None),
        P("dp", "ctx", None),
        P("dp", "ctx", None),
        P("dp", "ctx", None),
        P(),
        P("dp", "ctx", None),
    )
    return jax.shard_map(
        body,
        mesh=mesh,
        in_specs=placed,
        out_specs=(
            P("dp", "ctx", None),
            P("dp", "ctx", None),
            P("dp", "ctx", None),
            P("dp", "ctx", None),
            P("dp", None),
        ),
        check_vma=False,
    )
```

time: 131 us -> 42.2 us (0.32)
  waiting for transfers between devices: 91 us -> 15.5 us
  between operations: 14.2 us -> 0.79 us
  starting transfers between devices: 5.01 us -> 16.1 us
  matrix products: 10.6 us -> 0 us
  local copies, waits for them, and re-layouts: 9.2 us -> 3.68 us
  Pallas kernels: 0 us -> 4.84 us
    unnamed x3 -> x0, waiting for transfers between devices: 76.7 us -> none
    psum x1 -> x0, waiting for transfers between devices: 13.8 us -> none  [body(): grad_weight = lax.psum(row_share, 'ctx')]
    ppermute x0 -> x10, waiting for transfers between devices: none -> 13.4 us  [the longest x7 11.2 us: exchanged(): return lax.ppermute(value, BOTH, pairs)]
    ppermute x0 -> x10, starting transfers between devices: none -> 12.9 us  [the longest x7 11.9 us: exchanged(): return lax.ppermute(value, BOTH, pairs)]
    dot_general x17 -> x0, matrix products: 10.6 us -> none  [the longest x1 2.02 us: body(): jnp.einsum('td,tk->dk', upstream, rounded, preferred_element_type=jnp.flo...]
    unnamed x15 -> x18, local copies, waits for them, and re-layouts: 9.2 us -> 3.68 us
    pallas_call x0 -> x7, Pallas kernels: none -> 4.84 us  [local_call(): pl.pallas_call(kernel, out_shape=outs, scratch_shapes=list(scratch), comp...]
    ppermute x3 -> x2, starting transfers between devices: 4.93 us -> 3.23 us  [shifted(): lax.ppermute(value, axis, [(source, source + steps) for source in range(l...]
  transfers between devices with their start and end apart: 5 -> 12, of which waited for: 3 -> 10; matrix products, arithmetic and copies ran while one was open for 7% -> 0% of each run, Pallas kernels for 0% -> 8%
where the time goes in v1:
time: 42.2 us; the launch traced here: 41.8 us
  starting transfers between devices  16.1 us (38%)
  waiting for transfers between devices  15.5 us (37%)
  Pallas kernels  4.84 us (11%)
  local copies, waits for them, and re-layouts  3.68 us (9%)
  other arithmetic  0.86 us (2%)
  between operations  0.79 us (2%)
    ppermute x7, starting transfers between devices, exchanged(): return lax.ppermute(value, BOTH, pairs)  11.9 us
    ppermute x7, waiting for transfers between devices, exchanged(): return lax.ppermute(value, BOTH, pairs)  11.2 us
    pallas_call x7, Pallas kernels, local_call(): pl.pallas_call(kernel, out_shape=outs, scratch_shapes=list(scratch), comp...  4.84 us
    unnamed x18, local copies, waits for them, and re-layouts  3.68 us
    ppermute x2, starting transfers between devices, shifted(): lax.ppermute(value, axis, [(source, source + steps) for source in range(l...  3.23 us
    ppermute x3, waiting for transfers between devices, swap(): return lax.ppermute(value, 'ctx', [(0, 1), (1, 0)])  2.16 us
    ppermute x2, waiting for transfers between devices, shifted(): lax.ppermute(value, axis, [(source, source + steps) for source in range(l...  2.16 us
    ppermute x3, starting transfers between devices, swap(): return lax.ppermute(value, 'ctx', [(0, 1), (1, 0)])  1.01 us
  transfers between devices with their start and end apart: 12, of which 10 were waited for; matrix products, arithmetic and copies ran while one was open for 0% of the time, Pallas kernels for 8%

profile of v1, /device:TPU:0, one launch (start us, length us, event | category | flops | bytes accessed | tf_op | source)
XLA Modules:
  0.0 41.8 jit_solution(294661498410559932)
XLA Ops:
  0.6 0.0 copy-start.3
  0.6 0.8 %copy-done.3 = f32[1,128,128]{2,1,0:T(8,128)S(1)} copy-done((f32[1,128,128]{2,1,0:T(8,128)S(1)}, f32[1,128,128]{2,1,0:T(8,128)}, u32[]{:S(2)}) %copy-start.3) | copy-done | bytes 65560
  1.5 0.0 copy-start.6
  1.5 0.8 %copy-done.6 = bf16[1,128,128]{2,1,0:T(8,128)(2,1)S(1)} copy-done((bf16[1,128,128]{2,1,0:T(8,128)(2,1)S(1)}, bf16[1,128,128]{2,1,0:T(8,128)(2,1)}, u32[]{:S(2)}) %copy-start.6) | copy-done | bytes 32792
  2.2 0.0 copy-start.7
  2.2 0.8 %copy-done.7 = bf16[1,128,128]{2,1,0:T(8,128)(2,1)S(1)} copy-done((bf16[1,128,128]{2,1,0:T(8,128)(2,1)S(1)}, bf16[1,128,128]{2,1,0:T(8,128)(2,1)}, u32[]{:S(2)}) %copy-start.7) | copy-done | bytes 32792
  3.0 0.0 copy-start.4
  3.0 0.0 copy-start.5
  3.0 0.4 state.1.state_ref
  3.4 0.0 copy-start
  3.4 1.3 %copy-done = bf16[1,128,5120]{2,1,0:T(8,128)(2,1)S(1)} copy-done((bf16[1,128,5120]{2,1,0:T(8,128)(2,1)S(1)}, bf16[1,128,5120]{2,1,0:T(8,128)(2,1)}, u32[]{:S(2)}) %copy-start) | copy-done | bytes 1310744
  4.7 0.6 %turn.1 = (bf16[2560,128]{1,0:T(8,128)(2,1)S(1)}, f32[2560,128]{1,0:T(8,128)S(1)}) custom-call(bf16[1,128,5120]{2,1,0:T(8,128)(2,1)S(1)} %copy-done, f32[128,128]{1,0:T(8,128)S(1)} %state.1.state_ref), custom_call_target="tpu_custom_call" | custom-call | flops 335544320 | bytes 3342336 | tf_op jit(solution)/shard_map/turn/pallas_call | solution.py:137
  5.3 0.5 %collective-permute-start = (f32[2560,128]{1,0:T(8,128)S(1)}, f32[2560,128]{1,0:T(8,128)S(1)}, u32[]{:S(2)}, u32[]{:S(2)}) collective-permute-start(f32[2560,128]{1,0:T(8,128)S(1)} %get-tuple-element.30), channel_id=1, source_target_pairs={{0,1},{1,0},{2,3},{3,2},{4,5},{5,4},{6,7},{7,6},{8,9},{9,8},{10,11... | collective-permute-start | bytes 3932168 | tf_op jit(solution)/shard_map/ppermute | solution.py:148
  5.8 1.9 %collective-permute-start.1 = (f32[128,128]{1,0:T(8,128)S(1)}, f32[128,128]{1,0:T(8,128)S(1)}, u32[]{:S(2)}, u32[]{:S(2)}) collective-permute-start(f32[128,128]{1,0:T(8,128)S(1)} %state.1.state_ref), channel_id=1, source_target_pairs={{0,1},{2,3},{4,5},{6,7},{8,9},{10,11},{12,13},{14,15},{16,17},{18,... | collective-permute-start | bytes 196616 | tf_op jit(solution)/shard_map/ppermute | solution.py:241
  7.8 0.0 copy-done.4
  7.8 0.0 copy-done.5
  7.8 0.5 %within.1 = (f32[128,128]{1,0:T(8,128)S(1)}, f32[128,128]{1,0:T(8,128)S(1)}, f32[128,128]{1,0:T(8,128)S(1)}) custom-call(bf16[1,128,128]{2,1,0:T(8,128)(2,1)S(1)} %copy-done.5, bf16[1,128,128]{2,1,0:T(8,128)(2,1)S(1)} %copy-done.6, bf16[1,128,128]{2,1,0:T(8,128)(2,1)S(1)} %copy-done.7, f32[1,128,128]{2,1,0:T(8,128)S(1)} %copy-done.4), custom_call_target="tpu_custom_call" | custom-call | flops 335544320 | bytes 360448 | tf_op jit(solution)/shard_map/within/pallas_call | solution.py:137
  8.3 0.3 collective-permute-done.1.state_ref
  8.6 0.0 copy-start.1
  8.6 0.3 normed.1
  8.9 0.4 collective-permute-start.2
  9.3 0.9 %collective-permute-done.2.other_ref = f32[128,128]{1,0:T(8,128)S(1)} collective-permute-done((f32[128,128]{1,0:T(8,128)S(1)}, f32[128,128]{1,0:T(8,128)S(1)}, u32[]{:S(2)}, u32[]{:S(2)}) %collective-permute-start.2) | collective-permute-done | bytes 65568 | tf_op jit(solution)/shard_map/ppermute | solution.py:148
  10.2 0.0 collective-permute-done.received_ref
  10.2 0.5 %shares.1 = (f32[896,128]{1,0:T(8,128)S(1)}, f32[896,128]{1,0:T(8,128)S(1)}, f32[384,128]{1,0:T(8,128)S(1)}, f32[384,128]{1,0:T(8,128)S(1)}) custom-call(bf16[2560,128]{1,0:T(8,128)(2,1)S(1)} %get-tuple-element.29.own_ref, f32[2560,128]{1,0:T(8,128)S(1)} %collective-permute-done.received_ref, f32[128,128]{1,0:T(8,128)S(1)} %get-tuple-element.33.rounded_ref, ...), custom_call_target="tpu_custom_call" | custom-call | flops 335544320 | bytes 3407872 | tf_op jit(solution)/shard_map/shares/pallas_call | solution.py:137
  10.7 3.1 %collective-permute-start.3 = (f32[384,128]{1,0:T(8,128)S(1)}, f32[384,128]{1,0:T(8,128)S(1)}, u32[]{:S(2)}, u32[]{:S(2)}) collective-permute-start(f32[384,128]{1,0:T(8,128)S(1)} %get-tuple-element.34), channel_id=1, source_target_pairs={{0,8},{1,9},{2,10},{3,11},{4,12},{5,13},{6,14},{7,15},{8,0},{9,1},... | collective-permute-start | bytes 589832 | tf_op jit(solution)/shard_map/ppermute | solution.py:206
  13.8 1.5 %collective-permute-start.6 = (f32[896,128]{1,0:T(8,128)S(1)}, f32[896,128]{1,0:T(8,128)S(1)}, u32[]{:S(2)}, u32[]{:S(2)}) collective-permute-start(f32[896,128]{1,0:T(8,128)S(1)} %get-tuple-element.51), channel_id=1, source_target_pairs={{0,2},{1,5},{2,0},{3,7},{4,6},{5,1},{6,4},{7,3},{8,10},{9,13},{10,... | collective-permute-start | bytes 1376264 | tf_op jit(solution)/shard_map/ppermute | solution.py:206
  15.3 0.0 copy-done.1
  15.3 0.0 copy-done.2
  15.3 0.0 copy-done.8
  15.3 1.6 %grads.1 = (bf16[1,128,128]{2,1,0:T(8,128)(2,1)}, f32[128,128]{1,0:T(8,128)S(1)}, f32[128,128]{1,0:T(8,128)S(1)}, f32[128,128]{1,0:T(8,128)S(1)}, f32[136,128]{1,0:T(8,128)S(1)}) custom-call(bf16[1,128,128]{2,1,0:T(8,128)(2,1)S(1)} %copy-done.5, bf16[1,128,128]{2,1,0:T(8,128)(2,1)S(1)} %copy-done.6, bf16[1,128,128]{2,1,0:T(8,128)(2,1)S(1)} %copy-done.8, ...), custom_call_target="tpu_custom_call" | custom-call | flops 1342177280 | bytes 3346432 | tf_op jit(solution)/shard_map/grads/pallas_call | solution.py:137
  16.9 1.3 %collective-permute-start.4 = (f32[136,128]{1,0:T(8,128)S(1)}, f32[136,128]{1,0:T(8,128)S(1)}, u32[]{:S(2)}, u32[]{:S(2)}) collective-permute-start(f32[136,128]{1,0:T(8,128)S(1)} %get-tuple-element.43), channel_id=1, source_target_pairs={{1,0},{3,2},{5,4},{7,6},{9,8},{11,10},{13,12},{15,14},{17,16},{19,... | collective-permute-start | bytes 208904 | tf_op jit(solution)/shard_map/ppermute | solution.py:241
  18.2 1.9 %collective-permute-done.4.later_ref = f32[136,128]{1,0:T(8,128)S(1)} collective-permute-done((f32[136,128]{1,0:T(8,128)S(1)}, f32[136,128]{1,0:T(8,128)S(1)}, u32[]{:S(2)}, u32[]{:S(2)}) %collective-permute-start.4) | collective-permute-done | bytes 69664 | tf_op jit(solution)/shard_map/ppermute | solution.py:241
  20.1 1.0 %finish.1 = (bf16[1,128,128]{2,1,0:T(8,128)(2,1)}, bf16[1,128,128]{2,1,0:T(8,128)(2,1)}, f32[1,128,128]{2,1,0:T(8,128)}) custom-call(bf16[1,128,128]{2,1,0:T(8,128)(2,1)S(1)} %copy-done.6, bf16[1,128,128]{2,1,0:T(8,128)(2,1)S(1)} %copy-done.8, f32[128,128]{1,0:T(8,128)S(1)} %get-tuple-element.31.cumul_ref, f32[128,128]{1,0:T(8,128)S(1)} %get-tuple-element.40.grad_key_ref, ...), custom_call_target="tpu_custom_call" | custom-call | flops 671088640 | bytes 528384 | tf_op jit(solution)/shard_map/finish/pallas_call | solution.py:137
  21.1 0.0 collective-permute-done.3
  21.1 0.6 %collective-permute-start.5 = (f32[192,128]{1,0:T(8,128)S(1)}, f32[192,128]{1,0:T(8,128)S(1)}, u32[]{:S(2)}, u32[]{:S(2)}) collective-permute-start(f32[192,128]{1,0:T(8,128)S(1)} %get-tuple-element.58), channel_id=1, source_target_pairs={{0,2},{1,5},{2,0},{3,7},{4,6},{5,1},{6,4},{7,3},{8,10},{9,13},{10,... | collective-permute-start | bytes 294920 | tf_op jit(solution)/shard_map/ppermute | solution.py:206
  21.7 0.6 %collective-permute-done.6 = f32[896,128]{1,0:T(8,128)S(1)} collective-permute-done((f32[896,128]{1,0:T(8,128)S(1)}, f32[896,128]{1,0:T(8,128)S(1)}, u32[]{:S(2)}, u32[]{:S(2)}) %collective-permute-start.6) | collective-permute-done | bytes 458784 | tf_op jit(solution)/shard_map/ppermute | solution.py:206
  22.4 1.6 %collective-permute-start.7 = (f32[448,128]{1,0:T(8,128)S(1)}, f32[448,128]{1,0:T(8,128)S(1)}, u32[]{:S(2)}, u32[]{:S(2)}) collective-permute-start(f32[448,128]{1,0:T(8,128)S(1)} %get-tuple-element.54), channel_id=1, source_target_pairs={{0,4},{1,3},{2,6},{3,1},{4,0},{5,7},{6,2},{7,5},{8,12},{9,11},{10,... | collective-permute-start | bytes 688136 | tf_op jit(solution)/shard_map/ppermute | solution.py:206
  23.9 2.4 %collective-permute-done.5 = f32[192,128]{1,0:T(8,128)S(1)} collective-permute-done((f32[192,128]{1,0:T(8,128)S(1)}, f32[192,128]{1,0:T(8,128)S(1)}, u32[]{:S(2)}, u32[]{:S(2)}) %collective-permute-start.5) | collective-permute-done | bytes 98336 | tf_op jit(solution)/shard_map/ppermute | solution.py:206
  26.4 2.0 %collective-permute-start.9 = (f32[96,128]{1,0:T(8,128)S(1)}, f32[96,128]{1,0:T(8,128)S(1)}, u32[]{:S(2)}, u32[]{:S(2)}) collective-permute-start(f32[96,128]{1,0:T(8,128)S(1)} %get-tuple-element.60), channel_id=1, source_target_pairs={{0,4},{1,3},{2,6},{3,1},{4,0},{5,7},{6,2},{7,5},{8,12},{9,11},{10,... | collective-permute-start | bytes 147464 | tf_op jit(solution)/shard_map/ppermute | solution.py:206
  28.4 0.1 collective-permute-done.7
  28.5 0.4 %collective-permute-start.8 = (f32[224,128]{1,0:T(8,128)S(1)}, f32[224,128]{1,0:T(8,128)S(1)}, u32[]{:S(2)}, u32[]{:S(2)}) collective-permute-start(f32[224,128]{1,0:T(8,128)S(1)} %get-tuple-element.56), channel_id=1, source_target_pairs={{0,8},{1,9},{2,10},{3,11},{4,12},{5,13},{6,14},{7,15},{8,0},{9,1},... | collective-permute-start | bytes 344072 | tf_op jit(solution)/shard_map/ppermute | solution.py:206
  28.9 1.6 %collective-permute-done.9 = f32[96,128]{1,0:T(8,128)S(1)} collective-permute-done((f32[96,128]{1,0:T(8,128)S(1)}, f32[96,128]{1,0:T(8,128)S(1)}, u32[]{:S(2)}, u32[]{:S(2)}) %collective-permute-start.9) | collective-permute-done | bytes 49184 | tf_op jit(solution)/shard_map/ppermute | solution.py:206
  30.5 3.0 %collective-permute-done.8 = f32[224,128]{1,0:T(8,128)S(1)} collective-permute-done((f32[224,128]{1,0:T(8,128)S(1)}, f32[224,128]{1,0:T(8,128)S(1)}, u32[]{:S(2)}, u32[]{:S(2)}) %collective-permute-start.8) | collective-permute-done | bytes 114720 | tf_op jit(solution)/shard_map/ppermute | solution.py:206
  33.5 2.7 %collective-permute-start.10 = (f32[160,128]{1,0:T(8,128)S(1)}, f32[160,128]{1,0:T(8,128)S(1)}, u32[]{:S(2)}, u32[]{:S(2)}) collective-permute-start(f32[160,128]{1,0:T(8,128)S(1)} %pad_maximum_fusion.1), channel_id=1, source_target_pairs={{0,16},{1,17},{2,18},{3,19},{4,20},{5,21},{6,22},{7,23},{8,24},{9,... | collective-permute-start | bytes 245768 | tf_op jit(solution)/shard_map/ppermute | solution.py:206
  36.2 3.5 %collective-permute-done.10 = f32[160,128]{1,0:T(8,128)S(1)} collective-permute-done((f32[160,128]{1,0:T(8,128)S(1)}, f32[160,128]{1,0:T(8,128)S(1)}, u32[]{:S(2)}, u32[]{:S(2)}) %collective-permute-start.10) | collective-permute-done | bytes 81952 | tf_op jit(solution)/shard_map/ppermute | solution.py:206
  39.8 0.1 collective-permute-start.11
  39.8 1.3 %collective-permute-done.11 = f32[160,128]{1,0:T(8,128)S(1)} collective-permute-done((f32[160,128]{1,0:T(8,128)S(1)}, f32[160,128]{1,0:T(8,128)S(1)}, u32[]{:S(2)}, u32[]{:S(2)}) %collective-permute-start.11) | collective-permute-done | bytes 81952 | tf_op jit(solution)/shard_map/ppermute | solution.py:148
  41.1 0.7 %pad_maximum_fusion = f32[320,128]{1,0:T(8,128)} fusion(f32[160,128]{1,0:T(8,128)S(1)} %get-tuple-element.62, f32[160,128]{1,0:T(8,128)S(1)} %get-tuple-element.61), kind=kLoop, calls=%fused_computation.2 | loop fusion | flops 40960 | bytes 327680 | tf_op jit(solution)/shard_map/concatenate | solution.py:318
  (13 shorter events, 0.2 us)
Async XLA Ops:
  0.6 0.8 %copy-start.3 = (f32[1,128,128]{2,1,0:T(8,128)S(1)}, f32[1,128,128]{2,1,0:T(8,128)}, u32[]{:S(2)}) copy-start(f32[1,128,128]{2,1,0:T(8,128)} %decay_ref.3) | copy-start | bytes 196612
  1.5 0.8 %copy-start.6 = (bf16[1,128,128]{2,1,0:T(8,128)(2,1)S(1)}, bf16[1,128,128]{2,1,0:T(8,128)(2,1)}, u32[]{:S(2)}) copy-start(bf16[1,128,128]{2,1,0:T(8,128)(2,1)} %key_ref.7) | copy-start | bytes 98308
  2.2 0.8 %copy-start.7 = (bf16[1,128,128]{2,1,0:T(8,128)(2,1)S(1)}, bf16[1,128,128]{2,1,0:T(8,128)(2,1)}, u32[]{:S(2)}) copy-start(bf16[1,128,128]{2,1,0:T(8,128)(2,1)} %value_ref.7) | copy-start | bytes 98308
  3.0 4.8 %copy-start.4 = (f32[1,128,128]{2,1,0:T(8,128)S(1)}, f32[1,128,128]{2,1,0:T(8,128)}, u32[]{:S(2)}) copy-start(f32[1,128,128]{2,1,0:T(8,128)} %decay_ref.3) | copy-start | bytes 196612
  3.0 4.8 %copy-start.5 = (bf16[1,128,128]{2,1,0:T(8,128)(2,1)S(1)}, bf16[1,128,128]{2,1,0:T(8,128)(2,1)}, u32[]{:S(2)}) copy-start(bf16[1,128,128]{2,1,0:T(8,128)(2,1)} %query_ref.5) | copy-start | bytes 98308
  3.4 1.3 %copy-start = (bf16[1,128,5120]{2,1,0:T(8,128)(2,1)S(1)}, bf16[1,128,5120]{2,1,0:T(8,128)(2,1)}, u32[]{:S(2)}) copy-start(bf16[1,128,5120]{2,1,0:T(8,128)(2,1)} %upstream_ref.3) | copy-start | bytes 3932164
  5.3 5.0 %collective-permute-start = (f32[2560,128]{1,0:T(8,128)S(1)}, f32[2560,128]{1,0:T(8,128)S(1)}, u32[]{:S(2)}, u32[]{:S(2)}) collective-permute-start(f32[2560,128]{1,0:T(8,128)S(1)} %get-tuple-element.30), channel_id=1, source_target_pairs={{0,1},{1,0},{2,3},{3,2},{4,5},{5,4},{6,7},{7,6},{8,9},{9,8},{10,11... | collective-permute-start | bytes 3932168 | tf_op jit(solution)/shard_map/ppermute | solution.py:148
  5.8 2.8 %collective-permute-start.1 = (f32[128,128]{1,0:T(8,128)S(1)}, f32[128,128]{1,0:T(8,128)S(1)}, u32[]{:S(2)}, u32[]{:S(2)}) collective-permute-start(f32[128,128]{1,0:T(8,128)S(1)} %state.1.state_ref), channel_id=1, source_target_pairs={{0,1},{2,3},{4,5},{6,7},{8,9},{10,11},{12,13},{14,15},{16,17},{18,... | collective-permute-start | bytes 196616 | tf_op jit(solution)/shard_map/ppermute | solution.py:241
  8.6 6.7 %copy-start.1 = (bf16[1,128,5120]{2,1,0:T(8,128)(2,1)S(1)}, bf16[1,128,5120]{2,1,0:T(8,128)(2,1)}, u32[]{:S(2)}) copy-start(bf16[1,128,5120]{2,1,0:T(8,128)(2,1)} %upstream_ref.3) | copy-start | bytes 3932164
  8.6 6.7 %copy-start.2 = (bf16[5120,128]{1,0:T(8,128)(2,1)S(1)}, bf16[5120,128]{1,0:T(8,128)(2,1)}, u32[]{:S(2)}) copy-start(bf16[5120,128]{1,0:T(8,128)(2,1)} %weight_ref.1) | copy-start | bytes 3932164
  8.6 6.7 %copy-start.8 = (bf16[1,128,128]{2,1,0:T(8,128)(2,1)S(1)}, bf16[1,128,128]{2,1,0:T(8,128)(2,1)}, u32[]{:S(2)}) copy-start(bf16[1,128,128]{2,1,0:T(8,128)(2,1)} %value_ref.7) | copy-start | bytes 98308
  8.9 1.3 %collective-permute-start.2 = (f32[128,128]{1,0:T(8,128)S(1)}, f32[128,128]{1,0:T(8,128)S(1)}, u32[]{:S(2)}, u32[]{:S(2)}) collective-permute-start(f32[128,128]{1,0:T(8,128)S(1)} %get-tuple-element.33.rounded_ref), channel_id=1, source_target_pairs={{0,1},{1,0},{2,3},{3,2},{4,5},{5,4},{6,7},{7,6},{8,9},{9,8},{10,11... | collective-permute-start | bytes 196616 | tf_op jit(solution)/shard_map/ppermute | solution.py:148
  10.7 10.3 %collective-permute-start.3 = (f32[384,128]{1,0:T(8,128)S(1)}, f32[384,128]{1,0:T(8,128)S(1)}, u32[]{:S(2)}, u32[]{:S(2)}) collective-permute-start(f32[384,128]{1,0:T(8,128)S(1)} %get-tuple-element.34), channel_id=1, source_target_pairs={{0,8},{1,9},{2,10},{3,11},{4,12},{5,13},{6,14},{7,15},{8,0},{9,1},... | collective-permute-start | bytes 589832 | tf_op jit(solution)/shard_map/ppermute | solution.py:206
  13.8 8.5 %collective-permute-start.6 = (f32[896,128]{1,0:T(8,128)S(1)}, f32[896,128]{1,0:T(8,128)S(1)}, u32[]{:S(2)}, u32[]{:S(2)}) collective-permute-start(f32[896,128]{1,0:T(8,128)S(1)} %get-tuple-element.51), channel_id=1, source_target_pairs={{0,2},{1,5},{2,0},{3,7},{4,6},{5,1},{6,4},{7,3},{8,10},{9,13},{10,... | collective-permute-start | bytes 1376264 | tf_op jit(solution)/shard_map/ppermute | solution.py:206
  16.9 3.1 %collective-permute-start.4 = (f32[136,128]{1,0:T(8,128)S(1)}, f32[136,128]{1,0:T(8,128)S(1)}, u32[]{:S(2)}, u32[]{:S(2)}) collective-permute-start(f32[136,128]{1,0:T(8,128)S(1)} %get-tuple-element.43), channel_id=1, source_target_pairs={{1,0},{3,2},{5,4},{7,6},{9,8},{11,10},{13,12},{15,14},{17,16},{19,... | collective-permute-start | bytes 208904 | tf_op jit(solution)/shard_map/ppermute | solution.py:241
  21.1 5.2 %collective-permute-start.5 = (f32[192,128]{1,0:T(8,128)S(1)}, f32[192,128]{1,0:T(8,128)S(1)}, u32[]{:S(2)}, u32[]{:S(2)}) collective-permute-start(f32[192,128]{1,0:T(8,128)S(1)} %get-tuple-element.58), channel_id=1, source_target_pairs={{0,2},{1,5},{2,0},{3,7},{4,6},{5,1},{6,4},{7,3},{8,10},{9,13},{10,... | collective-permute-start | bytes 294920 | tf_op jit(solution)/shard_map/ppermute | solution.py:206
  22.4 6.1 %collective-permute-start.7 = (f32[448,128]{1,0:T(8,128)S(1)}, f32[448,128]{1,0:T(8,128)S(1)}, u32[]{:S(2)}, u32[]{:S(2)}) collective-permute-start(f32[448,128]{1,0:T(8,128)S(1)} %get-tuple-element.54), channel_id=1, source_target_pairs={{0,4},{1,3},{2,6},{3,1},{4,0},{5,7},{6,2},{7,5},{8,12},{9,11},{10,... | collective-permute-start | bytes 688136 | tf_op jit(solution)/shard_map/ppermute | solution.py:206
  26.4 4.2 %collective-permute-start.9 = (f32[96,128]{1,0:T(8,128)S(1)}, f32[96,128]{1,0:T(8,128)S(1)}, u32[]{:S(2)}, u32[]{:S(2)}) collective-permute-start(f32[96,128]{1,0:T(8,128)S(1)} %get-tuple-element.60), channel_id=1, source_target_pairs={{0,4},{1,3},{2,6},{3,1},{4,0},{5,7},{6,2},{7,5},{8,12},{9,11},{10,... | collective-permute-start | bytes 147464 | tf_op jit(solution)/shard_map/ppermute | solution.py:206
  28.5 5.0 %collective-permute-start.8 = (f32[224,128]{1,0:T(8,128)S(1)}, f32[224,128]{1,0:T(8,128)S(1)}, u32[]{:S(2)}, u32[]{:S(2)}) collective-permute-start(f32[224,128]{1,0:T(8,128)S(1)} %get-tuple-element.56), channel_id=1, source_target_pairs={{0,8},{1,9},{2,10},{3,11},{4,12},{5,13},{6,14},{7,15},{8,0},{9,1},... | collective-permute-start | bytes 344072 | tf_op jit(solution)/shard_map/ppermute | solution.py:206
  33.5 6.2 %collective-permute-start.10 = (f32[160,128]{1,0:T(8,128)S(1)}, f32[160,128]{1,0:T(8,128)S(1)}, u32[]{:S(2)}, u32[]{:S(2)}) collective-permute-start(f32[160,128]{1,0:T(8,128)S(1)} %pad_maximum_fusion.1), channel_id=1, source_target_pairs={{0,16},{1,17},{2,18},{3,19},{4,20},{5,21},{6,22},{7,23},{8,24},{9,... | collective-permute-start | bytes 245768 | tf_op jit(solution)/shard_map/ppermute | solution.py:206
  39.8 1.3 %collective-permute-start.11 = (f32[160,128]{1,0:T(8,128)S(1)}, f32[160,128]{1,0:T(8,128)S(1)}, u32[]{:S(2)}, u32[]{:S(2)}) collective-permute-start(f32[160,128]{1,0:T(8,128)S(1)} %pad_maximum_fusion.2), channel_id=1, source_target_pairs={{0,1},{1,0},{2,3},{3,2},{4,5},{5,4},{6,7},{7,6},{8,9},{9,8},{10,11... | collective-permute-start | bytes 245768 | tf_op jit(solution)/shard_map/ppermute | solution.py:148

commit v2 on v1

--- a/solution.py
+++ b/solution.py
@@ -9,6 +9,7 @@
 
 EPSILON = 1e-05
 VMEM_BYTES = 24 * 1024 * 1024
+PACK_BYTES = 58 * 1024 * 1024
 F32 = jnp.float32
 BF16 = jnp.bfloat16
 BOTH = ("dp", "ctx")
@@ -77,13 +78,13 @@
 
 
 def grads_kernel(
-    query_ref, key_ref, value_ref, cumul_ref, scores_ref, state_ref, normed_ref, scale_ref,
+    packed_ref, cumul_ref, scores_ref, state_ref, normed_ref, scale_ref,
     upstream_ref, weight_ref,
     grad_query_ref, grad_key_ref, grad_value_ref, gate_ref, sent_ref,
 ):
-    query = query_ref[0].astype(F32)
-    key = key_ref[0].astype(F32)
-    value = value_ref[0]
+    query = packed_ref[0]
+    key = packed_ref[1]
+    value = packed_ref[2].astype(BF16)
     cumul = cumul_ref[...]
     rising = jnp.exp(cumul)
     falling = jnp.exp(-cumul)
@@ -114,15 +115,15 @@
 
 
 def finish_kernel(
-    key_ref, value_ref, cumul_ref, grad_key_ref, grad_value_ref, gate_ref, later_ref,
+    packed_ref, cumul_ref, grad_key_ref, grad_value_ref, gate_ref, later_ref,
     key_out_ref, value_out_ref, decay_out_ref,
 ):
-    key = key_ref[0].astype(F32)
+    key = packed_ref[1]
     cumul = cumul_ref[...]
     width = key.shape[1]
     to_end = jnp.exp(cumul[-1:] - cumul)
     grad_in = split(later_ref[:width], 2)
-    extra = to_end * product([value_ref[0]], grad_in, 1, 1)
+    extra = to_end * product([packed_ref[2].astype(BF16)], grad_in, 1, 1)
     key_out_ref[0] = (grad_key_ref[...] + extra).astype(BF16)
     grad_value = grad_value_ref[...] + product(split(key * to_end, 2), grad_in, 1, 0)
     value_out_ref[0] = grad_value.astype(BF16)
@@ -131,14 +132,15 @@
     decay_out_ref[0] = product([lower], split(gate, 3), 0, 0) + later_ref[width:width + 1]
 
 
-def local_call(kernel, shapes, *operands, name, flops, scratch=()):
+def local_call(kernel, shapes, *operands, name, flops, scratch=(), space=pltpu.VMEM, limit=VMEM_BYTES):
     outs = [jax.ShapeDtypeStruct(shape, dtype) for shape, dtype in shapes]
     moved = sum(array.size * array.dtype.itemsize for array in [*operands, *outs])
     return pl.pallas_call(
         kernel,
         out_shape=outs,
+        in_specs=[pl.BlockSpec(memory_space=space)] * len(operands),
         scratch_shapes=list(scratch),
-        compiler_params=pltpu.CompilerParams(vmem_limit_bytes=VMEM_BYTES),
+        compiler_params=pltpu.CompilerParams(vmem_limit_bytes=limit),
         cost_estimate=pl.CostEstimate(flops=flops, bytes_accessed=moved, transcendentals=0),
         name=name,
     )(*operands)
@@ -163,37 +165,101 @@
     return sum(((place >> (top - step)) & 1) << bit for step, bit in enumerate(order))
 
 
-def turn_kernel(count, plan, upstream_ref, state_ref, own_ref, send_ref, turned):
-    del state_ref
-
+def pack_kernel(query_ref, key_ref, value_ref, decay_ref, packed_ref, query, key, value, semaphores):
+    pairs = [
+        (decay_ref.at[0], packed_ref.at[3]), (query_ref.at[0], query),
+        (key_ref.at[0], key), (value_ref.at[0], value),
+    ]
+    copies = [
+        pltpu.make_async_copy(source, target, semaphores.at[index])
+        for index, (source, target) in enumerate(pairs)
+    ]
+    for copy in copies:
+        copy.start()
+    for copy in copies:
+        copy.wait()
+    packed_ref[0] = query[...].astype(F32)
+    packed_ref[1] = key[...].astype(F32)
+    packed_ref[2] = value[...].astype(F32)
+
+
+def turn_kernel(count, plan, upstream_ref, own_ref, first_ref, second_ref, turned):
     me, core = lax.axis_index("dp"), lax.axis_index("ctx")
+    model = turned.shape[0]
     lanes = 128
-    for start in range(0, turned.shape[0], lanes):
-        block = upstream_ref[0, :, start:start + lanes].astype(F32)
-        turned[start:start + lanes] = jnp.transpose(block)
-    share = turned.shape[0] // count
+    for start in range(0, model, lanes):
+        turned[start:start + lanes] = jnp.transpose(upstream_ref[0, :, start:start + lanes].astype(F32))
+    share = model // count
     half = share // 2
-    at = offset = 0
-    for rows, orders in plan:
-        for place in range(count):
-            masks = [relative(place, order) for order in orders]
-            for target, ref in ((core, own_ref), (1 - core, send_ref)):
-                owner = me ^ (masks[0] + target * (masks[1] - masks[0]))
-                begin = pl.multiple_of(owner * share + target * half + offset, 16)
-                ref[at:at + rows] = turned[pl.ds(begin, rows)].astype(ref.dtype)
-            at += rows
-        offset += rows
-
-
-def share_kernel(own_ref, received_ref, rounded_ref, other_ref, *outs):
-    rounded = jnp.concatenate([rounded_ref[...], other_ref[...]], axis=0).astype(BF16)
+    at = 0
+    for ref, places in ((first_ref, range(count // 2, count)), (second_ref, range(count // 2))):
+        offset = sent = 0
+        for rows, orders in plan:
+            for place in places:
+                masks = [relative(place, order) for order in orders]
+                mine = me ^ (masks[0] + core * (masks[1] - masks[0]))
+                other = me ^ (masks[1] + core * (masks[0] - masks[1]))
+                begin = pl.multiple_of(mine * share + core * half + offset, 16)
+                own_ref[at:at + rows] = turned[pl.ds(begin, rows)].astype(BF16)
+                begin = pl.multiple_of(other * share + (1 - core) * half + offset, 16)
+                ref[sent:sent + rows] = turned[pl.ds(begin, rows)]
+                at += rows
+                sent += rows
+            offset += rows
+
+
+def joint_kernel(
+    own_ref, other_ref,
+    cumul_ref, scores_ref, state_ref, normed_ref, scale_ref, rounded_ref,
+):
+    first = lax.axis_index("ctx") == 0
+    length = cumul_ref.shape[0]
+    lower = lower_mask(length)
+
+    def scaled(block):
+        query, key, value, decay = block
+        cumul = cumulate(decay)
+        query_scaled = split(query * jnp.exp(cumul), 2)
+        key_scaled = split(key * jnp.exp(-cumul), 2)
+        return cumul, query_scaled, key_scaled, value.astype(BF16)
+
+    def within(query_scaled, key_scaled, value):
+        scores = jnp.where(lower, product(query_scaled, key_scaled, 1, 1), 0.0)
+        return scores, product(split(scores, 2), [value], 1, 0)
+
+    def normalized(output):
+        scale_inv = lax.rsqrt(jnp.mean(output * output, axis=-1, keepdims=True) + EPSILON)
+        normed = output * scale_inv
+        return normed, jnp.broadcast_to(scale_inv, normed.shape), normed.astype(BF16)
+
+    early = [jnp.where(first, own_ref[i], other_ref[i]) for i in range(4)]
+    late = [jnp.where(first, other_ref[i], own_ref[i]) for i in range(4)]
+    cumul_early, queries_early, keys_early, values_early = scaled(early)
+    cumul_late, queries_late, keys_late, values_late = scaled(late)
+    to_end = jnp.exp(cumul_early[-1:] - cumul_early)
+    state = product(split(early[1] * to_end, 2), [values_early], 0, 0)
+    scores_early, output_early = within(queries_early, keys_early, values_early)
+    scores_late, output_late = within(queries_late, keys_late, values_late)
+    output_late += product(queries_late, split(state, 2), 1, 0)
+    done_early = normalized(output_early)
+    done_late = normalized(output_late)
+    cumul_ref[...] = jnp.where(first, cumul_early, cumul_late)
+    scores_ref[...] = jnp.where(first, scores_early, scores_late)
+    state_ref[...] = jnp.where(first, 0.0, state)
+    normed_ref[...] = jnp.where(first, done_early[0], done_late[0])
+    scale_ref[...] = jnp.where(first, done_early[1], done_late[1])
+    rounded_ref[:length] = jnp.where(first, done_early[2], done_late[2])
+    rounded_ref[length:] = jnp.where(first, done_late[2], done_early[2])
+
+
+def share_kernel(begin, own_ref, received_ref, rounded_ref, *outs):
     at = 0
     for out in outs:
         rows = out.shape[0]
         left = jnp.concatenate(
-            [own_ref[at:at + rows], received_ref[at:at + rows].astype(BF16)], axis=1
-        )
-        out[...] = jnp.dot(left, rounded, preferred_element_type=F32)
+            [own_ref[begin + at:begin + at + rows], received_ref[at:at + rows].astype(BF16)], axis=1
+        )
+        out[...] = jnp.dot(left, rounded_ref[...], preferred_element_type=F32)
         at += rows
 
 
@@ -206,25 +272,23 @@
     return lax.ppermute(value, BOTH, pairs)
 
 
-def halving(chunks, plan, count, beside):
-    beside = dict(beside)
+def halving(kept, sent, plan, count, beside):
     stages = len(plan[0][1][0])
     joined = 3
     for stage in range(joined):
         arrived = [
-            exchanged(sent, count, [order[stage] for order in orders])
-            for (_, sent), (_, orders) in zip(chunks, plan)
+            exchanged(part, count, [order[stage] for order in orders])
+            for part, (_, orders) in zip(sent, plan)
         ]
         if stage in beside:
-            arrived[-1], beside[stage] = lax.optimization_barrier((arrived[-1], beside[stage]))
-        chunks = [
-            (kept[: len(kept) // 2] + new[: len(kept) // 2], kept[len(kept) // 2:] + new[len(kept) // 2:])
-            if stage + 1 < stages
-            else (kept + new, None)
-            for (kept, _), new in zip(chunks, arrived)
+            arrived = beside[stage](arrived)
+        half = [len(part) // 2 if stage + 1 < stages else len(part) for part in kept]
+        sums = [
+            (old[:size] + new[:size], old[size:] + new[size:])
+            for old, new, size in zip(kept, arrived, half)
         ]
-    kept = [chunk[0] for chunk in chunks]
-    sent = [chunk[1] for chunk in chunks]
+        kept = [pair[0] for pair in sums]
+        sent = [pair[1] for pair in sums]
     for stage in range(joined, stages):
         sizes = [len(part) for part in sent]
         new = exchanged(jnp.concatenate(sent), count, [stage] * 2)
@@ -232,7 +296,7 @@
         sums = [part + new[at:at + size] for part, at, size in zip(kept, starts, sizes)]
         kept = [part[: len(part) // 2] if stage + 1 < stages else part for part in sums]
         sent = [part[len(part) // 2:] for part in sums]
-    return jnp.concatenate(kept), beside
+    return jnp.concatenate(kept)
 
 
 def shifted(value, axis, steps):
@@ -246,79 +310,125 @@
     model = cotangent.shape[2]
     shards, count = lax.axis_size("ctx"), lax.axis_size("dp")
     square = (length, width)
+    rows = model // count // 2
     flops = 8 * length * width * model
-    rows = model // count // 2
     paired = shards == 2 and count >= 8 and count & (count - 1) == 0 and rows % 16 == 0
 
-    (local_state,) = local_call(
-        state_kernel, [((width, width), F32)], key_vectors, value_vectors, log_decay, name="state", flops=flops // 2
-    )
-    state_in = shifted(local_state, "ctx", 1)
+    (packed,) = local_call(
+        pack_kernel,
+        [((4, length, width), F32)],
+        queries, key_vectors, value_vectors, log_decay,
+        name="pack", flops=20 * flops, space=pltpu.HBM, limit=PACK_BYTES,
+        scratch=[pltpu.VMEM(square, BF16)] * 3 + [pltpu.SemaphoreType.DMA((4,))],
+    )
     if paired:
         plan = halving_plan(count, rows)
-        own, send = local_call(
+        part_rows = rows * count // 2
+        own, send_first, send_second = local_call(
             functools.partial(turn_kernel, count, plan),
-            [((rows * count, length), BF16), ((rows * count, length), F32)],
-            cotangent, local_state,
-            name="turn", flops=flops // 2,
+            [((2 * part_rows, length), BF16), ((part_rows, length), F32), ((part_rows, length), F32)],
+            cotangent,
+            name="turn", flops=20 * flops,
             scratch=[pltpu.VMEM((model, length), F32)],
         )
-        received = swap(send)
-    within, scores, cumul = local_call(
-        within_kernel,
-        [(square, F32), ((length, length), F32), (square, F32)],
-        queries, key_vectors, value_vectors, log_decay,
-        name="within", flops=flops // 2,
-    )
-    device_decay = jnp.exp(cumul[-1])[:, None]
-    for _ in range(shards - 2):
-        state_in = shifted(local_state + device_decay * state_in, "ctx", 1)
-    normed, scale_inv, rounded = local_call(
-        normed_kernel, [(square, F32)] * 3, queries, cumul, within, state_in, name="normed", flops=flops // 4
-    )
-    grad_query, grad_key_zero, grad_value_zero, gate, sent = local_call(
+        others = swap(packed)
+        received_first = swap(send_first)
+        received_second = swap(send_second)
+        cumul, scores, state_in, normed, scale_inv, rounded = local_call(
+            joint_kernel,
+            [
+                (square, F32), ((length, length), F32), ((width, width), F32), (square, F32),
+                (square, F32), ((2 * length, width), BF16),
+            ],
+            packed, others,
+            name="joint", flops=40 * flops,
+        )
+        sent = local_call(
+            functools.partial(share_kernel, 0),
+            [((count // 2 * part, width), F32) for part, _ in plan],
+            own, received_first, rounded,
+            name="sent_shares", flops=flops // 4,
+        )
+        kept = local_call(
+            functools.partial(share_kernel, part_rows),
+            [((count // 2 * part, width), F32) for part, _ in plan],
+            own, received_second, rounded,
+            name="kept_shares", flops=flops // 4,
+        )
+    else:
+        (local_state,) = local_call(
+            state_kernel, [((width, width), F32)], key_vectors, value_vectors, log_decay,
+            name="state", flops=flops // 2,
+        )
+        state_in = shifted(local_state, "ctx", 1)
+        within, scores, cumul = local_call(
+            within_kernel,
+            [(square, F32), ((length, length), F32), (square, F32)],
+            queries, key_vectors, value_vectors, log_decay,
+            name="within", flops=flops // 2,
+        )
+        device_decay = jnp.exp(cumul[-1])[:, None]
+        for _ in range(shards - 2):
+            state_in = shifted(local_state + device_decay * state_in, "ctx", 1)
+        normed, scale_inv, rounded = local_call(
+            normed_kernel, [(square, F32)] * 3, queries, cumul, within, state_in,
+            name="normed", flops=flops // 4,
+        )
+
+    grad_query, grad_key_zero, grad_value_zero, gate, grad_sent = local_call(
         grads_kernel,
         [
             (queries.shape, BF16), (square, F32), (square, F32), (square, F32),
             ((width + 8, width), F32),
         ],
-        queries, key_vectors, value_vectors, cumul, scores, state_in, normed, scale_inv,
+        packed, cumul, scores, state_in, normed, scale_inv,
         cotangent, out_weight,
         name="grads", flops=2 * flops,
     )
-    later = shifted(sent, "ctx", -1)
-    for _ in range(shards - 2):
-        grad_in = later[:width]
-        own_sum = sent[width:] - jnp.sum(grad_in * local_state, axis=-1)[None]
-        later = shifted(
-            jnp.concatenate([sent[:width] + device_decay * grad_in, own_sum + later[width:]]),
-            "ctx",
-            -1,
-        )
-    grad_key, grad_value, grad_decay = local_call(
-        finish_kernel,
-        [(queries.shape, BF16), (queries.shape, BF16), (queries.shape, F32)],
-        key_vectors, value_vectors, cumul, grad_key_zero, grad_value_zero, gate, later,
-        name="finish", flops=flops,
-    )
+    later = shifted(grad_sent, "ctx", -1)
+
+    def finish(later):
+        return local_call(
+            finish_kernel,
+            [(queries.shape, BF16), (queries.shape, BF16), (queries.shape, F32)],
+            packed, cumul, grad_key_zero, grad_value_zero, gate, later,
+            name="finish", flops=flops,
+        )
+
     if paired:
-        sizes = [count // 2 * part for part, _ in plan for _ in range(2)]
-        pieces = local_call(
-            share_kernel,
-            [((size, width), F32) for size in sizes],
-            own, received, rounded, swap(rounded),
-            name="shares", flops=flops // 2,
-        )
-        mine, beside = halving(
-            list(zip(pieces[::2], pieces[1::2])), plan, count, {0: grad_query, 1: grad_decay}
-        )
-        grad_query, grad_decay = beside[0], beside[1]
+        held = {}
+
+        def beside_first(arrived):
+            large, small = arrived
+            small, held["query"] = lax.optimization_barrier((small, grad_query))
+            large, held["later"] = lax.optimization_barrier((large, later))
+            return [large, small]
+
+        def beside_second(arrived):
+            large, small = arrived
+            key, value, decay = finish(held["later"])
+            large, decay = lax.optimization_barrier((large, decay))
+            held["finished"] = key, value, decay
+            return [large, small]
+
+        mine = halving(kept=kept, sent=sent, plan=plan, count=count, beside={0: beside_first, 1: beside_second})
+        grad_query = held["query"]
+        grad_key, grad_value, grad_decay = held["finished"]
         theirs = swap(mine)
         first = lax.axis_index("ctx") == 0
         grad_weight = jnp.concatenate(
             [jnp.where(first, mine, theirs), jnp.where(first, theirs, mine)], axis=0
         )
     else:
+        for _ in range(shards - 2):
+            grad_in = later[:width]
+            own_sum = grad_sent[width:] - jnp.sum(grad_in * local_state, axis=-1)[None]
+            later = shifted(
+                jnp.concatenate([grad_sent[:width] + device_decay * grad_in, own_sum + later[width:]]),
+                "ctx",
+                -1,
+            )
+        grad_key, grad_value, grad_decay = finish(later)
         share = jnp.einsum(
             "td,tk->dk", cotangent[0], rounded.astype(BF16), preferred_element_type=F32
         )

time: 42.2 us -> 35.3 us (0.84)
  local copies, waits for them, and re-layouts: 3.68 us -> 0.01 us
  waiting for transfers between devices: 15.5 us -> 12.8 us
  starting transfers between devices: 16.1 us -> 14.2 us
  Pallas kernels: 4.84 us -> 6.49 us
    unnamed x18 -> x6, local copies, waits for them, and re-layouts: 3.68 us -> 0.01 us
    ppermute x2 -> x1, waiting for transfers between devices: 2.16 us -> 0.01 us  [shifted(): lax.ppermute(value, axis, [(source, source + steps) for source in range(l...]
    ppermute x2 -> x1, starting transfers between devices: 3.23 us -> 1.28 us  [shifted(): lax.ppermute(value, axis, [(source, source + steps) for source in range(l...]
    pallas_call x7, Pallas kernels: 4.84 us -> 6.49 us  [local_call(): pl.pallas_call(kernel, out_shape=outs, in_specs=[pl.BlockSpec(memory_spac...]
    ppermute x3 -> x4, waiting for transfers between devices: 2.16 us -> 1.86 us  [swap(): return lax.ppermute(value, 'ctx', [(0, 1), (1, 0)])]
    ppermute x3 -> x4, starting transfers between devices: 1.01 us -> 1.16 us  [swap(): return lax.ppermute(value, 'ctx', [(0, 1), (1, 0)])]
  transfers between devices with their start and end apart: 12 -> 12, of which waited for: 10 -> 8; matrix products, arithmetic and copies ran while one was open for 0% -> 0% of each run, Pallas kernels for 8% -> 14%
where the time goes in v2:
time: 35.3 us; the launch traced here: 35.2 us
  starting transfers between devices  14.2 us (40%)
  waiting for transfers between devices  12.8 us (36%)
  Pallas kernels  6.49 us (18%)
  other arithmetic  0.85 us (2%)
  between operations  0.78 us (2%)
    ppermute x7, starting transfers between devices, exchanged(): return lax.ppermute(value, BOTH, pairs)  11.8 us
    ppermute x7, waiting for transfers between devices, exchanged(): return lax.ppermute(value, BOTH, pairs)  11 us
    pallas_call x7, Pallas kernels, local_call(): pl.pallas_call(kernel, out_shape=outs, in_specs=[pl.BlockSpec(memory_spac...  6.49 us
    ppermute x4, waiting for transfers between devices, swap(): return lax.ppermute(value, 'ctx', [(0, 1), (1, 0)])  1.86 us
    ppermute x1, starting transfers between devices, shifted(): lax.ppermute(value, axis, [(source, source + steps) for source in range(l...  1.28 us
    ppermute x4, starting transfers between devices, swap(): return lax.ppermute(value, 'ctx', [(0, 1), (1, 0)])  1.16 us
  transfers between devices with their start and end apart: 12, of which 8 were waited for; matrix products, arithmetic and copies ran while one was open for 0% of the time, Pallas kernels for 14%

profile of v2, /device:TPU:0, one launch (start us, length us, event | category | flops | bytes accessed | tf_op | source)
XLA Modules:
  0.0 35.2 jit_solution(16218290765029825863)
XLA Ops:
  0.6 0.0 copy-start
  0.6 1.7 %pack.1.own_ref.packed_ref = f32[4,128,128]{2,1,0:T(8,128)} custom-call(bf16[1,128,128]{2,1,0:T(8,128)(2,1)} %query_ref.1, bf16[1,128,128]{2,1,0:T(8,128)(2,1)} %key_ref.1, bf16[1,128,128]{2,1,0:T(8,128)(2,1)} %value_ref.1, f32[1,128,128]{2,1,0:T(8,128)} %decay_ref.1), custom_call_target="tpu_custom_call" | custom-call | flops 13421772800 | bytes 425984 | tf_op jit(solution)/shard_map/pack/pallas_call | solution.py:138
  2.3 0.0 copy-start.2
  2.4 0.5 %collective-permute-start.1 = (f32[4,128,128]{2,1,0:T(8,128)}, f32[4,128,128]{2,1,0:T(8,128)S(1)}, u32[]{:S(2)}, u32[]{:S(2)}) collective-permute-start(f32[4,128,128]{2,1,0:T(8,128)} %pack.1.own_ref.packed_ref), channel_id=1, source_target_pairs={{0,1},{1,0},{2,3},{3,2},{4,5},{5,4},{6,7},{7,6},{8,9},{9,8},{10,11... | collective-permute-start | bytes 786440 | tf_op jit(solution)/shard_map/ppermute | solution.py:150
  2.9 0.0 copy-done
  2.9 0.6 %turn.1 = (bf16[2560,128]{1,0:T(8,128)(2,1)S(1)}, f32[1280,128]{1,0:T(8,128)S(1)}, f32[1280,128]{1,0:T(8,128)S(1)}) custom-call(bf16[1,128,5120]{2,1,0:T(8,128)(2,1)S(1)} %copy-done), custom_call_target="tpu_custom_call" | custom-call | flops 13421772800 | bytes 3276800 | tf_op jit(solution)/shard_map/turn/pallas_call | solution.py:138
  3.4 0.1 collective-permute-start
  3.6 0.5 %collective-permute-start.5 = (f32[1280,128]{1,0:T(8,128)S(1)}, f32[1280,128]{1,0:T(8,128)S(1)}, u32[]{:S(2)}, u32[]{:S(2)}) collective-permute-start(f32[1280,128]{1,0:T(8,128)S(1)} %get-tuple-element.51), channel_id=1, source_target_pairs={{0,1},{1,0},{2,3},{3,2},{4,5},{5,4},{6,7},{7,6},{8,9},{9,8},{10,11... | collective-permute-start | bytes 1966088 | tf_op jit(solution)/shard_map/ppermute | solution.py:150
  4.0 0.2 collective-permute-done.1.other_ref
  4.2 0.0 copy-done.2
  4.3 1.0 %joint.1 = (f32[128,128]{1,0:T(8,128)S(1)}, f32[128,128]{1,0:T(8,128)S(1)}, f32[128,128]{1,0:T(8,128)S(1)}, f32[128,128]{1,0:T(8,128)S(1)}, f32[128,128]{1,0:T(8,128)S(1)}, /*index=5*/bf16[256,128]{1,0:T(8,128)(2,1)S(1)}) custom-call(f32[4,128,128]{2,1,0:T(8,128)S(1)} %copy-done.2, f32[4,128,128]{2,1,0:T(8,128)S(1)} %collective-permute-done.1.other_ref), custom_call_target="tpu_custom_call" | custom-call | flops 26843545600 | bytes 917504 | tf_op jit(solution)/shard_map/joint/pallas_call | solution.py:138
  5.2 0.0 copy-start.1
  5.2 0.4 %collective-permute-done.received_ref = f32[1280,128]{1,0:T(8,128)S(1)} collective-permute-done((f32[1280,128]{1,0:T(8,128)S(1)}, f32[1280,128]{1,0:T(8,128)S(1)}, u32[]{:S(2)}, u32[]{:S(2)}) %collective-permute-start) | collective-permute-done | bytes 655392 | tf_op jit(solution)/shard_map/ppermute | solution.py:150
  5.6 0.3 sent_shares.1
  5.9 2.7 %collective-permute-start.3 = (f32[896,128]{1,0:T(8,128)S(1)}, f32[896,128]{1,0:T(8,128)S(1)}, u32[]{:S(2)}, u32[]{:S(2)}) collective-permute-start(f32[896,128]{1,0:T(8,128)S(1)} %get-tuple-element.46), channel_id=1, source_target_pairs={{0,2},{1,5},{2,0},{3,7},{4,6},{5,1},{6,4},{7,3},{8,10},{9,13},{10,... | collective-permute-start | bytes 1376264 | tf_op jit(solution)/shard_map/ppermute | solution.py:272
  8.6 1.6 %collective-permute-start.2 = (f32[384,128]{1,0:T(8,128)S(1)}, f32[384,128]{1,0:T(8,128)S(1)}, u32[]{:S(2)}, u32[]{:S(2)}) collective-permute-start(f32[384,128]{1,0:T(8,128)S(1)} %get-tuple-element.35), channel_id=1, source_target_pairs={{0,8},{1,9},{2,10},{3,11},{4,12},{5,13},{6,14},{7,15},{8,0},{9,1},... | collective-permute-start | bytes 589832 | tf_op jit(solution)/shard_map/ppermute | solution.py:272
  10.2 0.0 copy-done.1
  10.2 1.6 %grads.1 = (bf16[1,128,128]{2,1,0:T(8,128)(2,1)}, f32[128,128]{1,0:T(8,128)S(1)}, f32[128,128]{1,0:T(8,128)S(1)}, f32[128,128]{1,0:T(8,128)S(1)}, f32[136,128]{1,0:T(8,128)S(1)}) custom-call(f32[4,128,128]{2,1,0:T(8,128)S(1)} %copy-done.2, f32[128,128]{1,0:T(8,128)S(1)} %get-tuple-element.36.cumul_ref, f32[128,128]{1,0:T(8,128)S(1)} %get-tuple-element.37.scores_ref, ...), custom_call_target="tpu_custom_call" | custom-call | flops 1342177280 | bytes 3510272 | tf_op jit(solution)/shard_map/grads/pallas_call | solution.py:138
  11.8 1.3 %collective-permute-start.4 = (f32[136,128]{1,0:T(8,128)S(1)}, f32[136,128]{1,0:T(8,128)S(1)}, u32[]{:S(2)}, u32[]{:S(2)}) collective-permute-start(f32[136,128]{1,0:T(8,128)S(1)} %get-tuple-element.47), channel_id=1, source_target_pairs={{1,0},{3,2},{5,4},{7,6},{9,8},{11,10},{13,12},{15,14},{17,16},{19,... | collective-permute-start | bytes 208904 | tf_op jit(solution)/shard_map/ppermute | solution.py:305
  13.1 0.0 collective-permute-done.5.received_ref
  13.1 0.3 kept_shares.1
  13.4 2.1 %collective-permute-done.2 = f32[384,128]{1,0:T(8,128)S(1)} collective-permute-done((f32[384,128]{1,0:T(8,128)S(1)}, f32[384,128]{1,0:T(8,128)S(1)}, u32[]{:S(2)}, u32[]{:S(2)}) %collective-permute-start.2) | collective-permute-done | bytes 196640 | tf_op jit(solution)/shard_map/ppermute | solution.py:272
  15.6 0.5 %collective-permute-start.8 = (f32[192,128]{1,0:T(8,128)S(1)}, f32[192,128]{1,0:T(8,128)S(1)}, u32[]{:S(2)}, u32[]{:S(2)}) collective-permute-start(f32[192,128]{1,0:T(8,128)S(1)} %get-tuple-element.64), channel_id=1, source_target_pairs={{0,2},{1,5},{2,0},{3,7},{4,6},{5,1},{6,4},{7,3},{8,10},{9,13},{10,... | collective-permute-start | bytes 294920 | tf_op jit(solution)/shard_map/ppermute | solution.py:272
  16.1 0.0 collective-permute-done.4.later_ref
  16.1 0.0 collective-permute-done.3
  16.1 1.6 %collective-permute-start.6 = (f32[448,128]{1,0:T(8,128)S(1)}, f32[448,128]{1,0:T(8,128)S(1)}, u32[]{:S(2)}, u32[]{:S(2)}) collective-permute-start(f32[448,128]{1,0:T(8,128)S(1)} %get-tuple-element.60), channel_id=1, source_target_pairs={{0,4},{1,3},{2,6},{3,1},{4,0},{5,7},{6,2},{7,5},{8,12},{9,11},{10,... | collective-permute-start | bytes 688136 | tf_op jit(solution)/shard_map/ppermute | solution.py:272
  17.8 3.5 %collective-permute-done.8 = f32[192,128]{1,0:T(8,128)S(1)} collective-permute-done((f32[192,128]{1,0:T(8,128)S(1)}, f32[192,128]{1,0:T(8,128)S(1)}, u32[]{:S(2)}, u32[]{:S(2)}) %collective-permute-start.8) | collective-permute-done | bytes 98336 | tf_op jit(solution)/shard_map/ppermute | solution.py:272
  21.3 0.5 %collective-permute-start.9 = (f32[96,128]{1,0:T(8,128)S(1)}, f32[96,128]{1,0:T(8,128)S(1)}, u32[]{:S(2)}, u32[]{:S(2)}) collective-permute-start(f32[96,128]{1,0:T(8,128)S(1)} %get-tuple-element.66), channel_id=1, source_target_pairs={{0,4},{1,3},{2,6},{3,1},{4,0},{5,7},{6,2},{7,5},{8,12},{9,11},{10,... | collective-permute-start | bytes 147464 | tf_op jit(solution)/shard_map/ppermute | solution.py:272
  21.8 1.0 %finish.1 = (bf16[1,128,128]{2,1,0:T(8,128)(2,1)}, bf16[1,128,128]{2,1,0:T(8,128)(2,1)}, f32[1,128,128]{2,1,0:T(8,128)}) custom-call(f32[4,128,128]{2,1,0:T(8,128)S(1)} %copy-done.2, f32[128,128]{1,0:T(8,128)S(1)} %get-tuple-element.36.cumul_ref, f32[128,128]{1,0:T(8,128)S(1)} %get-tuple-element.43.grad_key_ref, ...), custom_call_target="tpu_custom_call" | custom-call | flops 671088640 | bytes 724992 | tf_op jit(solution)/shard_map/finish/pallas_call | solution.py:138
  22.8 0.0 collective-permute-done.6
  22.8 1.9 %collective-permute-start.7 = (f32[224,128]{1,0:T(8,128)S(1)}, f32[224,128]{1,0:T(8,128)S(1)}, u32[]{:S(2)}, u32[]{:S(2)}) collective-permute-start(f32[224,128]{1,0:T(8,128)S(1)} %get-tuple-element.62), channel_id=1, source_target_pairs={{0,8},{1,9},{2,10},{3,11},{4,12},{5,13},{6,14},{7,15},{8,0},{9,1},... | collective-permute-start | bytes 344072 | tf_op jit(solution)/shard_map/ppermute | solution.py:272
  24.8 0.7 %collective-permute-done.9 = f32[96,128]{1,0:T(8,128)S(1)} collective-permute-done((f32[96,128]{1,0:T(8,128)S(1)}, f32[96,128]{1,0:T(8,128)S(1)}, u32[]{:S(2)}, u32[]{:S(2)}) %collective-permute-start.9) | collective-permute-done | bytes 49184 | tf_op jit(solution)/shard_map/ppermute | solution.py:272
  25.5 2.2 %collective-permute-done.7 = f32[224,128]{1,0:T(8,128)S(1)} collective-permute-done((f32[224,128]{1,0:T(8,128)S(1)}, f32[224,128]{1,0:T(8,128)S(1)}, u32[]{:S(2)}, u32[]{:S(2)}) %collective-permute-start.7) | collective-permute-done | bytes 114720 | tf_op jit(solution)/shard_map/ppermute | solution.py:272
  27.7 3.0 %collective-permute-start.10 = (f32[160,128]{1,0:T(8,128)S(1)}, f32[160,128]{1,0:T(8,128)S(1)}, u32[]{:S(2)}, u32[]{:S(2)}) collective-permute-start(f32[160,128]{1,0:T(8,128)S(1)} %pad_maximum_fusion.1), channel_id=1, source_target_pairs={{0,16},{1,17},{2,18},{3,19},{4,20},{5,21},{6,22},{7,23},{8,24},{9,... | collective-permute-start | bytes 245768 | tf_op jit(solution)/shard_map/ppermute | solution.py:272
  30.7 2.4 %collective-permute-done.10 = f32[160,128]{1,0:T(8,128)S(1)} collective-permute-done((f32[160,128]{1,0:T(8,128)S(1)}, f32[160,128]{1,0:T(8,128)S(1)}, u32[]{:S(2)}, u32[]{:S(2)}) %collective-permute-start.10) | collective-permute-done | bytes 81952 | tf_op jit(solution)/shard_map/ppermute | solution.py:272
  33.1 0.1 collective-permute-start.11
  33.2 1.3 %collective-permute-done.11 = f32[160,128]{1,0:T(8,128)S(1)} collective-permute-done((f32[160,128]{1,0:T(8,128)S(1)}, f32[160,128]{1,0:T(8,128)S(1)}, u32[]{:S(2)}, u32[]{:S(2)}) %collective-permute-start.11) | collective-permute-done | bytes 81952 | tf_op jit(solution)/shard_map/ppermute | solution.py:150
  34.5 0.7 %pad_maximum_fusion = f32[320,128]{1,0:T(8,128)} fusion(f32[160,128]{1,0:T(8,128)S(1)} %get-tuple-element.68, f32[160,128]{1,0:T(8,128)S(1)} %get-tuple-element.67), kind=kLoop, calls=%fused_computation.2 | loop fusion | flops 40960 | bytes 327680 | tf_op jit(solution)/shard_map/concatenate | solution.py:419
  (11 shorter events, 0.2 us)
Async XLA Ops:
  0.6 2.2 %copy-start = (bf16[1,128,5120]{2,1,0:T(8,128)(2,1)S(1)}, bf16[1,128,5120]{2,1,0:T(8,128)(2,1)}, u32[]{:S(2)}) copy-start(bf16[1,128,5120]{2,1,0:T(8,128)(2,1)} %upstream_ref.3) | copy-start | bytes 3932164
  2.3 1.9 %copy-start.2 = (f32[4,128,128]{2,1,0:T(8,128)S(1)}, f32[4,128,128]{2,1,0:T(8,128)}, u32[]{:S(2)}) copy-start(f32[4,128,128]{2,1,0:T(8,128)} %pack.1.own_ref.packed_ref) | copy-start | bytes 786436
  2.4 1.9 %collective-permute-start.1 = (f32[4,128,128]{2,1,0:T(8,128)}, f32[4,128,128]{2,1,0:T(8,128)S(1)}, u32[]{:S(2)}, u32[]{:S(2)}) collective-permute-start(f32[4,128,128]{2,1,0:T(8,128)} %pack.1.own_ref.packed_ref), channel_id=1, source_target_pairs={{0,1},{1,0},{2,3},{3,2},{4,5},{5,4},{6,7},{7,6},{8,9},{9,8},{10,11... | collective-permute-start | bytes 786440 | tf_op jit(solution)/shard_map/ppermute | solution.py:150
  3.4 2.2 %collective-permute-start = (f32[1280,128]{1,0:T(8,128)S(1)}, f32[1280,128]{1,0:T(8,128)S(1)}, u32[]{:S(2)}, u32[]{:S(2)}) collective-permute-start(f32[1280,128]{1,0:T(8,128)S(1)} %get-tuple-element.33), channel_id=1, source_target_pairs={{0,1},{1,0},{2,3},{3,2},{4,5},{5,4},{6,7},{7,6},{8,9},{9,8},{10,11... | collective-permute-start | bytes 1966088 | tf_op jit(solution)/shard_map/ppermute | solution.py:150
  3.6 9.5 %collective-permute-start.5 = (f32[1280,128]{1,0:T(8,128)S(1)}, f32[1280,128]{1,0:T(8,128)S(1)}, u32[]{:S(2)}, u32[]{:S(2)}) collective-permute-start(f32[1280,128]{1,0:T(8,128)S(1)} %get-tuple-element.51), channel_id=1, source_target_pairs={{0,1},{1,0},{2,3},{3,2},{4,5},{5,4},{6,7},{7,6},{8,9},{9,8},{10,11... | collective-permute-start | bytes 1966088 | tf_op jit(solution)/shard_map/ppermute | solution.py:150
  5.2 5.0 %copy-start.1 = (bf16[5120,128]{1,0:T(8,128)(2,1)S(1)}, bf16[5120,128]{1,0:T(8,128)(2,1)}, u32[]{:S(2)}) copy-start(bf16[5120,128]{1,0:T(8,128)(2,1)} %weight_ref.1) | copy-start | bytes 3932164
  5.9 10.2 %collective-permute-start.3 = (f32[896,128]{1,0:T(8,128)S(1)}, f32[896,128]{1,0:T(8,128)S(1)}, u32[]{:S(2)}, u32[]{:S(2)}) collective-permute-start(f32[896,128]{1,0:T(8,128)S(1)} %get-tuple-element.46), channel_id=1, source_target_pairs={{0,2},{1,5},{2,0},{3,7},{4,6},{5,1},{6,4},{7,3},{8,10},{9,13},{10,... | collective-permute-start | bytes 1376264 | tf_op jit(solution)/shard_map/ppermute | solution.py:272
  8.6 6.9 %collective-permute-start.2 = (f32[384,128]{1,0:T(8,128)S(1)}, f32[384,128]{1,0:T(8,128)S(1)}, u32[]{:S(2)}, u32[]{:S(2)}) collective-permute-start(f32[384,128]{1,0:T(8,128)S(1)} %get-tuple-element.35), channel_id=1, source_target_pairs={{0,8},{1,9},{2,10},{3,11},{4,12},{5,13},{6,14},{7,15},{8,0},{9,1},... | collective-permute-start | bytes 589832 | tf_op jit(solution)/shard_map/ppermute | solution.py:272
  11.8 4.3 %collective-permute-start.4 = (f32[136,128]{1,0:T(8,128)S(1)}, f32[136,128]{1,0:T(8,128)S(1)}, u32[]{:S(2)}, u32[]{:S(2)}) collective-permute-start(f32[136,128]{1,0:T(8,128)S(1)} %get-tuple-element.47), channel_id=1, source_target_pairs={{1,0},{3,2},{5,4},{7,6},{9,8},{11,10},{13,12},{15,14},{17,16},{19,... | collective-permute-start | bytes 208904 | tf_op jit(solution)/shard_map/ppermute | solution.py:305
  15.6 5.7 %collective-permute-start.8 = (f32[192,128]{1,0:T(8,128)S(1)}, f32[192,128]{1,0:T(8,128)S(1)}, u32[]{:S(2)}, u32[]{:S(2)}) collective-permute-start(f32[192,128]{1,0:T(8,128)S(1)} %get-tuple-element.64), channel_id=1, source_target_pairs={{0,2},{1,5},{2,0},{3,7},{4,6},{5,1},{6,4},{7,3},{8,10},{9,13},{10,... | collective-permute-start | bytes 294920 | tf_op jit(solution)/shard_map/ppermute | solution.py:272
  16.1 6.6 %collective-permute-start.6 = (f32[448,128]{1,0:T(8,128)S(1)}, f32[448,128]{1,0:T(8,128)S(1)}, u32[]{:S(2)}, u32[]{:S(2)}) collective-permute-start(f32[448,128]{1,0:T(8,128)S(1)} %get-tuple-element.60), channel_id=1, source_target_pairs={{0,4},{1,3},{2,6},{3,1},{4,0},{5,7},{6,2},{7,5},{8,12},{9,11},{10,... | collective-permute-start | bytes 688136 | tf_op jit(solution)/shard_map/ppermute | solution.py:272
  21.3 4.2 %collective-permute-start.9 = (f32[96,128]{1,0:T(8,128)S(1)}, f32[96,128]{1,0:T(8,128)S(1)}, u32[]{:S(2)}, u32[]{:S(2)}) collective-permute-start(f32[96,128]{1,0:T(8,128)S(1)} %get-tuple-element.66), channel_id=1, source_target_pairs={{0,4},{1,3},{2,6},{3,1},{4,0},{5,7},{6,2},{7,5},{8,12},{9,11},{10,... | collective-permute-start | bytes 147464 | tf_op jit(solution)/shard_map/ppermute | solution.py:272
  22.8 4.9 %collective-permute-start.7 = (f32[224,128]{1,0:T(8,128)S(1)}, f32[224,128]{1,0:T(8,128)S(1)}, u32[]{:S(2)}, u32[]{:S(2)}) collective-permute-start(f32[224,128]{1,0:T(8,128)S(1)} %get-tuple-element.62), channel_id=1, source_target_pairs={{0,8},{1,9},{2,10},{3,11},{4,12},{5,13},{6,14},{7,15},{8,0},{9,1},... | collective-permute-start | bytes 344072 | tf_op jit(solution)/shard_map/ppermute | solution.py:272
  27.7 5.4 %collective-permute-start.10 = (f32[160,128]{1,0:T(8,128)S(1)}, f32[160,128]{1,0:T(8,128)S(1)}, u32[]{:S(2)}, u32[]{:S(2)}) collective-permute-start(f32[160,128]{1,0:T(8,128)S(1)} %pad_maximum_fusion.1), channel_id=1, source_target_pairs={{0,16},{1,17},{2,18},{3,19},{4,20},{5,21},{6,22},{7,23},{8,24},{9,... | collective-permute-start | bytes 245768 | tf_op jit(solution)/shard_map/ppermute | solution.py:272
  33.1 1.3 %collective-permute-start.11 = (f32[160,128]{1,0:T(8,128)S(1)}, f32[160,128]{1,0:T(8,128)S(1)}, u32[]{:S(2)}, u32[]{:S(2)}) collective-permute-start(f32[160,128]{1,0:T(8,128)S(1)} %pad_maximum_fusion.2), channel_id=1, source_target_pairs={{0,1},{1,0},{2,3},{3,2},{4,5},{5,4},{6,7},{7,6},{8,9},{9,8},{10,11... | collective-permute-start | bytes 245768 | tf_op jit(solution)/shard_map/ppermute | solution.py:150

commit v3 on v2

--- a/solution.py
+++ b/solution.py
@@ -152,11 +152,11 @@
 
 def halving_plan(count, rows):
     bits = count.bit_length() - 1
-    last = rows // 3 // 16 * 16
+    last = rows // 32 * 16
     rest = list(range(3, bits))
     return [
         (rows - last, ([0, 1, 2] + rest, [1, 0, 2] + rest)),
-        (last, ([2, 0, 1] + rest, [2, 1, 0] + rest)),
+        (last, ([1, 2, 0] + rest, [2, 0, 1] + rest)),
     ]
 
 
@@ -292,6 +292,8 @@
     for stage in range(joined, stages):
         sizes = [len(part) for part in sent]
         new = exchanged(jnp.concatenate(sent), count, [stage] * 2)
+        if stage in beside:
+            new = beside[stage](new)
         starts = [sum(sizes[:index]) for index in range(len(sizes))]
         sums = [part + new[at:at + size] for part, at, size in zip(kept, starts, sizes)]
         kept = [part[: len(part) // 2] if stage + 1 < stages else part for part in sums]
@@ -312,7 +314,7 @@
     square = (length, width)
     rows = model // count // 2
     flops = 8 * length * width * model
-    paired = shards == 2 and count >= 8 and count & (count - 1) == 0 and rows % 16 == 0
+    paired = shards == 2 and count >= 16 and count & (count - 1) == 0 and rows % 16 == 0
 
     (packed,) = local_call(
         pack_kernel,
@@ -401,17 +403,21 @@
         def beside_first(arrived):
             large, small = arrived
             small, held["query"] = lax.optimization_barrier((small, grad_query))
+            return [large, small]
+
+        def beside_third(arrived):
+            large, small = arrived
             large, held["later"] = lax.optimization_barrier((large, later))
             return [large, small]
 
-        def beside_second(arrived):
-            large, small = arrived
+        def beside_last(arrived):
             key, value, decay = finish(held["later"])
-            large, decay = lax.optimization_barrier((large, decay))
+            arrived, decay = lax.optimization_barrier((arrived, decay))
             held["finished"] = key, value, decay
-            return [large, small]
-
-        mine = halving(kept=kept, sent=sent, plan=plan, count=count, beside={0: beside_first, 1: beside_second})
+            return arrived
+
+        beside = {0: beside_first, 2: beside_third, 3: beside_last}
+        mine = halving(kept, sent, plan, count, beside)
         grad_query = held["query"]
         grad_key, grad_value, grad_decay = held["finished"]
         theirs = swap(mine)

time: 35.3 us -> 35.5 us (level)
  starting transfers between devices: 14.2 us -> 17.4 us
  waiting for transfers between devices: 12.8 us -> 9.8 us
    ppermute x7, waiting for transfers between devices: 11 us -> 7.01 us  [exchanged(): return lax.ppermute(value, BOTH, pairs)]
    ppermute x7, starting transfers between devices: 11.8 us -> 15 us  [exchanged(): return lax.ppermute(value, BOTH, pairs)]
    ppermute x4, waiting for transfers between devices: 1.86 us -> 2.8 us  [swap(): return lax.ppermute(value, 'ctx', [(0, 1), (1, 0)])]
  transfers between devices with their start and end apart: 12 -> 12, of which waited for: 8 -> 9; matrix products, arithmetic and copies ran while one was open for 0% -> 0% of each run, Pallas kernels for 14% -> 13%
where the time goes in v3:
time: 35.5 us; the launch traced here: 35.3 us
  starting transfers between devices  17.4 us (49%)
  waiting for transfers between devices  9.8 us (28%)
  Pallas kernels  6.45 us (18%)
  other arithmetic  0.89 us (3%)
  between operations  0.76 us (2%)
    ppermute x7, starting transfers between devices, exchanged(): return lax.ppermute(value, BOTH, pairs)  15 us
    ppermute x7, waiting for transfers between devices, exchanged(): return lax.ppermute(value, BOTH, pairs)  7.01 us
    pallas_call x7, Pallas kernels, local_call(): pl.pallas_call(kernel, out_shape=outs, in_specs=[pl.BlockSpec(memory_spac...  6.45 us
    ppermute x4, waiting for transfers between devices, swap(): return lax.ppermute(value, 'ctx', [(0, 1), (1, 0)])  2.8 us
    ppermute x1, starting transfers between devices, shifted(): lax.ppermute(value, axis, [(source, source + steps) for source in range(l...  1.28 us
    ppermute x4, starting transfers between devices, swap(): return lax.ppermute(value, 'ctx', [(0, 1), (1, 0)])  1.16 us
  transfers between devices with their start and end apart: 12, of which 9 were waited for; matrix products, arithmetic and copies ran while one was open for 0% of the time, Pallas kernels for 13%

profile of v3, /device:TPU:0, one launch (start us, length us, event | category | flops | bytes accessed | tf_op | source)
XLA Modules:
  0.0 35.3 jit_solution(598586155539300368)
XLA Ops:
  0.6 0.0 copy-start
  0.6 1.7 %pack.1.own_ref.packed_ref = f32[4,128,128]{2,1,0:T(8,128)} custom-call(bf16[1,128,128]{2,1,0:T(8,128)(2,1)} %query_ref.1, bf16[1,128,128]{2,1,0:T(8,128)(2,1)} %key_ref.1, bf16[1,128,128]{2,1,0:T(8,128)(2,1)} %value_ref.1, f32[1,128,128]{2,1,0:T(8,128)} %decay_ref.1), custom_call_target="tpu_custom_call" | custom-call | flops 13421772800 | bytes 425984 | tf_op jit(solution)/shard_map/pack/pallas_call | solution.py:138
  2.3 0.0 copy-start.2
  2.4 0.5 %collective-permute-start.1 = (f32[4,128,128]{2,1,0:T(8,128)}, f32[4,128,128]{2,1,0:T(8,128)S(1)}, u32[]{:S(2)}, u32[]{:S(2)}) collective-permute-start(f32[4,128,128]{2,1,0:T(8,128)} %pack.1.own_ref.packed_ref), channel_id=1, source_target_pairs={{0,1},{1,0},{2,3},{3,2},{4,5},{5,4},{6,7},{7,6},{8,9},{9,8},{10,11... | collective-permute-start | bytes 786440 | tf_op jit(solution)/shard_map/ppermute | solution.py:150
  2.9 0.0 copy-done
  2.9 0.6 %turn.1 = (bf16[2560,128]{1,0:T(8,128)(2,1)S(1)}, f32[1280,128]{1,0:T(8,128)S(1)}, f32[1280,128]{1,0:T(8,128)S(1)}) custom-call(bf16[1,128,5120]{2,1,0:T(8,128)(2,1)S(1)} %copy-done), custom_call_target="tpu_custom_call" | custom-call | flops 13421772800 | bytes 3276800 | tf_op jit(solution)/shard_map/turn/pallas_call | solution.py:138
  3.4 0.1 collective-permute-start.3
  3.6 0.5 %collective-permute-start = (f32[1280,128]{1,0:T(8,128)S(1)}, f32[1280,128]{1,0:T(8,128)S(1)}, u32[]{:S(2)}, u32[]{:S(2)}) collective-permute-start(f32[1280,128]{1,0:T(8,128)S(1)} %get-tuple-element.33), channel_id=1, source_target_pairs={{0,1},{1,0},{2,3},{3,2},{4,5},{5,4},{6,7},{7,6},{8,9},{9,8},{10,11... | collective-permute-start | bytes 1966088 | tf_op jit(solution)/shard_map/ppermute | solution.py:150
  4.0 0.2 collective-permute-done.1.other_ref
  4.2 0.0 copy-done.2
  4.3 1.0 %joint.1 = (f32[128,128]{1,0:T(8,128)S(1)}, f32[128,128]{1,0:T(8,128)S(1)}, f32[128,128]{1,0:T(8,128)S(1)}, f32[128,128]{1,0:T(8,128)S(1)}, f32[128,128]{1,0:T(8,128)S(1)}, /*index=5*/bf16[256,128]{1,0:T(8,128)(2,1)S(1)}) custom-call(f32[4,128,128]{2,1,0:T(8,128)S(1)} %copy-done.2, f32[4,128,128]{2,1,0:T(8,128)S(1)} %collective-permute-done.1.other_ref), custom_call_target="tpu_custom_call" | custom-call | flops 26843545600 | bytes 917504 | tf_op jit(solution)/shard_map/joint/pallas_call | solution.py:138
  5.2 0.0 copy-start.1
  5.2 1.3 %collective-permute-done.received_ref = f32[1280,128]{1,0:T(8,128)S(1)} collective-permute-done((f32[1280,128]{1,0:T(8,128)S(1)}, f32[1280,128]{1,0:T(8,128)S(1)}, u32[]{:S(2)}, u32[]{:S(2)}) %collective-permute-start) | collective-permute-done | bytes 655392 | tf_op jit(solution)/shard_map/ppermute | solution.py:150
  6.5 0.3 sent_shares.1
  6.9 2.7 %collective-permute-start.4 = (f32[640,128]{1,0:T(8,128)S(1)}, f32[640,128]{1,0:T(8,128)S(1)}, u32[]{:S(2)}, u32[]{:S(2)}) collective-permute-start(f32[640,128]{1,0:T(8,128)S(1)} %get-tuple-element.48), channel_id=1, source_target_pairs={{0,2},{1,5},{2,0},{3,7},{4,6},{5,1},{6,4},{7,3},{8,10},{9,13},{10,... | collective-permute-start | bytes 983048 | tf_op jit(solution)/shard_map/ppermute | solution.py:272
  9.6 1.5 %collective-permute-start.2 = (f32[640,128]{1,0:T(8,128)S(1)}, f32[640,128]{1,0:T(8,128)S(1)}, u32[]{:S(2)}, u32[]{:S(2)}) collective-permute-start(f32[640,128]{1,0:T(8,128)S(1)} %get-tuple-element.35), channel_id=1, source_target_pairs={{0,4},{1,9},{2,6},{3,11},{4,0},{5,13},{6,2},{7,15},{8,12},{9,1},{1... | collective-permute-start | bytes 983048 | tf_op jit(solution)/shard_map/ppermute | solution.py:272
  11.1 0.0 copy-done.1
  11.1 1.6 %grads.1 = (bf16[1,128,128]{2,1,0:T(8,128)(2,1)}, f32[128,128]{1,0:T(8,128)S(1)}, f32[128,128]{1,0:T(8,128)S(1)}, f32[128,128]{1,0:T(8,128)S(1)}, f32[136,128]{1,0:T(8,128)S(1)}) custom-call(f32[4,128,128]{2,1,0:T(8,128)S(1)} %copy-done.2, f32[128,128]{1,0:T(8,128)S(1)} %get-tuple-element.36.cumul_ref, f32[128,128]{1,0:T(8,128)S(1)} %get-tuple-element.37.scores_ref, ...), custom_call_target="tpu_custom_call" | custom-call | flops 1342177280 | bytes 3510272 | tf_op jit(solution)/shard_map/grads/pallas_call | solution.py:138
  12.7 1.3 %collective-permute-start.7 = (f32[136,128]{1,0:T(8,128)S(1)}, f32[136,128]{1,0:T(8,128)S(1)}, u32[]{:S(2)}, u32[]{:S(2)}) collective-permute-start(f32[136,128]{1,0:T(8,128)S(1)} %get-tuple-element.49), channel_id=1, source_target_pairs={{1,0},{3,2},{5,4},{7,6},{9,8},{11,10},{13,12},{15,14},{17,16},{19,... | collective-permute-start | bytes 208904 | tf_op jit(solution)/shard_map/ppermute | solution.py:307
  14.0 0.0 collective-permute-done.3.received_ref
  14.0 0.3 kept_shares.1
  14.3 0.3 collective-permute-done.4
  14.6 0.1 slice_add_fusion.1
  14.7 2.1 %collective-permute-start.5 = (f32[320,128]{1,0:T(8,128)S(1)}, f32[320,128]{1,0:T(8,128)S(1)}, u32[]{:S(2)}, u32[]{:S(2)}) collective-permute-start(f32[320,128]{1,0:T(8,128)S(1)} %get-tuple-element.62), channel_id=1, source_target_pairs={{0,4},{1,3},{2,6},{3,1},{4,0},{5,7},{6,2},{7,5},{8,12},{9,11},{10,... | collective-permute-start | bytes 491528 | tf_op jit(solution)/shard_map/ppermute | solution.py:272
  16.8 1.1 %collective-permute-done.2 = f32[640,128]{1,0:T(8,128)S(1)} collective-permute-done((f32[640,128]{1,0:T(8,128)S(1)}, f32[640,128]{1,0:T(8,128)S(1)}, u32[]{:S(2)}, u32[]{:S(2)}) %collective-permute-start.2) | collective-permute-done | bytes 327712 | tf_op jit(solution)/shard_map/ppermute | solution.py:272
  17.8 0.1 slice_add_fusion.3
  17.9 1.9 %collective-permute-start.8 = (f32[320,128]{1,0:T(8,128)S(1)}, f32[320,128]{1,0:T(8,128)S(1)}, u32[]{:S(2)}, u32[]{:S(2)}) collective-permute-start(f32[320,128]{1,0:T(8,128)S(1)} %get-tuple-element.60), channel_id=1, source_target_pairs={{0,8},{1,3},{2,10},{3,1},{4,12},{5,7},{6,14},{7,5},{8,0},{9,11},{1... | collective-permute-start | bytes 491528 | tf_op jit(solution)/shard_map/ppermute | solution.py:272
  19.7 0.3 collective-permute-done.5
  20.1 2.1 %collective-permute-start.6 = (f32[160,128]{1,0:T(8,128)S(1)}, f32[160,128]{1,0:T(8,128)S(1)}, u32[]{:S(2)}, u32[]{:S(2)}) collective-permute-start(f32[160,128]{1,0:T(8,128)S(1)} %get-tuple-element.64), channel_id=1, source_target_pairs={{0,8},{1,9},{2,10},{3,11},{4,12},{5,13},{6,14},{7,15},{8,0},{9,1},... | collective-permute-start | bytes 245768 | tf_op jit(solution)/shard_map/ppermute | solution.py:272
  22.2 1.0 %collective-permute-done.8 = f32[320,128]{1,0:T(8,128)S(1)} collective-permute-done((f32[320,128]{1,0:T(8,128)S(1)}, f32[320,128]{1,0:T(8,128)S(1)}, u32[]{:S(2)}, u32[]{:S(2)}) %collective-permute-start.8) | collective-permute-done | bytes 163872 | tf_op jit(solution)/shard_map/ppermute | solution.py:272
  23.3 1.8 %collective-permute-start.9 = (f32[160,128]{1,0:T(8,128)S(1)}, f32[160,128]{1,0:T(8,128)S(1)}, u32[]{:S(2)}, u32[]{:S(2)}) collective-permute-start(f32[160,128]{1,0:T(8,128)S(1)} %get-tuple-element.66), channel_id=1, source_target_pairs={{0,2},{1,5},{2,0},{3,7},{4,6},{5,1},{6,4},{7,3},{8,10},{9,13},{10,... | collective-permute-start | bytes 245768 | tf_op jit(solution)/shard_map/ppermute | solution.py:272
  25.1 0.0 collective-permute-done.7.later_ref
  25.1 0.0 collective-permute-done.6
  25.1 2.7 %collective-permute-done.9 = f32[160,128]{1,0:T(8,128)S(1)} collective-permute-done((f32[160,128]{1,0:T(8,128)S(1)}, f32[160,128]{1,0:T(8,128)S(1)}, u32[]{:S(2)}, u32[]{:S(2)}) %collective-permute-start.9) | collective-permute-done | bytes 81952 | tf_op jit(solution)/shard_map/ppermute | solution.py:272
  27.8 2.9 %collective-permute-start.10 = (f32[160,128]{1,0:T(8,128)S(1)}, f32[160,128]{1,0:T(8,128)S(1)}, u32[]{:S(2)}, u32[]{:S(2)}) collective-permute-start(f32[160,128]{1,0:T(8,128)S(1)} %pad_maximum_fusion.1), channel_id=1, source_target_pairs={{0,16},{1,17},{2,18},{3,19},{4,20},{5,21},{6,22},{7,23},{8,24},{9,... | collective-permute-start | bytes 245768 | tf_op jit(solution)/shard_map/ppermute | solution.py:272
  30.7 1.0 %finish.1 = (bf16[1,128,128]{2,1,0:T(8,128)(2,1)}, bf16[1,128,128]{2,1,0:T(8,128)(2,1)}, f32[1,128,128]{2,1,0:T(8,128)}) custom-call(f32[4,128,128]{2,1,0:T(8,128)S(1)} %copy-done.2, f32[128,128]{1,0:T(8,128)S(1)} %get-tuple-element.36.cumul_ref, f32[128,128]{1,0:T(8,128)S(1)} %get-tuple-element.43.grad_key_ref, ...), custom_call_target="tpu_custom_call" | custom-call | flops 671088640 | bytes 724992 | tf_op jit(solution)/shard_map/finish/pallas_call | solution.py:138
  31.7 1.6 %collective-permute-done.10 = f32[160,128]{1,0:T(8,128)S(1)} collective-permute-done((f32[160,128]{1,0:T(8,128)S(1)}, f32[160,128]{1,0:T(8,128)S(1)}, u32[]{:S(2)}, u32[]{:S(2)}) %collective-permute-start.10) | collective-permute-done | bytes 81952 | tf_op jit(solution)/shard_map/ppermute | solution.py:272
  33.3 0.1 collective-permute-start.11
  33.4 1.3 %collective-permute-done.11 = f32[160,128]{1,0:T(8,128)S(1)} collective-permute-done((f32[160,128]{1,0:T(8,128)S(1)}, f32[160,128]{1,0:T(8,128)S(1)}, u32[]{:S(2)}, u32[]{:S(2)}) %collective-permute-start.11) | collective-permute-done | bytes 81952 | tf_op jit(solution)/shard_map/ppermute | solution.py:150
  34.7 0.7 %pad_maximum_fusion = f32[320,128]{1,0:T(8,128)} fusion(f32[160,128]{1,0:T(8,128)S(1)} %get-tuple-element.68, f32[160,128]{1,0:T(8,128)S(1)} %get-tuple-element.67), kind=kLoop, calls=%fused_computation.2 | loop fusion | flops 40960 | bytes 327680 | tf_op jit(solution)/shard_map/concatenate | solution.py:425
  (8 shorter events, 0.1 us)
Async XLA Ops:
  0.6 2.2 %copy-start = (bf16[1,128,5120]{2,1,0:T(8,128)(2,1)S(1)}, bf16[1,128,5120]{2,1,0:T(8,128)(2,1)}, u32[]{:S(2)}) copy-start(bf16[1,128,5120]{2,1,0:T(8,128)(2,1)} %upstream_ref.3) | copy-start | bytes 3932164
  2.3 1.9 %copy-start.2 = (f32[4,128,128]{2,1,0:T(8,128)S(1)}, f32[4,128,128]{2,1,0:T(8,128)}, u32[]{:S(2)}) copy-start(f32[4,128,128]{2,1,0:T(8,128)} %pack.1.own_ref.packed_ref) | copy-start | bytes 786436
  2.4 1.9 %collective-permute-start.1 = (f32[4,128,128]{2,1,0:T(8,128)}, f32[4,128,128]{2,1,0:T(8,128)S(1)}, u32[]{:S(2)}, u32[]{:S(2)}) collective-permute-start(f32[4,128,128]{2,1,0:T(8,128)} %pack.1.own_ref.packed_ref), channel_id=1, source_target_pairs={{0,1},{1,0},{2,3},{3,2},{4,5},{5,4},{6,7},{7,6},{8,9},{9,8},{10,11... | collective-permute-start | bytes 786440 | tf_op jit(solution)/shard_map/ppermute | solution.py:150
  3.4 10.5 %collective-permute-start.3 = (f32[1280,128]{1,0:T(8,128)S(1)}, f32[1280,128]{1,0:T(8,128)S(1)}, u32[]{:S(2)}, u32[]{:S(2)}) collective-permute-start(f32[1280,128]{1,0:T(8,128)S(1)} %get-tuple-element.46), channel_id=1, source_target_pairs={{0,1},{1,0},{2,3},{3,2},{4,5},{5,4},{6,7},{7,6},{8,9},{9,8},{10,11... | collective-permute-start | bytes 1966088 | tf_op jit(solution)/shard_map/ppermute | solution.py:150
  3.6 3.0 %collective-permute-start = (f32[1280,128]{1,0:T(8,128)S(1)}, f32[1280,128]{1,0:T(8,128)S(1)}, u32[]{:S(2)}, u32[]{:S(2)}) collective-permute-start(f32[1280,128]{1,0:T(8,128)S(1)} %get-tuple-element.33), channel_id=1, source_target_pairs={{0,1},{1,0},{2,3},{3,2},{4,5},{5,4},{6,7},{7,6},{8,9},{9,8},{10,11... | collective-permute-start | bytes 1966088 | tf_op jit(solution)/shard_map/ppermute | solution.py:150
  5.2 5.9 %copy-start.1 = (bf16[5120,128]{1,0:T(8,128)(2,1)S(1)}, bf16[5120,128]{1,0:T(8,128)(2,1)}, u32[]{:S(2)}) copy-start(bf16[5120,128]{1,0:T(8,128)(2,1)} %weight_ref.1) | copy-start | bytes 3932164
  6.9 7.8 %collective-permute-start.4 = (f32[640,128]{1,0:T(8,128)S(1)}, f32[640,128]{1,0:T(8,128)S(1)}, u32[]{:S(2)}, u32[]{:S(2)}) collective-permute-start(f32[640,128]{1,0:T(8,128)S(1)} %get-tuple-element.48), channel_id=1, source_target_pairs={{0,2},{1,5},{2,0},{3,7},{4,6},{5,1},{6,4},{7,3},{8,10},{9,13},{10,... | collective-permute-start | bytes 983048 | tf_op jit(solution)/shard_map/ppermute | solution.py:272
  9.6 8.3 %collective-permute-start.2 = (f32[640,128]{1,0:T(8,128)S(1)}, f32[640,128]{1,0:T(8,128)S(1)}, u32[]{:S(2)}, u32[]{:S(2)}) collective-permute-start(f32[640,128]{1,0:T(8,128)S(1)} %get-tuple-element.35), channel_id=1, source_target_pairs={{0,4},{1,9},{2,6},{3,11},{4,0},{5,13},{6,2},{7,15},{8,12},{9,1},{1... | collective-permute-start | bytes 983048 | tf_op jit(solution)/shard_map/ppermute | solution.py:272
  12.7 12.4 %collective-permute-start.7 = (f32[136,128]{1,0:T(8,128)S(1)}, f32[136,128]{1,0:T(8,128)S(1)}, u32[]{:S(2)}, u32[]{:S(2)}) collective-permute-start(f32[136,128]{1,0:T(8,128)S(1)} %get-tuple-element.49), channel_id=1, source_target_pairs={{1,0},{3,2},{5,4},{7,6},{9,8},{11,10},{13,12},{15,14},{17,16},{19,... | collective-permute-start | bytes 208904 | tf_op jit(solution)/shard_map/ppermute | solution.py:307
  14.7 5.4 %collective-permute-start.5 = (f32[320,128]{1,0:T(8,128)S(1)}, f32[320,128]{1,0:T(8,128)S(1)}, u32[]{:S(2)}, u32[]{:S(2)}) collective-permute-start(f32[320,128]{1,0:T(8,128)S(1)} %get-tuple-element.62), channel_id=1, source_target_pairs={{0,4},{1,3},{2,6},{3,1},{4,0},{5,7},{6,2},{7,5},{8,12},{9,11},{10,... | collective-permute-start | bytes 491528 | tf_op jit(solution)/shard_map/ppermute | solution.py:272
  17.9 5.4 %collective-permute-start.8 = (f32[320,128]{1,0:T(8,128)S(1)}, f32[320,128]{1,0:T(8,128)S(1)}, u32[]{:S(2)}, u32[]{:S(2)}) collective-permute-start(f32[320,128]{1,0:T(8,128)S(1)} %get-tuple-element.60), channel_id=1, source_target_pairs={{0,8},{1,3},{2,10},{3,1},{4,12},{5,7},{6,14},{7,5},{8,0},{9,11},{1... | collective-permute-start | bytes 491528 | tf_op jit(solution)/shard_map/ppermute | solution.py:272
  20.1 5.0 %collective-permute-start.6 = (f32[160,128]{1,0:T(8,128)S(1)}, f32[160,128]{1,0:T(8,128)S(1)}, u32[]{:S(2)}, u32[]{:S(2)}) collective-permute-start(f32[160,128]{1,0:T(8,128)S(1)} %get-tuple-element.64), channel_id=1, source_target_pairs={{0,8},{1,9},{2,10},{3,11},{4,12},{5,13},{6,14},{7,15},{8,0},{9,1},... | collective-permute-start | bytes 245768 | tf_op jit(solution)/shard_map/ppermute | solution.py:272
  23.3 4.5 %collective-permute-start.9 = (f32[160,128]{1,0:T(8,128)S(1)}, f32[160,128]{1,0:T(8,128)S(1)}, u32[]{:S(2)}, u32[]{:S(2)}) collective-permute-start(f32[160,128]{1,0:T(8,128)S(1)} %get-tuple-element.66), channel_id=1, source_target_pairs={{0,2},{1,5},{2,0},{3,7},{4,6},{5,1},{6,4},{7,3},{8,10},{9,13},{10,... | collective-permute-start | bytes 245768 | tf_op jit(solution)/shard_map/ppermute | solution.py:272
  27.8 5.5 %collective-permute-start.10 = (f32[160,128]{1,0:T(8,128)S(1)}, f32[160,128]{1,0:T(8,128)S(1)}, u32[]{:S(2)}, u32[]{:S(2)}) collective-permute-start(f32[160,128]{1,0:T(8,128)S(1)} %pad_maximum_fusion.1), channel_id=1, source_target_pairs={{0,16},{1,17},{2,18},{3,19},{4,20},{5,21},{6,22},{7,23},{8,24},{9,... | collective-permute-start | bytes 245768 | tf_op jit(solution)/shard_map/ppermute | solution.py:272
  33.3 1.3 %collective-permute-start.11 = (f32[160,128]{1,0:T(8,128)S(1)}, f32[160,128]{1,0:T(8,128)S(1)}, u32[]{:S(2)}, u32[]{:S(2)}) collective-permute-start(f32[160,128]{1,0:T(8,128)S(1)} %pad_maximum_fusion.2), channel_id=1, source_target_pairs={{0,1},{1,0},{2,3},{3,2},{4,5},{5,4},{6,7},{7,6},{8,9},{9,8},{10,11... | collective-permute-start | bytes 245768 | tf_op jit(solution)/shard_map/ppermute | solution.py:150

commit v4 on v3

--- a/solution.py
+++ b/solution.py
@@ -122,14 +122,16 @@
     cumul = cumul_ref[...]
     width = key.shape[1]
     to_end = jnp.exp(cumul[-1:] - cumul)
-    grad_in = split(later_ref[:width], 2)
+    last = lax.axis_index("ctx") == lax.axis_size("ctx") - 1
+    later = jnp.where(last, 0.0, later_ref[...])
+    grad_in = split(later[:width], 2)
     extra = to_end * product([packed_ref[2].astype(BF16)], grad_in, 1, 1)
     key_out_ref[0] = (grad_key_ref[...] + extra).astype(BF16)
     grad_value = grad_value_ref[...] + product(split(key * to_end, 2), grad_in, 1, 0)
     value_out_ref[0] = grad_value.astype(BF16)
     gate = gate_ref[...] - key * extra
     lower = lower_mask(cumul.shape[0]).astype(F32).astype(BF16)
-    decay_out_ref[0] = product([lower], split(gate, 3), 0, 0) + later_ref[width:width + 1]
+    decay_out_ref[0] = product([lower], split(gate, 3), 0, 0) + later[width:width + 1]
 
 
 def local_call(kernel, shapes, *operands, name, flops, scratch=(), space=pltpu.VMEM, limit=VMEM_BYTES):
@@ -156,7 +158,7 @@
     rest = list(range(3, bits))
     return [
         (rows - last, ([0, 1, 2] + rest, [1, 0, 2] + rest)),
-        (last, ([1, 2, 0] + rest, [2, 0, 1] + rest)),
+        (last, ([2, 0, 1] + rest, [1, 2, 0] + rest)),
     ]
 
 
@@ -335,6 +337,7 @@
         )
         others = swap(packed)
         received_first = swap(send_first)
+        others, send_second = lax.optimization_barrier((others, send_second))
         received_second = swap(send_second)
         cumul, scores, state_in, normed, scale_inv, rounded = local_call(
             joint_kernel,
@@ -387,7 +390,7 @@
         cotangent, out_weight,
         name="grads", flops=2 * flops,
     )
-    later = shifted(grad_sent, "ctx", -1)
+    later = swap(grad_sent) if paired else shifted(grad_sent, "ctx", -1)
 
     def finish(later):
         return local_call(

time: 35.5 us -> 33.7 us (0.949)
  starting transfers between devices: 17.4 us -> 15.4 us
    ppermute x1 -> x0, starting transfers between devices: 1.28 us -> none  [shifted(): lax.ppermute(value, axis, [(source, source + steps) for source in range(l...]
    ppermute x7, waiting for transfers between devices: 7.01 us -> 8.06 us  [exchanged(): return lax.ppermute(value, BOTH, pairs)]
    ppermute x4 -> x5, waiting for transfers between devices: 2.8 us -> 1.95 us  [swap(): return lax.ppermute(value, 'ctx', [(0, 1), (1, 0)])]
    ppermute x7, starting transfers between devices: 15 us -> 14.3 us  [exchanged(): return lax.ppermute(value, BOTH, pairs)]
    ppermute x4 -> x5, starting transfers between devices: 1.16 us -> 1.09 us  [swap(): return lax.ppermute(value, 'ctx', [(0, 1), (1, 0)])]
  transfers between devices with their start and end apart: 12 -> 12, of which waited for: 9 -> 7; matrix products, arithmetic and copies ran while one was open for 0% -> 0% of each run, Pallas kernels for 13% -> 14%
where the time goes in v4:
time: 33.7 us; the launch traced here: 33.5 us
  starting transfers between devices  15.4 us (46%)
  waiting for transfers between devices  10 us (30%)
  Pallas kernels  6.46 us (19%)
  other arithmetic  0.87 us (3%)
  between operations  0.76 us (2%)
    ppermute x7, starting transfers between devices, exchanged(): return lax.ppermute(value, BOTH, pairs)  14.3 us
    ppermute x7, waiting for transfers between devices, exchanged(): return lax.ppermute(value, BOTH, pairs)  8.06 us
    pallas_call x7, Pallas kernels, local_call(): pl.pallas_call(kernel, out_shape=outs, in_specs=[pl.BlockSpec(memory_spac...  6.46 us
    ppermute x5, waiting for transfers between devices, swap(): return lax.ppermute(value, 'ctx', [(0, 1), (1, 0)])  1.95 us
    ppermute x5, starting transfers between devices, swap(): return lax.ppermute(value, 'ctx', [(0, 1), (1, 0)])  1.09 us
    concatenate x1, other arithmetic, body(): jnp.concatenate([jnp.where(first, mine, theirs), jnp.where(first, theirs,...  0.68 us
  transfers between devices with their start and end apart: 12, of which 7 were waited for; matrix products, arithmetic and copies ran while one was open for 0% of the time, Pallas kernels for 14%

profile of v4, /device:TPU:0, one launch (start us, length us, event | category | flops | bytes accessed | tf_op | source)
XLA Modules:
  0.0 33.5 jit_solution(3826978337118202715)
XLA Ops:
  0.6 0.0 copy-start
  0.6 1.7 %pack.1.own_ref.packed_ref = f32[4,128,128]{2,1,0:T(8,128)} custom-call(bf16[1,128,128]{2,1,0:T(8,128)(2,1)} %query_ref.1, bf16[1,128,128]{2,1,0:T(8,128)(2,1)} %key_ref.1, bf16[1,128,128]{2,1,0:T(8,128)(2,1)} %value_ref.1, f32[1,128,128]{2,1,0:T(8,128)} %decay_ref.1), custom_call_target="tpu_custom_call" | custom-call | flops 13421772800 | bytes 425984 | tf_op jit(solution)/shard_map/pack/pallas_call | solution.py:140
  2.3 0.0 copy-start.2
  2.4 0.5 %collective-permute-start.1 = (f32[4,128,128]{2,1,0:T(8,128)}, f32[4,128,128]{2,1,0:T(8,128)S(1)}, u32[]{:S(2)}, u32[]{:S(2)}) collective-permute-start(f32[4,128,128]{2,1,0:T(8,128)} %pack.1.own_ref.packed_ref), channel_id=1, source_target_pairs={{0,1},{1,0},{2,3},{3,2},{4,5},{5,4},{6,7},{7,6},{8,9},{9,8},{10,11... | collective-permute-start | bytes 786440 | tf_op jit(solution)/shard_map/ppermute | solution.py:152
  2.9 0.0 copy-done
  2.9 0.6 %turn.1 = (bf16[2560,128]{1,0:T(8,128)(2,1)S(1)}, f32[1280,128]{1,0:T(8,128)S(1)}, f32[1280,128]{1,0:T(8,128)S(1)}) custom-call(bf16[1,128,5120]{2,1,0:T(8,128)(2,1)S(1)} %copy-done), custom_call_target="tpu_custom_call" | custom-call | flops 13421772800 | bytes 3276800 | tf_op jit(solution)/shard_map/turn/pallas_call | solution.py:140
  3.4 0.1 collective-permute-start
  3.6 0.7 %collective-permute-done.1.other_ref = f32[4,128,128]{2,1,0:T(8,128)S(1)} collective-permute-done((f32[4,128,128]{2,1,0:T(8,128)}, f32[4,128,128]{2,1,0:T(8,128)S(1)}, u32[]{:S(2)}, u32[]{:S(2)}) %collective-permute-start.1) | collective-permute-done | bytes 262176 | tf_op jit(solution)/shard_map/ppermute | solution.py:152
  4.2 0.4 %collective-permute-start.3 = (f32[1280,128]{1,0:T(8,128)S(1)}, f32[1280,128]{1,0:T(8,128)S(1)}, u32[]{:S(2)}, u32[]{:S(2)}) collective-permute-start(f32[1280,128]{1,0:T(8,128)S(1)} %get-tuple-element.50), channel_id=1, source_target_pairs={{0,1},{1,0},{2,3},{3,2},{4,5},{5,4},{6,7},{7,6},{8,9},{9,8},{10,11... | collective-permute-start | bytes 1966088 | tf_op jit(solution)/shard_map/ppermute | solution.py:152
  4.6 0.0 copy-done.2
  4.6 1.0 %joint.1 = (f32[128,128]{1,0:T(8,128)S(1)}, f32[128,128]{1,0:T(8,128)S(1)}, f32[128,128]{1,0:T(8,128)S(1)}, f32[128,128]{1,0:T(8,128)S(1)}, f32[128,128]{1,0:T(8,128)S(1)}, /*index=5*/bf16[256,128]{1,0:T(8,128)(2,1)S(1)}) custom-call(f32[4,128,128]{2,1,0:T(8,128)S(1)} %copy-done.2, f32[4,128,128]{2,1,0:T(8,128)S(1)} %collective-permute-done.1.other_ref), custom_call_target="tpu_custom_call" | custom-call | flops 26843545600 | bytes 917504 | tf_op jit(solution)/shard_map/joint/pallas_call | solution.py:140
  5.6 0.0 copy-start.1
  5.6 0.0 collective-permute-done.received_ref
  5.6 0.3 sent_shares.1
  6.0 2.7 %collective-permute-start.4 = (f32[640,128]{1,0:T(8,128)S(1)}, f32[640,128]{1,0:T(8,128)S(1)}, u32[]{:S(2)}, u32[]{:S(2)}) collective-permute-start(f32[640,128]{1,0:T(8,128)S(1)} %get-tuple-element.52), channel_id=1, source_target_pairs={{0,2},{1,5},{2,0},{3,7},{4,6},{5,1},{6,4},{7,3},{8,10},{9,13},{10,... | collective-permute-start | bytes 983048 | tf_op jit(solution)/shard_map/ppermute | solution.py:274
  8.6 1.6 %collective-permute-start.2 = (f32[640,128]{1,0:T(8,128)S(1)}, f32[640,128]{1,0:T(8,128)S(1)}, u32[]{:S(2)}, u32[]{:S(2)}) collective-permute-start(f32[640,128]{1,0:T(8,128)S(1)} %get-tuple-element.39), channel_id=1, source_target_pairs={{0,8},{1,5},{2,10},{3,7},{4,12},{5,1},{6,14},{7,3},{8,0},{9,13},{1... | collective-permute-start | bytes 983048 | tf_op jit(solution)/shard_map/ppermute | solution.py:274
  10.2 0.0 copy-done.1
  10.2 1.6 %grads.1 = (bf16[1,128,128]{2,1,0:T(8,128)(2,1)}, f32[128,128]{1,0:T(8,128)S(1)}, f32[128,128]{1,0:T(8,128)S(1)}, f32[128,128]{1,0:T(8,128)S(1)}, f32[136,128]{1,0:T(8,128)S(1)}) custom-call(f32[4,128,128]{2,1,0:T(8,128)S(1)} %copy-done.2, f32[128,128]{1,0:T(8,128)S(1)} %get-tuple-element.40.cumul_ref, f32[128,128]{1,0:T(8,128)S(1)} %get-tuple-element.41.scores_ref, ...), custom_call_target="tpu_custom_call" | custom-call | flops 1342177280 | bytes 3510272 | tf_op jit(solution)/shard_map/grads/pallas_call | solution.py:140
  11.8 0.0 collective-permute-start.7
  11.8 0.0 collective-permute-done.3.received_ref
  11.8 0.3 kept_shares.1
  12.1 1.6 %collective-permute-done.4 = f32[640,128]{1,0:T(8,128)S(1)} collective-permute-done((f32[640,128]{1,0:T(8,128)S(1)}, f32[640,128]{1,0:T(8,128)S(1)}, u32[]{:S(2)}, u32[]{:S(2)}) %collective-permute-start.4) | collective-permute-done | bytes 327712 | tf_op jit(solution)/shard_map/ppermute | solution.py:274
  13.7 0.1 slice_add_fusion.1
  13.7 2.1 %collective-permute-start.5 = (f32[320,128]{1,0:T(8,128)S(1)}, f32[320,128]{1,0:T(8,128)S(1)}, u32[]{:S(2)}, u32[]{:S(2)}) collective-permute-start(f32[320,128]{1,0:T(8,128)S(1)} %get-tuple-element.66), channel_id=1, source_target_pairs={{0,4},{1,3},{2,6},{3,1},{4,0},{5,7},{6,2},{7,5},{8,12},{9,11},{10,... | collective-permute-start | bytes 491528 | tf_op jit(solution)/shard_map/ppermute | solution.py:274
  15.9 0.0 collective-permute-done.2
  15.9 0.1 slice_add_fusion.3
  15.9 1.6 %collective-permute-start.8 = (f32[320,128]{1,0:T(8,128)S(1)}, f32[320,128]{1,0:T(8,128)S(1)}, u32[]{:S(2)}, u32[]{:S(2)}) collective-permute-start(f32[320,128]{1,0:T(8,128)S(1)} %get-tuple-element.64), channel_id=1, source_target_pairs={{0,2},{1,9},{2,0},{3,11},{4,6},{5,13},{6,4},{7,15},{8,10},{9,1},{1... | collective-permute-start | bytes 491528 | tf_op jit(solution)/shard_map/ppermute | solution.py:274
  17.5 1.7 %collective-permute-done.5 = f32[320,128]{1,0:T(8,128)S(1)} collective-permute-done((f32[320,128]{1,0:T(8,128)S(1)}, f32[320,128]{1,0:T(8,128)S(1)}, u32[]{:S(2)}, u32[]{:S(2)}) %collective-permute-start.5) | collective-permute-done | bytes 163872 | tf_op jit(solution)/shard_map/ppermute | solution.py:274
  19.2 2.1 %collective-permute-start.6 = (f32[160,128]{1,0:T(8,128)S(1)}, f32[160,128]{1,0:T(8,128)S(1)}, u32[]{:S(2)}, u32[]{:S(2)}) collective-permute-start(f32[160,128]{1,0:T(8,128)S(1)} %get-tuple-element.68), channel_id=1, source_target_pairs={{0,8},{1,9},{2,10},{3,11},{4,12},{5,13},{6,14},{7,15},{8,0},{9,1},... | collective-permute-start | bytes 245768 | tf_op jit(solution)/shard_map/ppermute | solution.py:274
  21.3 0.0 collective-permute-done.8
  21.4 1.6 %collective-permute-start.9 = (f32[160,128]{1,0:T(8,128)S(1)}, f32[160,128]{1,0:T(8,128)S(1)}, u32[]{:S(2)}, u32[]{:S(2)}) collective-permute-start(f32[160,128]{1,0:T(8,128)S(1)} %get-tuple-element.70), channel_id=1, source_target_pairs={{0,4},{1,3},{2,6},{3,1},{4,0},{5,7},{6,2},{7,5},{8,12},{9,11},{10,... | collective-permute-start | bytes 245768 | tf_op jit(solution)/shard_map/ppermute | solution.py:274
  22.9 0.0 collective-permute-done.7.later_ref
  22.9 0.8 %collective-permute-done.6 = f32[160,128]{1,0:T(8,128)S(1)} collective-permute-done((f32[160,128]{1,0:T(8,128)S(1)}, f32[160,128]{1,0:T(8,128)S(1)}, u32[]{:S(2)}, u32[]{:S(2)}) %collective-permute-start.6) | collective-permute-done | bytes 81952 | tf_op jit(solution)/shard_map/ppermute | solution.py:274
  23.8 2.1 %collective-permute-done.9 = f32[160,128]{1,0:T(8,128)S(1)} collective-permute-done((f32[160,128]{1,0:T(8,128)S(1)}, f32[160,128]{1,0:T(8,128)S(1)}, u32[]{:S(2)}, u32[]{:S(2)}) %collective-permute-start.9) | collective-permute-done | bytes 81952 | tf_op jit(solution)/shard_map/ppermute | solution.py:274
  25.9 2.7 %collective-permute-start.10 = (f32[160,128]{1,0:T(8,128)S(1)}, f32[160,128]{1,0:T(8,128)S(1)}, u32[]{:S(2)}, u32[]{:S(2)}) collective-permute-start(f32[160,128]{1,0:T(8,128)S(1)} %pad_maximum_fusion.1), channel_id=1, source_target_pairs={{0,16},{1,17},{2,18},{3,19},{4,20},{5,21},{6,22},{7,23},{8,24},{9,... | collective-permute-start | bytes 245768 | tf_op jit(solution)/shard_map/ppermute | solution.py:274
  28.5 1.0 %finish.1 = (bf16[1,128,128]{2,1,0:T(8,128)(2,1)}, bf16[1,128,128]{2,1,0:T(8,128)(2,1)}, f32[1,128,128]{2,1,0:T(8,128)}) custom-call(f32[4,128,128]{2,1,0:T(8,128)S(1)} %copy-done.2, f32[128,128]{1,0:T(8,128)S(1)} %get-tuple-element.40.cumul_ref, f32[128,128]{1,0:T(8,128)S(1)} %get-tuple-element.47.grad_key_ref, ...), custom_call_target="tpu_custom_call" | custom-call | flops 671088640 | bytes 724992 | tf_op jit(solution)/shard_map/finish/pallas_call | solution.py:140
  29.6 1.9 %collective-permute-done.10 = f32[160,128]{1,0:T(8,128)S(1)} collective-permute-done((f32[160,128]{1,0:T(8,128)S(1)}, f32[160,128]{1,0:T(8,128)S(1)}, u32[]{:S(2)}, u32[]{:S(2)}) %collective-permute-start.10) | collective-permute-done | bytes 81952 | tf_op jit(solution)/shard_map/ppermute | solution.py:274
  31.5 0.1 collective-permute-start.11
  31.6 1.3 %collective-permute-done.11 = f32[160,128]{1,0:T(8,128)S(1)} collective-permute-done((f32[160,128]{1,0:T(8,128)S(1)}, f32[160,128]{1,0:T(8,128)S(1)}, u32[]{:S(2)}, u32[]{:S(2)}) %collective-permute-start.11) | collective-permute-done | bytes 81952 | tf_op jit(solution)/shard_map/ppermute | solution.py:152
  32.8 0.7 %pad_maximum_fusion = f32[320,128]{1,0:T(8,128)} fusion(f32[160,128]{1,0:T(8,128)S(1)} %get-tuple-element.72, f32[160,128]{1,0:T(8,128)S(1)} %get-tuple-element.71), kind=kLoop, calls=%fused_computation.2 | loop fusion | flops 40960 | bytes 327680 | tf_op jit(solution)/shard_map/concatenate | solution.py:428
  (8 shorter events, 0.1 us)
Async XLA Ops:
  0.6 2.2 %copy-start = (bf16[1,128,5120]{2,1,0:T(8,128)(2,1)S(1)}, bf16[1,128,5120]{2,1,0:T(8,128)(2,1)}, u32[]{:S(2)}) copy-start(bf16[1,128,5120]{2,1,0:T(8,128)(2,1)} %upstream_ref.3) | copy-start | bytes 3932164
  2.3 2.3 %copy-start.2 = (f32[4,128,128]{2,1,0:T(8,128)S(1)}, f32[4,128,128]{2,1,0:T(8,128)}, u32[]{:S(2)}) copy-start(f32[4,128,128]{2,1,0:T(8,128)} %pack.1.own_ref.packed_ref) | copy-start | bytes 786436
  2.4 1.9 %collective-permute-start.1 = (f32[4,128,128]{2,1,0:T(8,128)}, f32[4,128,128]{2,1,0:T(8,128)S(1)}, u32[]{:S(2)}, u32[]{:S(2)}) collective-permute-start(f32[4,128,128]{2,1,0:T(8,128)} %pack.1.own_ref.packed_ref), channel_id=1, source_target_pairs={{0,1},{1,0},{2,3},{3,2},{4,5},{5,4},{6,7},{7,6},{8,9},{9,8},{10,11... | collective-permute-start | bytes 786440 | tf_op jit(solution)/shard_map/ppermute | solution.py:152
  3.4 2.2 %collective-permute-start = (f32[1280,128]{1,0:T(8,128)S(1)}, f32[1280,128]{1,0:T(8,128)S(1)}, u32[]{:S(2)}, u32[]{:S(2)}) collective-permute-start(f32[1280,128]{1,0:T(8,128)S(1)} %get-tuple-element.35), channel_id=1, source_target_pairs={{0,1},{1,0},{2,3},{3,2},{4,5},{5,4},{6,7},{7,6},{8,9},{9,8},{10,11... | collective-permute-start | bytes 1966088 | tf_op jit(solution)/shard_map/ppermute | solution.py:152
  4.2 7.6 %collective-permute-start.3 = (f32[1280,128]{1,0:T(8,128)S(1)}, f32[1280,128]{1,0:T(8,128)S(1)}, u32[]{:S(2)}, u32[]{:S(2)}) collective-permute-start(f32[1280,128]{1,0:T(8,128)S(1)} %get-tuple-element.50), channel_id=1, source_target_pairs={{0,1},{1,0},{2,3},{3,2},{4,5},{5,4},{6,7},{7,6},{8,9},{9,8},{10,11... | collective-permute-start | bytes 1966088 | tf_op jit(solution)/shard_map/ppermute | solution.py:152
  5.6 4.6 %copy-start.1 = (bf16[5120,128]{1,0:T(8,128)(2,1)S(1)}, bf16[5120,128]{1,0:T(8,128)(2,1)}, u32[]{:S(2)}) copy-start(bf16[5120,128]{1,0:T(8,128)(2,1)} %weight_ref.1) | copy-start | bytes 3932164
  6.0 7.7 %collective-permute-start.4 = (f32[640,128]{1,0:T(8,128)S(1)}, f32[640,128]{1,0:T(8,128)S(1)}, u32[]{:S(2)}, u32[]{:S(2)}) collective-permute-start(f32[640,128]{1,0:T(8,128)S(1)} %get-tuple-element.52), channel_id=1, source_target_pairs={{0,2},{1,5},{2,0},{3,7},{4,6},{5,1},{6,4},{7,3},{8,10},{9,13},{10,... | collective-permute-start | bytes 983048 | tf_op jit(solution)/shard_map/ppermute | solution.py:274
  8.6 7.2 %collective-permute-start.2 = (f32[640,128]{1,0:T(8,128)S(1)}, f32[640,128]{1,0:T(8,128)S(1)}, u32[]{:S(2)}, u32[]{:S(2)}) collective-permute-start(f32[640,128]{1,0:T(8,128)S(1)} %get-tuple-element.39), channel_id=1, source_target_pairs={{0,8},{1,5},{2,10},{3,7},{4,12},{5,1},{6,14},{7,3},{8,0},{9,13},{1... | collective-permute-start | bytes 983048 | tf_op jit(solution)/shard_map/ppermute | solution.py:274
  11.8 11.1 %collective-permute-start.7 = (f32[136,128]{1,0:T(8,128)S(1)}, f32[136,128]{1,0:T(8,128)S(1)}, u32[]{:S(2)}, u32[]{:S(2)}) collective-permute-start(f32[136,128]{1,0:T(8,128)S(1)} %get-tuple-element.53), channel_id=1, source_target_pairs={{0,1},{1,0},{2,3},{3,2},{4,5},{5,4},{6,7},{7,6},{8,9},{9,8},{10,11... | collective-permute-start | bytes 208904 | tf_op jit(solution)/shard_map/ppermute | solution.py:152
  13.7 5.4 %collective-permute-start.5 = (f32[320,128]{1,0:T(8,128)S(1)}, f32[320,128]{1,0:T(8,128)S(1)}, u32[]{:S(2)}, u32[]{:S(2)}) collective-permute-start(f32[320,128]{1,0:T(8,128)S(1)} %get-tuple-element.66), channel_id=1, source_target_pairs={{0,4},{1,3},{2,6},{3,1},{4,0},{5,7},{6,2},{7,5},{8,12},{9,11},{10,... | collective-permute-start | bytes 491528 | tf_op jit(solution)/shard_map/ppermute | solution.py:274
  15.9 5.4 %collective-permute-start.8 = (f32[320,128]{1,0:T(8,128)S(1)}, f32[320,128]{1,0:T(8,128)S(1)}, u32[]{:S(2)}, u32[]{:S(2)}) collective-permute-start(f32[320,128]{1,0:T(8,128)S(1)} %get-tuple-element.64), channel_id=1, source_target_pairs={{0,2},{1,9},{2,0},{3,11},{4,6},{5,13},{6,4},{7,15},{8,10},{9,1},{1... | collective-permute-start | bytes 491528 | tf_op jit(solution)/shard_map/ppermute | solution.py:274
  19.2 4.6 %collective-permute-start.6 = (f32[160,128]{1,0:T(8,128)S(1)}, f32[160,128]{1,0:T(8,128)S(1)}, u32[]{:S(2)}, u32[]{:S(2)}) collective-permute-start(f32[160,128]{1,0:T(8,128)S(1)} %get-tuple-element.68), channel_id=1, source_target_pairs={{0,8},{1,9},{2,10},{3,11},{4,12},{5,13},{6,14},{7,15},{8,0},{9,1},... | collective-permute-start | bytes 245768 | tf_op jit(solution)/shard_map/ppermute | solution.py:274
  21.4 4.5 %collective-permute-start.9 = (f32[160,128]{1,0:T(8,128)S(1)}, f32[160,128]{1,0:T(8,128)S(1)}, u32[]{:S(2)}, u32[]{:S(2)}) collective-permute-start(f32[160,128]{1,0:T(8,128)S(1)} %get-tuple-element.70), channel_id=1, source_target_pairs={{0,4},{1,3},{2,6},{3,1},{4,0},{5,7},{6,2},{7,5},{8,12},{9,11},{10,... | collective-permute-start | bytes 245768 | tf_op jit(solution)/shard_map/ppermute | solution.py:274
  25.9 5.6 %collective-permute-start.10 = (f32[160,128]{1,0:T(8,128)S(1)}, f32[160,128]{1,0:T(8,128)S(1)}, u32[]{:S(2)}, u32[]{:S(2)}) collective-permute-start(f32[160,128]{1,0:T(8,128)S(1)} %pad_maximum_fusion.1), channel_id=1, source_target_pairs={{0,16},{1,17},{2,18},{3,19},{4,20},{5,21},{6,22},{7,23},{8,24},{9,... | collective-permute-start | bytes 245768 | tf_op jit(solution)/shard_map/ppermute | solution.py:274
  31.5 1.3 %collective-permute-start.11 = (f32[160,128]{1,0:T(8,128)S(1)}, f32[160,128]{1,0:T(8,128)S(1)}, u32[]{:S(2)}, u32[]{:S(2)}) collective-permute-start(f32[160,128]{1,0:T(8,128)S(1)} %pad_maximum_fusion.2), channel_id=1, source_target_pairs={{0,1},{1,0},{2,3},{3,2},{4,5},{5,4},{6,7},{7,6},{8,9},{9,8},{10,11... | collective-permute-start | bytes 245768 | tf_op jit(solution)/shard_map/ppermute | solution.py:152

commit v5 on v4

--- a/solution.py
+++ b/solution.py
@@ -9,7 +9,6 @@
 
 EPSILON = 1e-05
 VMEM_BYTES = 24 * 1024 * 1024
-PACK_BYTES = 58 * 1024 * 1024
 F32 = jnp.float32
 BF16 = jnp.bfloat16
 BOTH = ("dp", "ctx")
@@ -44,8 +43,9 @@
     return rows >= columns
 
 
-def cumulate(decay):
-    lower = lower_mask(decay.shape[0]).astype(F32).astype(BF16)
+def cumulate(decay, lower=None):
+    if lower is None:
+        lower = lower_mask(decay.shape[0]).astype(F32).astype(BF16)
     return product([lower], split(decay, 3), 1, 0)
 
 
@@ -167,22 +167,8 @@
     return sum(((place >> (top - step)) & 1) << bit for step, bit in enumerate(order))
 
 
-def pack_kernel(query_ref, key_ref, value_ref, decay_ref, packed_ref, query, key, value, semaphores):
-    pairs = [
-        (decay_ref.at[0], packed_ref.at[3]), (query_ref.at[0], query),
-        (key_ref.at[0], key), (value_ref.at[0], value),
-    ]
-    copies = [
-        pltpu.make_async_copy(source, target, semaphores.at[index])
-        for index, (source, target) in enumerate(pairs)
-    ]
-    for copy in copies:
-        copy.start()
-    for copy in copies:
-        copy.wait()
-    packed_ref[0] = query[...].astype(F32)
-    packed_ref[1] = key[...].astype(F32)
-    packed_ref[2] = value[...].astype(F32)
+def lower_kernel(lower_ref):
+    lower_ref[...] = lower_mask(lower_ref.shape[0]).astype(F32).astype(BF16)
 
 
 def turn_kernel(count, plan, upstream_ref, own_ref, first_ref, second_ref, turned):
@@ -211,7 +197,7 @@
 
 
 def joint_kernel(
-    own_ref, other_ref,
+    own_ref, other_ref, lower_ref,
     cumul_ref, scores_ref, state_ref, normed_ref, scale_ref, rounded_ref,
 ):
     first = lax.axis_index("ctx") == 0
@@ -220,7 +206,7 @@
 
     def scaled(block):
         query, key, value, decay = block
-        cumul = cumulate(decay)
+        cumul = cumulate(decay, lower_ref[...])
         query_scaled = split(query * jnp.exp(cumul), 2)
         key_scaled = split(key * jnp.exp(-cumul), 2)
         return cumul, query_scaled, key_scaled, value.astype(BF16)
@@ -318,13 +304,10 @@
     flops = 8 * length * width * model
     paired = shards == 2 and count >= 16 and count & (count - 1) == 0 and rows % 16 == 0
 
-    (packed,) = local_call(
-        pack_kernel,
-        [((4, length, width), F32)],
-        queries, key_vectors, value_vectors, log_decay,
-        name="pack", flops=20 * flops, space=pltpu.HBM, limit=PACK_BYTES,
-        scratch=[pltpu.VMEM(square, BF16)] * 3 + [pltpu.SemaphoreType.DMA((4,))],
-    )
+    (lower,) = local_call(lower_kernel, [((length, length), BF16)], name="lower", flops=20 * flops)
+    inputs = (queries, key_vectors, value_vectors, log_decay)
+    *inputs, lower = lax.optimization_barrier((*inputs, lower))
+    packed = jnp.concatenate([jnp.concatenate(inputs[:3]).astype(F32), inputs[3]])
     if paired:
         plan = halving_plan(count, rows)
         part_rows = rows * count // 2
@@ -345,7 +328,7 @@
                 (square, F32), ((length, length), F32), ((width, width), F32), (square, F32),
                 (square, F32), ((2 * length, width), BF16),
             ],
-            packed, others,
+            packed, others, lower,
             name="joint", flops=40 * flops,
         )
         sent = local_call(

time: 33.7 us -> 32.9 us (0.976)
  Pallas kernels: 6.46 us -> 4.79 us
  local copies, waits for them, and re-layouts: 0.01 us -> 0.83 us
  starting transfers between devices: 15.4 us -> 16 us
  waiting for transfers between devices: 10 us -> 9.51 us
    pallas_call x7, Pallas kernels: 6.46 us -> 4.79 us  [local_call(): pl.pallas_call(kernel, out_shape=outs, in_specs=[pl.BlockSpec(memory_spac...]
    unnamed x6 -> x12, local copies, waits for them, and re-layouts: 0.01 us -> 0.83 us
    ppermute x5, starting transfers between devices: 1.09 us -> 1.45 us  [swap(): return lax.ppermute(value, 'ctx', [(0, 1), (1, 0)])]
  transfers between devices with their start and end apart: 12 -> 12, of which waited for: 7 -> 8; matrix products, arithmetic and copies ran while one was open for 0% -> 0% of each run, Pallas kernels for 14% -> 15%
where the time goes in v5:
time: 32.9 us; the launch traced here: 32.8 us
  starting transfers between devices  16 us (49%)
  waiting for transfers between devices  9.51 us (29%)
  Pallas kernels  4.79 us (15%)
  other arithmetic  0.89 us (3%)
  local copies, waits for them, and re-layouts  0.83 us (3%)
  between operations  0.78 us (2%)
    ppermute x7, starting transfers between devices, exchanged(): return lax.ppermute(value, BOTH, pairs)  14.5 us
    ppermute x7, waiting for transfers between devices, exchanged(): return lax.ppermute(value, BOTH, pairs)  7.89 us
    pallas_call x7, Pallas kernels, local_call(): pl.pallas_call(kernel, out_shape=outs, in_specs=[pl.BlockSpec(memory_spac...  4.79 us
    ppermute x5, waiting for transfers between devices, swap(): return lax.ppermute(value, 'ctx', [(0, 1), (1, 0)])  1.62 us
    ppermute x5, starting transfers between devices, swap(): return lax.ppermute(value, 'ctx', [(0, 1), (1, 0)])  1.45 us
    unnamed x12, local copies, waits for them, and re-layouts  0.83 us
    concatenate x1, other arithmetic, body(): jnp.concatenate([jnp.where(first, mine, theirs), jnp.where(first, theirs,...  0.68 us
  transfers between devices with their start and end apart: 12, of which 8 were waited for; matrix products, arithmetic and copies ran while one was open for 0% of the time, Pallas kernels for 15%

profile of v5, /device:TPU:0, one launch (start us, length us, event | category | flops | bytes accessed | tf_op | source)
XLA Modules:
  0.0 32.8 jit_solution(10360386079069126159)
XLA Ops:
  0.6 0.0 copy-start.5
  0.6 0.0 copy-start.4
  0.7 0.0 copy-start.3
  0.7 0.0 copy-start.2
  0.7 0.0 copy-start
  0.7 0.7 %copy-done.5 = bf16[1,128,128]{2,1,0:T(8,128)(2,1)S(1)} copy-done((bf16[1,128,128]{2,1,0:T(8,128)(2,1)S(1)}, bf16[1,128,128]{2,1,0:T(8,128)(2,1)}, u32[]{:S(2)}) %copy-start.5) | copy-done | bytes 32792
  1.4 0.0 copy-done.4
  1.4 0.0 copy-done.3
  1.4 0.1 copy-done.2
  1.6 0.5 %collective-permute-start.1 = (f32[4,128,128]{2,1,0:T(8,128)S(1)}, f32[4,128,128]{2,1,0:T(8,128)S(1)}, u32[]{:S(2)}, u32[]{:S(2)}) collective-permute-start(f32[4,128,128]{2,1,0:T(8,128)S(1)} %pad_maximum_fusion.own_ref.packed_ref), channel_id=1, source_target_pairs={{0,1},{1,0},{2,3},{3,2},{4,5},{5,4},{6,7},{7,6},{8,9},{9,8},{10,11... | collective-permute-start | bytes 786440 | tf_op jit(solution)/shard_map/ppermute | solution.py:152
  2.1 0.0 copy-done
  2.1 0.6 %turn.1 = (bf16[2560,128]{1,0:T(8,128)(2,1)S(1)}, f32[1280,128]{1,0:T(8,128)S(1)}, f32[1280,128]{1,0:T(8,128)S(1)}) custom-call(bf16[1,128,5120]{2,1,0:T(8,128)(2,1)S(1)} %copy-done), custom_call_target="tpu_custom_call" | custom-call | flops 13421772800 | bytes 3276800 | tf_op jit(solution)/shard_map/turn/pallas_call | solution.py:140
  2.6 0.5 %collective-permute-start = (f32[1280,128]{1,0:T(8,128)S(1)}, f32[1280,128]{1,0:T(8,128)S(1)}, u32[]{:S(2)}, u32[]{:S(2)}) collective-permute-start(f32[1280,128]{1,0:T(8,128)S(1)} %get-tuple-element.40), channel_id=1, source_target_pairs={{0,1},{1,0},{2,3},{3,2},{4,5},{5,4},{6,7},{7,6},{8,9},{9,8},{10,11... | collective-permute-start | bytes 1966088 | tf_op jit(solution)/shard_map/ppermute | solution.py:152
  3.1 0.1 collective-permute-done.1.other_ref
  3.2 0.4 %collective-permute-start.3 = (f32[1280,128]{1,0:T(8,128)S(1)}, f32[1280,128]{1,0:T(8,128)S(1)}, u32[]{:S(2)}, u32[]{:S(2)}) collective-permute-start(f32[1280,128]{1,0:T(8,128)S(1)} %get-tuple-element.60), channel_id=1, source_target_pairs={{0,1},{1,0},{2,3},{3,2},{4,5},{5,4},{6,7},{7,6},{8,9},{9,8},{10,11... | collective-permute-start | bytes 1966088 | tf_op jit(solution)/shard_map/ppermute | solution.py:152
  3.6 1.0 %joint.1 = (f32[128,128]{1,0:T(8,128)S(1)}, f32[128,128]{1,0:T(8,128)S(1)}, f32[128,128]{1,0:T(8,128)S(1)}, f32[128,128]{1,0:T(8,128)S(1)}, f32[128,128]{1,0:T(8,128)S(1)}, /*index=5*/bf16[256,128]{1,0:T(8,128)(2,1)S(1)}) custom-call(f32[4,128,128]{2,1,0:T(8,128)S(1)} %pad_maximum_fusion.own_ref.packed_ref, ...), custom_call_target="tpu_custom_call" | custom-call | flops 26843545600 | bytes 950272 | tf_op jit(solution)/shard_map/joint/pallas_call | solution.py:140
  4.6 0.0 copy-start.1
  4.6 0.3 collective-permute-done.received_ref
  4.9 0.3 sent_shares.1
  5.2 2.9 %collective-permute-start.4 = (f32[640,128]{1,0:T(8,128)S(1)}, f32[640,128]{1,0:T(8,128)S(1)}, u32[]{:S(2)}, u32[]{:S(2)}) collective-permute-start(f32[640,128]{1,0:T(8,128)S(1)} %get-tuple-element.62), channel_id=1, source_target_pairs={{0,2},{1,5},{2,0},{3,7},{4,6},{5,1},{6,4},{7,3},{8,10},{9,13},{10,... | collective-permute-start | bytes 983048 | tf_op jit(solution)/shard_map/ppermute | solution.py:260
  8.1 1.6 %collective-permute-start.2 = (f32[640,128]{1,0:T(8,128)S(1)}, f32[640,128]{1,0:T(8,128)S(1)}, u32[]{:S(2)}, u32[]{:S(2)}) collective-permute-start(f32[640,128]{1,0:T(8,128)S(1)} %get-tuple-element.49), channel_id=1, source_target_pairs={{0,8},{1,5},{2,10},{3,7},{4,12},{5,1},{6,14},{7,3},{8,0},{9,13},{1... | collective-permute-start | bytes 983048 | tf_op jit(solution)/shard_map/ppermute | solution.py:260
  9.7 0.0 copy-done.1
  9.7 1.6 %grads.1 = (bf16[1,128,128]{2,1,0:T(8,128)(2,1)}, f32[128,128]{1,0:T(8,128)S(1)}, f32[128,128]{1,0:T(8,128)S(1)}, f32[128,128]{1,0:T(8,128)S(1)}, f32[136,128]{1,0:T(8,128)S(1)}) custom-call(f32[4,128,128]{2,1,0:T(8,128)S(1)} %pad_maximum_fusion.own_ref.packed_ref, f32[128,128]{1,0:T(8,128)S(1)} %get-tuple-element.50.cumul_ref, ...), custom_call_target="tpu_custom_call" | custom-call | flops 1342177280 | bytes 3510272 | tf_op jit(solution)/shard_map/grads/pallas_call | solution.py:140
  11.3 0.0 collective-permute-start.7
  11.3 0.0 collective-permute-done.3.received_ref
  11.3 0.3 kept_shares.1
  11.6 1.6 %collective-permute-done.4 = f32[640,128]{1,0:T(8,128)S(1)} collective-permute-done((f32[640,128]{1,0:T(8,128)S(1)}, f32[640,128]{1,0:T(8,128)S(1)}, u32[]{:S(2)}, u32[]{:S(2)}) %collective-permute-start.4) | collective-permute-done | bytes 327712 | tf_op jit(solution)/shard_map/ppermute | solution.py:260
  13.2 2.1 %collective-permute-start.5 = (f32[320,128]{1,0:T(8,128)S(1)}, f32[320,128]{1,0:T(8,128)S(1)}, u32[]{:S(2)}, u32[]{:S(2)}) collective-permute-start(f32[320,128]{1,0:T(8,128)S(1)} %get-tuple-element.76), channel_id=1, source_target_pairs={{0,4},{1,3},{2,6},{3,1},{4,0},{5,7},{6,2},{7,5},{8,12},{9,11},{10,... | collective-permute-start | bytes 491528 | tf_op jit(solution)/shard_map/ppermute | solution.py:260
  15.3 0.0 collective-permute-done.2
  15.4 1.6 %collective-permute-start.8 = (f32[320,128]{1,0:T(8,128)S(1)}, f32[320,128]{1,0:T(8,128)S(1)}, u32[]{:S(2)}, u32[]{:S(2)}) collective-permute-start(f32[320,128]{1,0:T(8,128)S(1)} %get-tuple-element.74), channel_id=1, source_target_pairs={{0,2},{1,9},{2,0},{3,11},{4,6},{5,13},{6,4},{7,15},{8,10},{9,1},{1... | collective-permute-start | bytes 491528 | tf_op jit(solution)/shard_map/ppermute | solution.py:260
  16.9 1.7 %collective-permute-done.5 = f32[320,128]{1,0:T(8,128)S(1)} collective-permute-done((f32[320,128]{1,0:T(8,128)S(1)}, f32[320,128]{1,0:T(8,128)S(1)}, u32[]{:S(2)}, u32[]{:S(2)}) %collective-permute-start.5) | collective-permute-done | bytes 163872 | tf_op jit(solution)/shard_map/ppermute | solution.py:260
  18.6 2.1 %collective-permute-start.6 = (f32[160,128]{1,0:T(8,128)S(1)}, f32[160,128]{1,0:T(8,128)S(1)}, u32[]{:S(2)}, u32[]{:S(2)}) collective-permute-start(f32[160,128]{1,0:T(8,128)S(1)} %get-tuple-element.78), channel_id=1, source_target_pairs={{0,8},{1,9},{2,10},{3,11},{4,12},{5,13},{6,14},{7,15},{8,0},{9,1},... | collective-permute-start | bytes 245768 | tf_op jit(solution)/shard_map/ppermute | solution.py:260
  20.8 0.0 collective-permute-done.8
  20.8 1.6 %collective-permute-start.9 = (f32[160,128]{1,0:T(8,128)S(1)}, f32[160,128]{1,0:T(8,128)S(1)}, u32[]{:S(2)}, u32[]{:S(2)}) collective-permute-start(f32[160,128]{1,0:T(8,128)S(1)} %get-tuple-element.80), channel_id=1, source_target_pairs={{0,4},{1,3},{2,6},{3,1},{4,0},{5,7},{6,2},{7,5},{8,12},{9,11},{10,... | collective-permute-start | bytes 245768 | tf_op jit(solution)/shard_map/ppermute | solution.py:260
  22.4 0.0 collective-permute-done.7.later_ref
  22.4 0.8 %collective-permute-done.6 = f32[160,128]{1,0:T(8,128)S(1)} collective-permute-done((f32[160,128]{1,0:T(8,128)S(1)}, f32[160,128]{1,0:T(8,128)S(1)}, u32[]{:S(2)}, u32[]{:S(2)}) %collective-permute-start.6) | collective-permute-done | bytes 81952 | tf_op jit(solution)/shard_map/ppermute | solution.py:260
  23.2 2.1 %collective-permute-done.9 = f32[160,128]{1,0:T(8,128)S(1)} collective-permute-done((f32[160,128]{1,0:T(8,128)S(1)}, f32[160,128]{1,0:T(8,128)S(1)}, u32[]{:S(2)}, u32[]{:S(2)}) %collective-permute-start.9) | collective-permute-done | bytes 81952 | tf_op jit(solution)/shard_map/ppermute | solution.py:260
  25.3 2.7 %collective-permute-start.10 = (f32[160,128]{1,0:T(8,128)S(1)}, f32[160,128]{1,0:T(8,128)S(1)}, u32[]{:S(2)}, u32[]{:S(2)}) collective-permute-start(f32[160,128]{1,0:T(8,128)S(1)} %pad_maximum_fusion.2), channel_id=1, source_target_pairs={{0,16},{1,17},{2,18},{3,19},{4,20},{5,21},{6,22},{7,23},{8,24},{9,... | collective-permute-start | bytes 245768 | tf_op jit(solution)/shard_map/ppermute | solution.py:260
  28.0 1.0 %finish.1 = (bf16[1,128,128]{2,1,0:T(8,128)(2,1)}, bf16[1,128,128]{2,1,0:T(8,128)(2,1)}, f32[1,128,128]{2,1,0:T(8,128)}) custom-call(f32[4,128,128]{2,1,0:T(8,128)S(1)} %pad_maximum_fusion.own_ref.packed_ref, f32[128,128]{1,0:T(8,128)S(1)} %get-tuple-element.50.cumul_ref, f32[128,128]{1,0:T(8,128)S(1)} %get-tuple-element.57.grad_key_ref, ...), custom_call_target="tpu_custom_call" | custom-call | flops 671088640 | bytes 724992 | tf_op jit(solution)/shard_map/finish/pallas_call | solution.py:140
  29.0 1.7 %collective-permute-done.10 = f32[160,128]{1,0:T(8,128)S(1)} collective-permute-done((f32[160,128]{1,0:T(8,128)S(1)}, f32[160,128]{1,0:T(8,128)S(1)}, u32[]{:S(2)}, u32[]{:S(2)}) %collective-permute-start.10) | collective-permute-done | bytes 81952 | tf_op jit(solution)/shard_map/ppermute | solution.py:260
  30.8 0.1 collective-permute-start.11
  30.8 1.3 %collective-permute-done.11 = f32[160,128]{1,0:T(8,128)S(1)} collective-permute-done((f32[160,128]{1,0:T(8,128)S(1)}, f32[160,128]{1,0:T(8,128)S(1)}, u32[]{:S(2)}, u32[]{:S(2)}) %collective-permute-start.11) | collective-permute-done | bytes 81952 | tf_op jit(solution)/shard_map/ppermute | solution.py:152
  32.1 0.7 %pad_maximum_fusion.1 = f32[320,128]{1,0:T(8,128)} fusion(f32[160,128]{1,0:T(8,128)S(1)} %get-tuple-element.82, f32[160,128]{1,0:T(8,128)S(1)} %get-tuple-element.81), kind=kLoop, calls=%fused_computation.3 | loop fusion | flops 40960 | bytes 327680 | tf_op jit(solution)/shard_map/concatenate | solution.py:411
  (13 shorter events, 0.2 us)
Async XLA Ops:
  0.6 0.8 %copy-start.5 = (bf16[1,128,128]{2,1,0:T(8,128)(2,1)S(1)}, bf16[1,128,128]{2,1,0:T(8,128)(2,1)}, u32[]{:S(2)}) copy-start(bf16[1,128,128]{2,1,0:T(8,128)(2,1)} %param.6) | copy-start | bytes 98308
  0.6 0.8 %copy-start.4 = (bf16[1,128,128]{2,1,0:T(8,128)(2,1)S(1)}, bf16[1,128,128]{2,1,0:T(8,128)(2,1)}, u32[]{:S(2)}) copy-start(bf16[1,128,128]{2,1,0:T(8,128)(2,1)} %param.7) | copy-start | bytes 98308
  0.7 0.8 %copy-start.3 = (bf16[1,128,128]{2,1,0:T(8,128)(2,1)S(1)}, bf16[1,128,128]{2,1,0:T(8,128)(2,1)}, u32[]{:S(2)}) copy-start(bf16[1,128,128]{2,1,0:T(8,128)(2,1)} %param.8) | copy-start | bytes 98308
  0.7 0.9 %copy-start.2 = (f32[1,128,128]{2,1,0:T(8,128)S(1)}, f32[1,128,128]{2,1,0:T(8,128)}, u32[]{:S(2)}) copy-start(f32[1,128,128]{2,1,0:T(8,128)} %param.9) | copy-start | bytes 196612
  0.7 1.4 %copy-start = (bf16[1,128,5120]{2,1,0:T(8,128)(2,1)S(1)}, bf16[1,128,5120]{2,1,0:T(8,128)(2,1)}, u32[]{:S(2)}) copy-start(bf16[1,128,5120]{2,1,0:T(8,128)(2,1)} %upstream_ref.3) | copy-start | bytes 3932164
  1.6 1.7 %collective-permute-start.1 = (f32[4,128,128]{2,1,0:T(8,128)S(1)}, f32[4,128,128]{2,1,0:T(8,128)S(1)}, u32[]{:S(2)}, u32[]{:S(2)}) collective-permute-start(f32[4,128,128]{2,1,0:T(8,128)S(1)} %pad_maximum_fusion.own_ref.packed_ref), channel_id=1, source_target_pairs={{0,1},{1,0},{2,3},{3,2},{4,5},{5,4},{6,7},{7,6},{8,9},{9,8},{10,11... | collective-permute-start | bytes 786440 | tf_op jit(solution)/shard_map/ppermute | solution.py:152
  2.6 2.2 %collective-permute-start = (f32[1280,128]{1,0:T(8,128)S(1)}, f32[1280,128]{1,0:T(8,128)S(1)}, u32[]{:S(2)}, u32[]{:S(2)}) collective-permute-start(f32[1280,128]{1,0:T(8,128)S(1)} %get-tuple-element.40), channel_id=1, source_target_pairs={{0,1},{1,0},{2,3},{3,2},{4,5},{5,4},{6,7},{7,6},{8,9},{9,8},{10,11... | collective-permute-start | bytes 1966088 | tf_op jit(solution)/shard_map/ppermute | solution.py:152
  3.2 8.0 %collective-permute-start.3 = (f32[1280,128]{1,0:T(8,128)S(1)}, f32[1280,128]{1,0:T(8,128)S(1)}, u32[]{:S(2)}, u32[]{:S(2)}) collective-permute-start(f32[1280,128]{1,0:T(8,128)S(1)} %get-tuple-element.60), channel_id=1, source_target_pairs={{0,1},{1,0},{2,3},{3,2},{4,5},{5,4},{6,7},{7,6},{8,9},{9,8},{10,11... | collective-permute-start | bytes 1966088 | tf_op jit(solution)/shard_map/ppermute | solution.py:152
  4.6 5.1 %copy-start.1 = (bf16[5120,128]{1,0:T(8,128)(2,1)S(1)}, bf16[5120,128]{1,0:T(8,128)(2,1)}, u32[]{:S(2)}) copy-start(bf16[5120,128]{1,0:T(8,128)(2,1)} %weight_ref.1) | copy-start | bytes 3932164
  5.2 8.0 %collective-permute-start.4 = (f32[640,128]{1,0:T(8,128)S(1)}, f32[640,128]{1,0:T(8,128)S(1)}, u32[]{:S(2)}, u32[]{:S(2)}) collective-permute-start(f32[640,128]{1,0:T(8,128)S(1)} %get-tuple-element.62), channel_id=1, source_target_pairs={{0,2},{1,5},{2,0},{3,7},{4,6},{5,1},{6,4},{7,3},{8,10},{9,13},{10,... | collective-permute-start | bytes 983048 | tf_op jit(solution)/shard_map/ppermute | solution.py:260
  8.1 7.2 %collective-permute-start.2 = (f32[640,128]{1,0:T(8,128)S(1)}, f32[640,128]{1,0:T(8,128)S(1)}, u32[]{:S(2)}, u32[]{:S(2)}) collective-permute-start(f32[640,128]{1,0:T(8,128)S(1)} %get-tuple-element.49), channel_id=1, source_target_pairs={{0,8},{1,5},{2,10},{3,7},{4,12},{5,1},{6,14},{7,3},{8,0},{9,13},{1... | collective-permute-start | bytes 983048 | tf_op jit(solution)/shard_map/ppermute | solution.py:260
  11.3 11.1 %collective-permute-start.7 = (f32[136,128]{1,0:T(8,128)S(1)}, f32[136,128]{1,0:T(8,128)S(1)}, u32[]{:S(2)}, u32[]{:S(2)}) collective-permute-start(f32[136,128]{1,0:T(8,128)S(1)} %get-tuple-element.63), channel_id=1, source_target_pairs={{0,1},{1,0},{2,3},{3,2},{4,5},{5,4},{6,7},{7,6},{8,9},{9,8},{10,11... | collective-permute-start | bytes 208904 | tf_op jit(solution)/shard_map/ppermute | solution.py:152
  13.2 5.4 %collective-permute-start.5 = (f32[320,128]{1,0:T(8,128)S(1)}, f32[320,128]{1,0:T(8,128)S(1)}, u32[]{:S(2)}, u32[]{:S(2)}) collective-permute-start(f32[320,128]{1,0:T(8,128)S(1)} %get-tuple-element.76), channel_id=1, source_target_pairs={{0,4},{1,3},{2,6},{3,1},{4,0},{5,7},{6,2},{7,5},{8,12},{9,11},{10,... | collective-permute-start | bytes 491528 | tf_op jit(solution)/shard_map/ppermute | solution.py:260
  15.4 5.4 %collective-permute-start.8 = (f32[320,128]{1,0:T(8,128)S(1)}, f32[320,128]{1,0:T(8,128)S(1)}, u32[]{:S(2)}, u32[]{:S(2)}) collective-permute-start(f32[320,128]{1,0:T(8,128)S(1)} %get-tuple-element.74), channel_id=1, source_target_pairs={{0,2},{1,9},{2,0},{3,11},{4,6},{5,13},{6,4},{7,15},{8,10},{9,1},{1... | collective-permute-start | bytes 491528 | tf_op jit(solution)/shard_map/ppermute | solution.py:260
  18.6 4.6 %collective-permute-start.6 = (f32[160,128]{1,0:T(8,128)S(1)}, f32[160,128]{1,0:T(8,128)S(1)}, u32[]{:S(2)}, u32[]{:S(2)}) collective-permute-start(f32[160,128]{1,0:T(8,128)S(1)} %get-tuple-element.78), channel_id=1, source_target_pairs={{0,8},{1,9},{2,10},{3,11},{4,12},{5,13},{6,14},{7,15},{8,0},{9,1},... | collective-permute-start | bytes 245768 | tf_op jit(solution)/shard_map/ppermute | solution.py:260
  20.8 4.5 %collective-permute-start.9 = (f32[160,128]{1,0:T(8,128)S(1)}, f32[160,128]{1,0:T(8,128)S(1)}, u32[]{:S(2)}, u32[]{:S(2)}) collective-permute-start(f32[160,128]{1,0:T(8,128)S(1)} %get-tuple-element.80), channel_id=1, source_target_pairs={{0,4},{1,3},{2,6},{3,1},{4,0},{5,7},{6,2},{7,5},{8,12},{9,11},{10,... | collective-permute-start | bytes 245768 | tf_op jit(solution)/shard_map/ppermute | solution.py:260
  25.3 5.4 %collective-permute-start.10 = (f32[160,128]{1,0:T(8,128)S(1)}, f32[160,128]{1,0:T(8,128)S(1)}, u32[]{:S(2)}, u32[]{:S(2)}) collective-permute-start(f32[160,128]{1,0:T(8,128)S(1)} %pad_maximum_fusion.2), channel_id=1, source_target_pairs={{0,16},{1,17},{2,18},{3,19},{4,20},{5,21},{6,22},{7,23},{8,24},{9,... | collective-permute-start | bytes 245768 | tf_op jit(solution)/shard_map/ppermute | solution.py:260
  30.8 1.3 %collective-permute-start.11 = (f32[160,128]{1,0:T(8,128)S(1)}, f32[160,128]{1,0:T(8,128)S(1)}, u32[]{:S(2)}, u32[]{:S(2)}) collective-permute-start(f32[160,128]{1,0:T(8,128)S(1)} %pad_maximum_fusion.3), channel_id=1, source_target_pairs={{0,1},{1,0},{2,3},{3,2},{4,5},{5,4},{6,7},{7,6},{8,9},{9,8},{10,11... | collective-permute-start | bytes 245768 | tf_op jit(solution)/shard_map/ppermute | solution.py:152

commit v6 on v5

--- a/solution.py
+++ b/solution.py
@@ -15,6 +15,8 @@
 
 
 def split(value, parts):
+    if value.dtype == BF16:
+        return [value]
     pieces = []
     for index in range(parts):
         piece = value.astype(BF16)
@@ -43,9 +45,8 @@
     return rows >= columns
 
 
-def cumulate(decay, lower=None):
-    if lower is None:
-        lower = lower_mask(decay.shape[0]).astype(F32).astype(BF16)
+def cumulate(decay):
+    lower = lower_mask(decay.shape[0]).astype(F32).astype(BF16)
     return product([lower], split(decay, 3), 1, 0)
 
 
@@ -196,48 +197,58 @@
             offset += rows
 
 
+def joined(pairs, left_axis, right_axis):
+    lefts, rights = [], []
+    for left, left_parts, right, right_parts in pairs:
+        left, right = split(left, left_parts), split(right, right_parts)
+        for i in range(left_parts):
+            for j in range(right_parts):
+                if i + j < max(left_parts, right_parts):
+                    lefts.append(left[i])
+                    rights.append(right[j])
+    return lax.dot_general(
+        jnp.concatenate(lefts, axis=left_axis),
+        jnp.concatenate(rights, axis=right_axis),
+        (((left_axis,), (right_axis,)), ((), ())),
+        preferred_element_type=F32,
+    )
+
+
 def joint_kernel(
     own_ref, other_ref, lower_ref,
     cumul_ref, scores_ref, state_ref, normed_ref, scale_ref, rounded_ref,
 ):
     first = lax.axis_index("ctx") == 0
-    length = cumul_ref.shape[0]
+    length, width = cumul_ref.shape
     lower = lower_mask(length)
-
-    def scaled(block):
-        query, key, value, decay = block
-        cumul = cumulate(decay, lower_ref[...])
-        query_scaled = split(query * jnp.exp(cumul), 2)
-        key_scaled = split(key * jnp.exp(-cumul), 2)
-        return cumul, query_scaled, key_scaled, value.astype(BF16)
-
-    def within(query_scaled, key_scaled, value):
-        scores = jnp.where(lower, product(query_scaled, key_scaled, 1, 1), 0.0)
-        return scores, product(split(scores, 2), [value], 1, 0)
 
     def normalized(output):
         scale_inv = lax.rsqrt(jnp.mean(output * output, axis=-1, keepdims=True) + EPSILON)
         normed = output * scale_inv
         return normed, jnp.broadcast_to(scale_inv, normed.shape), normed.astype(BF16)
 
-    early = [jnp.where(first, own_ref[i], other_ref[i]) for i in range(4)]
-    late = [jnp.where(first, other_ref[i], own_ref[i]) for i in range(4)]
-    cumul_early, queries_early, keys_early, values_early = scaled(early)
-    cumul_late, queries_late, keys_late, values_late = scaled(late)
-    to_end = jnp.exp(cumul_early[-1:] - cumul_early)
-    state = product(split(early[1] * to_end, 2), [values_early], 0, 0)
-    scores_early, output_early = within(queries_early, keys_early, values_early)
-    scores_late, output_late = within(queries_late, keys_late, values_late)
-    output_late += product(queries_late, split(state, 2), 1, 0)
-    done_early = normalized(output_early)
-    done_late = normalized(output_late)
-    cumul_ref[...] = jnp.where(first, cumul_early, cumul_late)
-    scores_ref[...] = jnp.where(first, scores_early, scores_late)
+    query, key, value, decay = [
+        [jnp.where(first, own_ref[i], other_ref[i]), jnp.where(first, other_ref[i], own_ref[i])]
+        for i in range(4)
+    ]
+    cumuls = joined([(lower_ref[...], 1, jnp.concatenate(decay, axis=1), 3)], 1, 0)
+    cumul = [cumuls[:, :width], cumuls[:, width:]]
+    scaled = [q * jnp.exp(c) for q, c in zip(query, cumul)]
+    scores = [
+        jnp.where(lower, joined([(q, 2, k * jnp.exp(-c), 2)], 1, 1), 0.0)
+        for q, k, c in zip(scaled, key, cumul)
+    ]
+    to_end = jnp.exp(cumul[0][-1:] - cumul[0])
+    state = joined([(key[0] * to_end, 2, value[0], 1)], 0, 0)
+    early = normalized(joined([(scores[0], 2, value[0], 1)], 1, 0))
+    late = normalized(joined([(scores[1], 2, value[1], 1), (scaled[1], 2, state, 2)], 1, 0))
+    rounded_ref[:length] = jnp.where(first, early[2], late[2])
+    rounded_ref[length:] = jnp.where(first, late[2], early[2])
+    cumul_ref[...] = jnp.where(first, cumul[0], cumul[1])
+    scores_ref[...] = jnp.where(first, scores[0], scores[1])
     state_ref[...] = jnp.where(first, 0.0, state)
-    normed_ref[...] = jnp.where(first, done_early[0], done_late[0])
-    scale_ref[...] = jnp.where(first, done_early[1], done_late[1])
-    rounded_ref[:length] = jnp.where(first, done_early[2], done_late[2])
-    rounded_ref[length:] = jnp.where(first, done_late[2], done_early[2])
+    normed_ref[...] = jnp.where(first, early[0], late[0])
+    scale_ref[...] = jnp.where(first, early[1], late[1])
 
 
 def share_kernel(begin, own_ref, received_ref, rounded_ref, *outs):
@@ -289,6 +300,13 @@
     return jnp.concatenate(kept)
 
 
+def assemble_kernel(mine_ref, theirs_ref, out_ref):
+    core = lax.axis_index("ctx")
+    rows = mine_ref.shape[0]
+    out_ref[pl.ds(pl.multiple_of(core * rows, 8), rows)] = mine_ref[...]
+    out_ref[pl.ds(pl.multiple_of((1 - core) * rows, 8), rows)] = theirs_ref[...]
+
+
 def shifted(value, axis, steps):
     count = lax.axis_size(axis)
     leading, last = (max(0, -steps), min(count, count - steps))
@@ -320,8 +338,6 @@
         )
         others = swap(packed)
         received_first = swap(send_first)
-        others, send_second = lax.optimization_barrier((others, send_second))
-        received_second = swap(send_second)
         cumul, scores, state_in, normed, scale_inv, rounded = local_call(
             joint_kernel,
             [
@@ -331,6 +347,8 @@
             packed, others, lower,
             name="joint", flops=40 * flops,
         )
+        rounded, send_second = lax.optimization_barrier((rounded, send_second))
+        received_second = swap(send_second)
         sent = local_call(
             functools.partial(share_kernel, 0),
             [((count // 2 * part, width), F32) for part, _ in plan],
@@ -406,10 +424,9 @@
         mine = halving(kept, sent, plan, count, beside)
         grad_query = held["query"]
         grad_key, grad_value, grad_decay = held["finished"]
-        theirs = swap(mine)
-        first = lax.axis_index("ctx") == 0
-        grad_weight = jnp.concatenate(
-            [jnp.where(first, mine, theirs), jnp.where(first, theirs, mine)], axis=0
+        (grad_weight,) = local_call(
+            assemble_kernel, [((2 * rows, width), F32)], mine, swap(mine),
+            name="assemble", flops=flops // 4,
         )
     else:
         for _ in range(shards - 2):

time: 32.9 us -> 32.9 us (level)
  other arithmetic: 0.89 us -> 0.2 us
  Pallas kernels: 4.79 us -> 5.25 us
    concatenate x1 -> x0, other arithmetic: 0.68 us -> none  [body(): jnp.concatenate([jnp.where(first, mine, theirs), jnp.where(first, theirs,...]
    pallas_call x7 -> x8, Pallas kernels: 4.79 us -> 5.25 us  [local_call(): pl.pallas_call(kernel, out_shape=outs, in_specs=[pl.BlockSpec(memory_spac...]
  transfers between devices with their start and end apart: 12 -> 12, of which waited for: 8 -> 8; matrix products, arithmetic and copies ran while one was open for 0% -> 0% of each run, Pallas kernels for 15% -> 14%
where the time goes in v6:
time: 32.9 us; the launch traced here: 32.8 us
  starting transfers between devices  16.1 us (49%)
  waiting for transfers between devices  9.67 us (29%)
  Pallas kernels  5.25 us (16%)
  local copies, waits for them, and re-layouts  0.83 us (3%)
  between operations  0.77 us (2%)
    ppermute x7, starting transfers between devices, exchanged(): return lax.ppermute(value, BOTH, pairs)  14.5 us
    ppermute x7, waiting for transfers between devices, exchanged(): return lax.ppermute(value, BOTH, pairs)  7.89 us
    pallas_call x8, Pallas kernels, local_call(): pl.pallas_call(kernel, out_shape=outs, in_specs=[pl.BlockSpec(memory_spac...  5.25 us
    ppermute x5, waiting for transfers between devices, swap(): return lax.ppermute(value, 'ctx', [(0, 1), (1, 0)])  1.79 us
    ppermute x5, starting transfers between devices, swap(): return lax.ppermute(value, 'ctx', [(0, 1), (1, 0)])  1.52 us
    unnamed x12, local copies, waits for them, and re-layouts  0.83 us
  transfers between devices with their start and end apart: 12, of which 8 were waited for; matrix products, arithmetic and copies ran while one was open for 0% of the time, Pallas kernels for 14%

profile of v6, /device:TPU:0, one launch (start us, length us, event | category | flops | bytes accessed | tf_op | source)
XLA Modules:
  0.0 32.8 jit_solution(1566372346425483184)
XLA Ops:
  0.6 0.0 copy-start.5
  0.6 0.0 copy-start.4
  0.7 0.0 copy-start.3
  0.7 0.0 copy-start.2
  0.7 0.0 copy-start
  0.7 0.7 %copy-done.5 = bf16[1,128,128]{2,1,0:T(8,128)(2,1)S(1)} copy-done((bf16[1,128,128]{2,1,0:T(8,128)(2,1)S(1)}, bf16[1,128,128]{2,1,0:T(8,128)(2,1)}, u32[]{:S(2)}) %copy-start.5) | copy-done | bytes 32792
  1.4 0.0 copy-done.4
  1.4 0.0 copy-done.3
  1.4 0.1 copy-done.2
  1.6 0.5 %collective-permute-start.1 = (f32[4,128,128]{2,1,0:T(8,128)S(1)}, f32[4,128,128]{2,1,0:T(8,128)S(1)}, u32[]{:S(2)}, u32[]{:S(2)}) collective-permute-start(f32[4,128,128]{2,1,0:T(8,128)S(1)} %pad_maximum_fusion.own_ref.packed_ref), channel_id=1, source_target_pairs={{0,1},{1,0},{2,3},{3,2},{4,5},{5,4},{6,7},{7,6},{8,9},{9,8},{10,11... | collective-permute-start | bytes 786440 | tf_op jit(solution)/shard_map/ppermute | solution.py:153
  2.1 0.0 copy-done
  2.1 0.6 %turn.1 = (bf16[2560,128]{1,0:T(8,128)(2,1)S(1)}, f32[1280,128]{1,0:T(8,128)S(1)}, f32[1280,128]{1,0:T(8,128)S(1)}) custom-call(bf16[1,128,5120]{2,1,0:T(8,128)(2,1)S(1)} %copy-done), custom_call_target="tpu_custom_call" | custom-call | flops 13421772800 | bytes 3276800 | tf_op jit(solution)/shard_map/turn/pallas_call | solution.py:141
  2.6 0.5 %collective-permute-start = (f32[1280,128]{1,0:T(8,128)S(1)}, f32[1280,128]{1,0:T(8,128)S(1)}, u32[]{:S(2)}, u32[]{:S(2)}) collective-permute-start(f32[1280,128]{1,0:T(8,128)S(1)} %get-tuple-element.40), channel_id=1, source_target_pairs={{0,1},{1,0},{2,3},{3,2},{4,5},{5,4},{6,7},{7,6},{8,9},{9,8},{10,11... | collective-permute-start | bytes 1966088 | tf_op jit(solution)/shard_map/ppermute | solution.py:153
  3.1 0.1 collective-permute-done.1.other_ref
  3.2 0.7 %joint.1 = (f32[128,128]{1,0:T(8,128)S(1)}, f32[128,128]{1,0:T(8,128)S(1)}, f32[128,128]{1,0:T(8,128)S(1)}, f32[128,128]{1,0:T(8,128)S(1)}, f32[128,128]{1,0:T(8,128)S(1)}, /*index=5*/bf16[256,128]{1,0:T(8,128)(2,1)S(1)}) custom-call(f32[4,128,128]{2,1,0:T(8,128)S(1)} %pad_maximum_fusion.own_ref.packed_ref, ...), custom_call_target="tpu_custom_call" | custom-call | flops 26843545600 | bytes 950272 | tf_op jit(solution)/shard_map/joint/pallas_call | solution.py:141
  4.0 0.0 copy-start.1
  4.0 0.4 %collective-permute-start.3 = (f32[1280,128]{1,0:T(8,128)S(1)}, f32[1280,128]{1,0:T(8,128)S(1)}, u32[]{:S(2)}, u32[]{:S(2)}) collective-permute-start(f32[1280,128]{1,0:T(8,128)S(1)} %get-tuple-element.60), channel_id=1, source_target_pairs={{0,1},{1,0},{2,3},{3,2},{4,5},{5,4},{6,7},{7,6},{8,9},{9,8},{10,11... | collective-permute-start | bytes 1966088 | tf_op jit(solution)/shard_map/ppermute | solution.py:153
  4.4 0.4 %collective-permute-done.received_ref = f32[1280,128]{1,0:T(8,128)S(1)} collective-permute-done((f32[1280,128]{1,0:T(8,128)S(1)}, f32[1280,128]{1,0:T(8,128)S(1)}, u32[]{:S(2)}, u32[]{:S(2)}) %collective-permute-start) | collective-permute-done | bytes 655392 | tf_op jit(solution)/shard_map/ppermute | solution.py:153
  4.9 0.3 sent_shares.1
  5.2 2.9 %collective-permute-start.4 = (f32[640,128]{1,0:T(8,128)S(1)}, f32[640,128]{1,0:T(8,128)S(1)}, u32[]{:S(2)}, u32[]{:S(2)}) collective-permute-start(f32[640,128]{1,0:T(8,128)S(1)} %get-tuple-element.62), channel_id=1, source_target_pairs={{0,2},{1,5},{2,0},{3,7},{4,6},{5,1},{6,4},{7,3},{8,10},{9,13},{10,... | collective-permute-start | bytes 983048 | tf_op jit(solution)/shard_map/ppermute | solution.py:271
  8.1 1.6 %collective-permute-start.2 = (f32[640,128]{1,0:T(8,128)S(1)}, f32[640,128]{1,0:T(8,128)S(1)}, u32[]{:S(2)}, u32[]{:S(2)}) collective-permute-start(f32[640,128]{1,0:T(8,128)S(1)} %get-tuple-element.49), channel_id=1, source_target_pairs={{0,8},{1,5},{2,10},{3,7},{4,12},{5,1},{6,14},{7,3},{8,0},{9,13},{1... | collective-permute-start | bytes 983048 | tf_op jit(solution)/shard_map/ppermute | solution.py:271
  9.7 0.0 copy-done.1
  9.7 1.6 %grads.1 = (bf16[1,128,128]{2,1,0:T(8,128)(2,1)}, f32[128,128]{1,0:T(8,128)S(1)}, f32[128,128]{1,0:T(8,128)S(1)}, f32[128,128]{1,0:T(8,128)S(1)}, f32[136,128]{1,0:T(8,128)S(1)}) custom-call(f32[4,128,128]{2,1,0:T(8,128)S(1)} %pad_maximum_fusion.own_ref.packed_ref, f32[128,128]{1,0:T(8,128)S(1)} %get-tuple-element.50.cumul_ref, ...), custom_call_target="tpu_custom_call" | custom-call | flops 1342177280 | bytes 3510272 | tf_op jit(solution)/shard_map/grads/pallas_call | solution.py:141
  11.3 0.0 collective-permute-start.7
  11.3 0.0 collective-permute-done.3.received_ref
  11.3 0.3 kept_shares.1
  11.6 1.6 %collective-permute-done.4 = f32[640,128]{1,0:T(8,128)S(1)} collective-permute-done((f32[640,128]{1,0:T(8,128)S(1)}, f32[640,128]{1,0:T(8,128)S(1)}, u32[]{:S(2)}, u32[]{:S(2)}) %collective-permute-start.4) | collective-permute-done | bytes 327712 | tf_op jit(solution)/shard_map/ppermute | solution.py:271
  13.2 2.1 %collective-permute-start.5 = (f32[320,128]{1,0:T(8,128)S(1)}, f32[320,128]{1,0:T(8,128)S(1)}, u32[]{:S(2)}, u32[]{:S(2)}) collective-permute-start(f32[320,128]{1,0:T(8,128)S(1)} %get-tuple-element.76), channel_id=1, source_target_pairs={{0,4},{1,3},{2,6},{3,1},{4,0},{5,7},{6,2},{7,5},{8,12},{9,11},{10,... | collective-permute-start | bytes 491528 | tf_op jit(solution)/shard_map/ppermute | solution.py:271
  15.3 0.0 collective-permute-done.2
  15.4 1.6 %collective-permute-start.8 = (f32[320,128]{1,0:T(8,128)S(1)}, f32[320,128]{1,0:T(8,128)S(1)}, u32[]{:S(2)}, u32[]{:S(2)}) collective-permute-start(f32[320,128]{1,0:T(8,128)S(1)} %get-tuple-element.74), channel_id=1, source_target_pairs={{0,2},{1,9},{2,0},{3,11},{4,6},{5,13},{6,4},{7,15},{8,10},{9,1},{1... | collective-permute-start | bytes 491528 | tf_op jit(solution)/shard_map/ppermute | solution.py:271
  16.9 1.7 %collective-permute-done.5 = f32[320,128]{1,0:T(8,128)S(1)} collective-permute-done((f32[320,128]{1,0:T(8,128)S(1)}, f32[320,128]{1,0:T(8,128)S(1)}, u32[]{:S(2)}, u32[]{:S(2)}) %collective-permute-start.5) | collective-permute-done | bytes 163872 | tf_op jit(solution)/shard_map/ppermute | solution.py:271
  18.6 2.1 %collective-permute-start.6 = (f32[160,128]{1,0:T(8,128)S(1)}, f32[160,128]{1,0:T(8,128)S(1)}, u32[]{:S(2)}, u32[]{:S(2)}) collective-permute-start(f32[160,128]{1,0:T(8,128)S(1)} %get-tuple-element.78), channel_id=1, source_target_pairs={{0,8},{1,9},{2,10},{3,11},{4,12},{5,13},{6,14},{7,15},{8,0},{9,1},... | collective-permute-start | bytes 245768 | tf_op jit(solution)/shard_map/ppermute | solution.py:271
  20.8 0.0 collective-permute-done.8
  20.8 1.6 %collective-permute-start.9 = (f32[160,128]{1,0:T(8,128)S(1)}, f32[160,128]{1,0:T(8,128)S(1)}, u32[]{:S(2)}, u32[]{:S(2)}) collective-permute-start(f32[160,128]{1,0:T(8,128)S(1)} %get-tuple-element.80), channel_id=1, source_target_pairs={{0,4},{1,3},{2,6},{3,1},{4,0},{5,7},{6,2},{7,5},{8,12},{9,11},{10,... | collective-permute-start | bytes 245768 | tf_op jit(solution)/shard_map/ppermute | solution.py:271
  22.4 0.0 collective-permute-done.7.later_ref
  22.4 0.8 %collective-permute-done.6 = f32[160,128]{1,0:T(8,128)S(1)} collective-permute-done((f32[160,128]{1,0:T(8,128)S(1)}, f32[160,128]{1,0:T(8,128)S(1)}, u32[]{:S(2)}, u32[]{:S(2)}) %collective-permute-start.6) | collective-permute-done | bytes 81952 | tf_op jit(solution)/shard_map/ppermute | solution.py:271
  23.2 2.1 %collective-permute-done.9 = f32[160,128]{1,0:T(8,128)S(1)} collective-permute-done((f32[160,128]{1,0:T(8,128)S(1)}, f32[160,128]{1,0:T(8,128)S(1)}, u32[]{:S(2)}, u32[]{:S(2)}) %collective-permute-start.9) | collective-permute-done | bytes 81952 | tf_op jit(solution)/shard_map/ppermute | solution.py:271
  25.3 2.7 %collective-permute-start.10 = (f32[160,128]{1,0:T(8,128)S(1)}, f32[160,128]{1,0:T(8,128)S(1)}, u32[]{:S(2)}, u32[]{:S(2)}) collective-permute-start(f32[160,128]{1,0:T(8,128)S(1)} %pad_maximum_fusion.1), channel_id=1, source_target_pairs={{0,16},{1,17},{2,18},{3,19},{4,20},{5,21},{6,22},{7,23},{8,24},{9,... | collective-permute-start | bytes 245768 | tf_op jit(solution)/shard_map/ppermute | solution.py:271
  28.0 1.0 %finish.1 = (bf16[1,128,128]{2,1,0:T(8,128)(2,1)}, bf16[1,128,128]{2,1,0:T(8,128)(2,1)}, f32[1,128,128]{2,1,0:T(8,128)}) custom-call(f32[4,128,128]{2,1,0:T(8,128)S(1)} %pad_maximum_fusion.own_ref.packed_ref, f32[128,128]{1,0:T(8,128)S(1)} %get-tuple-element.50.cumul_ref, f32[128,128]{1,0:T(8,128)S(1)} %get-tuple-element.57.grad_key_ref, ...), custom_call_target="tpu_custom_call" | custom-call | flops 671088640 | bytes 724992 | tf_op jit(solution)/shard_map/finish/pallas_call | solution.py:141
  29.0 1.7 %collective-permute-done.10 = f32[160,128]{1,0:T(8,128)S(1)} collective-permute-done((f32[160,128]{1,0:T(8,128)S(1)}, f32[160,128]{1,0:T(8,128)S(1)}, u32[]{:S(2)}, u32[]{:S(2)}) %collective-permute-start.10) | collective-permute-done | bytes 81952 | tf_op jit(solution)/shard_map/ppermute | solution.py:271
  30.8 0.1 collective-permute-start.11
  30.8 1.3 %collective-permute-done.11.theirs_ref = f32[160,128]{1,0:T(8,128)S(1)} collective-permute-done((f32[160,128]{1,0:T(8,128)S(1)}, f32[160,128]{1,0:T(8,128)S(1)}, u32[]{:S(2)}, u32[]{:S(2)}) %collective-permute-start.11) | collective-permute-done | bytes 81952 | tf_op jit(solution)/shard_map/ppermute | solution.py:153
  32.1 0.7 %assemble.1 = f32[320,128]{1,0:T(8,128)} custom-call(f32[160,128]{1,0:T(8,128)S(1)} %pad_maximum_fusion.2.mine_ref, f32[160,128]{1,0:T(8,128)S(1)} %collective-permute-done.11.theirs_ref), custom_call_target="tpu_custom_call" | custom-call | flops 167772160 | bytes 327680 | tf_op jit(solution)/shard_map/assemble/pallas_call | solution.py:141
  (12 shorter events, 0.2 us)
Async XLA Ops:
  0.6 0.8 %copy-start.5 = (bf16[1,128,128]{2,1,0:T(8,128)(2,1)S(1)}, bf16[1,128,128]{2,1,0:T(8,128)(2,1)}, u32[]{:S(2)}) copy-start(bf16[1,128,128]{2,1,0:T(8,128)(2,1)} %param.6) | copy-start | bytes 98308
  0.6 0.8 %copy-start.4 = (bf16[1,128,128]{2,1,0:T(8,128)(2,1)S(1)}, bf16[1,128,128]{2,1,0:T(8,128)(2,1)}, u32[]{:S(2)}) copy-start(bf16[1,128,128]{2,1,0:T(8,128)(2,1)} %param.7) | copy-start | bytes 98308
  0.7 0.8 %copy-start.3 = (bf16[1,128,128]{2,1,0:T(8,128)(2,1)S(1)}, bf16[1,128,128]{2,1,0:T(8,128)(2,1)}, u32[]{:S(2)}) copy-start(bf16[1,128,128]{2,1,0:T(8,128)(2,1)} %param.8) | copy-start | bytes 98308
  0.7 0.9 %copy-start.2 = (f32[1,128,128]{2,1,0:T(8,128)S(1)}, f32[1,128,128]{2,1,0:T(8,128)}, u32[]{:S(2)}) copy-start(f32[1,128,128]{2,1,0:T(8,128)} %param.9) | copy-start | bytes 196612
  0.7 1.4 %copy-start = (bf16[1,128,5120]{2,1,0:T(8,128)(2,1)S(1)}, bf16[1,128,5120]{2,1,0:T(8,128)(2,1)}, u32[]{:S(2)}) copy-start(bf16[1,128,5120]{2,1,0:T(8,128)(2,1)} %upstream_ref.3) | copy-start | bytes 3932164
  1.6 1.7 %collective-permute-start.1 = (f32[4,128,128]{2,1,0:T(8,128)S(1)}, f32[4,128,128]{2,1,0:T(8,128)S(1)}, u32[]{:S(2)}, u32[]{:S(2)}) collective-permute-start(f32[4,128,128]{2,1,0:T(8,128)S(1)} %pad_maximum_fusion.own_ref.packed_ref), channel_id=1, source_target_pairs={{0,1},{1,0},{2,3},{3,2},{4,5},{5,4},{6,7},{7,6},{8,9},{9,8},{10,11... | collective-permute-start | bytes 786440 | tf_op jit(solution)/shard_map/ppermute | solution.py:153
  2.6 2.2 %collective-permute-start = (f32[1280,128]{1,0:T(8,128)S(1)}, f32[1280,128]{1,0:T(8,128)S(1)}, u32[]{:S(2)}, u32[]{:S(2)}) collective-permute-start(f32[1280,128]{1,0:T(8,128)S(1)} %get-tuple-element.40), channel_id=1, source_target_pairs={{0,1},{1,0},{2,3},{3,2},{4,5},{5,4},{6,7},{7,6},{8,9},{9,8},{10,11... | collective-permute-start | bytes 1966088 | tf_op jit(solution)/shard_map/ppermute | solution.py:153
  4.0 5.7 %copy-start.1 = (bf16[5120,128]{1,0:T(8,128)(2,1)S(1)}, bf16[5120,128]{1,0:T(8,128)(2,1)}, u32[]{:S(2)}) copy-start(bf16[5120,128]{1,0:T(8,128)(2,1)} %weight_ref.1) | copy-start | bytes 3932164
  4.0 7.3 %collective-permute-start.3 = (f32[1280,128]{1,0:T(8,128)S(1)}, f32[1280,128]{1,0:T(8,128)S(1)}, u32[]{:S(2)}, u32[]{:S(2)}) collective-permute-start(f32[1280,128]{1,0:T(8,128)S(1)} %get-tuple-element.60), channel_id=1, source_target_pairs={{0,1},{1,0},{2,3},{3,2},{4,5},{5,4},{6,7},{7,6},{8,9},{9,8},{10,11... | collective-permute-start | bytes 1966088 | tf_op jit(solution)/shard_map/ppermute | solution.py:153
  5.2 8.0 %collective-permute-start.4 = (f32[640,128]{1,0:T(8,128)S(1)}, f32[640,128]{1,0:T(8,128)S(1)}, u32[]{:S(2)}, u32[]{:S(2)}) collective-permute-start(f32[640,128]{1,0:T(8,128)S(1)} %get-tuple-element.62), channel_id=1, source_target_pairs={{0,2},{1,5},{2,0},{3,7},{4,6},{5,1},{6,4},{7,3},{8,10},{9,13},{10,... | collective-permute-start | bytes 983048 | tf_op jit(solution)/shard_map/ppermute | solution.py:271
  8.1 7.2 %collective-permute-start.2 = (f32[640,128]{1,0:T(8,128)S(1)}, f32[640,128]{1,0:T(8,128)S(1)}, u32[]{:S(2)}, u32[]{:S(2)}) collective-permute-start(f32[640,128]{1,0:T(8,128)S(1)} %get-tuple-element.49), channel_id=1, source_target_pairs={{0,8},{1,5},{2,10},{3,7},{4,12},{5,1},{6,14},{7,3},{8,0},{9,13},{1... | collective-permute-start | bytes 983048 | tf_op jit(solution)/shard_map/ppermute | solution.py:271
  11.3 11.1 %collective-permute-start.7 = (f32[136,128]{1,0:T(8,128)S(1)}, f32[136,128]{1,0:T(8,128)S(1)}, u32[]{:S(2)}, u32[]{:S(2)}) collective-permute-start(f32[136,128]{1,0:T(8,128)S(1)} %get-tuple-element.63), channel_id=1, source_target_pairs={{0,1},{1,0},{2,3},{3,2},{4,5},{5,4},{6,7},{7,6},{8,9},{9,8},{10,11... | collective-permute-start | bytes 208904 | tf_op jit(solution)/shard_map/ppermute | solution.py:153
  13.2 5.4 %collective-permute-start.5 = (f32[320,128]{1,0:T(8,128)S(1)}, f32[320,128]{1,0:T(8,128)S(1)}, u32[]{:S(2)}, u32[]{:S(2)}) collective-permute-start(f32[320,128]{1,0:T(8,128)S(1)} %get-tuple-element.76), channel_id=1, source_target_pairs={{0,4},{1,3},{2,6},{3,1},{4,0},{5,7},{6,2},{7,5},{8,12},{9,11},{10,... | collective-permute-start | bytes 491528 | tf_op jit(solution)/shard_map/ppermute | solution.py:271
  15.4 5.4 %collective-permute-start.8 = (f32[320,128]{1,0:T(8,128)S(1)}, f32[320,128]{1,0:T(8,128)S(1)}, u32[]{:S(2)}, u32[]{:S(2)}) collective-permute-start(f32[320,128]{1,0:T(8,128)S(1)} %get-tuple-element.74), channel_id=1, source_target_pairs={{0,2},{1,9},{2,0},{3,11},{4,6},{5,13},{6,4},{7,15},{8,10},{9,1},{1... | collective-permute-start | bytes 491528 | tf_op jit(solution)/shard_map/ppermute | solution.py:271
  18.6 4.6 %collective-permute-start.6 = (f32[160,128]{1,0:T(8,128)S(1)}, f32[160,128]{1,0:T(8,128)S(1)}, u32[]{:S(2)}, u32[]{:S(2)}) collective-permute-start(f32[160,128]{1,0:T(8,128)S(1)} %get-tuple-element.78), channel_id=1, source_target_pairs={{0,8},{1,9},{2,10},{3,11},{4,12},{5,13},{6,14},{7,15},{8,0},{9,1},... | collective-permute-start | bytes 245768 | tf_op jit(solution)/shard_map/ppermute | solution.py:271
  20.8 4.5 %collective-permute-start.9 = (f32[160,128]{1,0:T(8,128)S(1)}, f32[160,128]{1,0:T(8,128)S(1)}, u32[]{:S(2)}, u32[]{:S(2)}) collective-permute-start(f32[160,128]{1,0:T(8,128)S(1)} %get-tuple-element.80), channel_id=1, source_target_pairs={{0,4},{1,3},{2,6},{3,1},{4,0},{5,7},{6,2},{7,5},{8,12},{9,11},{10,... | collective-permute-start | bytes 245768 | tf_op jit(solution)/shard_map/ppermute | solution.py:271
  25.3 5.4 %collective-permute-start.10 = (f32[160,128]{1,0:T(8,128)S(1)}, f32[160,128]{1,0:T(8,128)S(1)}, u32[]{:S(2)}, u32[]{:S(2)}) collective-permute-start(f32[160,128]{1,0:T(8,128)S(1)} %pad_maximum_fusion.1), channel_id=1, source_target_pairs={{0,16},{1,17},{2,18},{3,19},{4,20},{5,21},{6,22},{7,23},{8,24},{9,... | collective-permute-start | bytes 245768 | tf_op jit(solution)/shard_map/ppermute | solution.py:271
  30.8 1.3 %collective-permute-start.11 = (f32[160,128]{1,0:T(8,128)S(1)}, f32[160,128]{1,0:T(8,128)S(1)}, u32[]{:S(2)}, u32[]{:S(2)}) collective-permute-start(f32[160,128]{1,0:T(8,128)S(1)} %pad_maximum_fusion.2.mine_ref), channel_id=1, source_target_pairs={{0,1},{1,0},{2,3},{3,2},{4,5},{5,4},{6,7},{7,6},{8,9},{9,8},{10,11... | collective-permute-start | bytes 245768 | tf_op jit(solution)/shard_map/ppermute | solution.py:153

commit v7 on v6

--- a/solution.py
+++ b/solution.py
@@ -154,12 +154,11 @@
 
 
 def halving_plan(count, rows):
-    bits = count.bit_length() - 1
+    rest = list(range(3, count.bit_length() - 2))
     last = rows // 32 * 16
-    rest = list(range(3, bits))
     return [
-        (rows - last, ([0, 1, 2] + rest, [1, 0, 2] + rest)),
-        (last, ([2, 0, 1] + rest, [1, 2, 0] + rest)),
+        (rows - last, ([0, 2, 1] + rest, [1, 2, 0] + rest)),
+        (last, ([0, 1, 2] + rest, [2, 1, 0] + rest)),
     ]
 
 
@@ -179,18 +178,18 @@
     for start in range(0, model, lanes):
         turned[start:start + lanes] = jnp.transpose(upstream_ref[0, :, start:start + lanes].astype(F32))
     share = model // count
-    half = share // 2
+    places = count // 2
     at = 0
-    for ref, places in ((first_ref, range(count // 2, count)), (second_ref, range(count // 2))):
+    for ref, part in ((first_ref, range(places // 2, places)), (second_ref, range(places // 2))):
         offset = sent = 0
         for rows, orders in plan:
-            for place in places:
-                masks = [relative(place, order) for order in orders]
+            for place in part:
+                masks = [relative(place, orders[0]), relative(place, orders[1]) + places]
                 mine = me ^ (masks[0] + core * (masks[1] - masks[0]))
                 other = me ^ (masks[1] + core * (masks[0] - masks[1]))
-                begin = pl.multiple_of(mine * share + core * half + offset, 16)
+                begin = pl.multiple_of(mine * share + offset, 16)
                 own_ref[at:at + rows] = turned[pl.ds(begin, rows)].astype(BF16)
-                begin = pl.multiple_of(other * share + (1 - core) * half + offset, 16)
+                begin = pl.multiple_of(other * share + offset, 16)
                 ref[sent:sent + rows] = turned[pl.ds(begin, rows)]
                 at += rows
                 sent += rows
@@ -300,11 +299,12 @@
     return jnp.concatenate(kept)
 
 
-def assemble_kernel(mine_ref, theirs_ref, out_ref):
-    core = lax.axis_index("ctx")
-    rows = mine_ref.shape[0]
-    out_ref[pl.ds(pl.multiple_of(core * rows, 8), rows)] = mine_ref[...]
-    out_ref[pl.ds(pl.multiple_of((1 - core) * rows, 8), rows)] = theirs_ref[...]
+def pick_kernel(near_ref, far_ref, out_ref):
+    out_ref[...] = jnp.where(lax.axis_index("ctx") == 0, near_ref[...], far_ref[...])
+
+
+def add_kernel(mine_ref, theirs_ref, out_ref):
+    out_ref[...] = mine_ref[...] + theirs_ref[...]
 
 
 def shifted(value, axis, steps):
@@ -318,9 +318,9 @@
     model = cotangent.shape[2]
     shards, count = lax.axis_size("ctx"), lax.axis_size("dp")
     square = (length, width)
-    rows = model // count // 2
+    rows = model // count
     flops = 8 * length * width * model
-    paired = shards == 2 and count >= 16 and count & (count - 1) == 0 and rows % 16 == 0
+    paired = shards == 2 and count >= 16 and count & (count - 1) == 0 and rows % 32 == 0
 
     (lower,) = local_call(lower_kernel, [((length, length), BF16)], name="lower", flops=20 * flops)
     inputs = (queries, key_vectors, value_vectors, log_decay)
@@ -328,7 +328,7 @@
     packed = jnp.concatenate([jnp.concatenate(inputs[:3]).astype(F32), inputs[3]])
     if paired:
         plan = halving_plan(count, rows)
-        part_rows = rows * count // 2
+        part_rows = rows * count // 4
         own, send_first, send_second = local_call(
             functools.partial(turn_kernel, count, plan),
             [((2 * part_rows, length), BF16), ((part_rows, length), F32), ((part_rows, length), F32)],
@@ -351,13 +351,13 @@
         received_second = swap(send_second)
         sent = local_call(
             functools.partial(share_kernel, 0),
-            [((count // 2 * part, width), F32) for part, _ in plan],
+            [((count // 4 * part, width), F32) for part, _ in plan],
             own, received_first, rounded,
             name="sent_shares", flops=flops // 4,
         )
         kept = local_call(
             functools.partial(share_kernel, part_rows),
-            [((count // 2 * part, width), F32) for part, _ in plan],
+            [((count // 4 * part, width), F32) for part, _ in plan],
             own, received_second, rounded,
             name="kept_shares", flops=flops // 4,
         )
@@ -414,20 +414,20 @@
             large, held["later"] = lax.optimization_barrier((large, later))
             return [large, small]
 
-        def beside_last(arrived):
-            key, value, decay = finish(held["later"])
-            arrived, decay = lax.optimization_barrier((arrived, decay))
-            held["finished"] = key, value, decay
-            return arrived
-
-        beside = {0: beside_first, 2: beside_third, 3: beside_last}
-        mine = halving(kept, sent, plan, count, beside)
+        beside = {0: beside_first, 2: beside_third}
+        near = halving(kept, sent, plan, count, beside)
+        far = lax.ppermute(
+            near, BOTH, [(device * 2 + 1, (device ^ (count // 2)) * 2 + 1) for device in range(count)]
+        )
+        grad_key, grad_value, grad_decay = finish(held["later"])
+        far, grad_decay = lax.optimization_barrier((far, grad_decay))
+        (mine,) = local_call(
+            pick_kernel, [((rows, width), F32)], near, far, name="pick", flops=flops // 4
+        )
+        (grad_weight,) = local_call(
+            add_kernel, [((rows, width), F32)], mine, swap(mine), name="add", flops=flops // 4
+        )
         grad_query = held["query"]
-        grad_key, grad_value, grad_decay = held["finished"]
-        (grad_weight,) = local_call(
-            assemble_kernel, [((2 * rows, width), F32)], mine, swap(mine),
-            name="assemble", flops=flops // 4,
-        )
     else:
         for _ in range(shards - 2):
             grad_in = later[:width]

time: 32.9 us -> 33.3 us (1.012)
  starting transfers between devices: 16.1 us -> 17.3 us
  waiting for transfers between devices: 9.67 us -> 8.77 us
    ppermute x5, starting transfers between devices: 1.52 us -> 5.49 us  [swap(): return lax.ppermute(value, 'ctx', [(0, 1), (1, 0)])]
    ppermute x7 -> x6, starting transfers between devices: 14.5 us -> 11.1 us  [exchanged(): return lax.ppermute(value, BOTH, pairs)]
    ppermute x7 -> x6, waiting for transfers between devices: 7.89 us -> 7.21 us  [exchanged(): return lax.ppermute(value, BOTH, pairs)]
    ppermute x0 -> x1, starting transfers between devices: none -> 0.67 us  [body(): lax.ppermute(near, BOTH, [(device * 2 + 1, (device ^ count // 2) * 2 + 1)...]
    pallas_call x8 -> x9, Pallas kernels: 5.25 us -> 5.27 us  [local_call(): pl.pallas_call(kernel, out_shape=outs, in_specs=[pl.BlockSpec(memory_spac...]
where the time goes in v7:
time: 33.3 us; the launch traced here: 33.1 us
  starting transfers between devices  17.3 us (52%)
  waiting for transfers between devices  8.77 us (26%)
  Pallas kernels  5.27 us (16%)
  local copies, waits for them, and re-layouts  0.83 us (2%)
  between operations  0.77 us (2%)
    ppermute x6, starting transfers between devices, exchanged(): return lax.ppermute(value, BOTH, pairs)  11.1 us
    ppermute x6, waiting for transfers between devices, exchanged(): return lax.ppermute(value, BOTH, pairs)  7.21 us
    ppermute x5, starting transfers between devices, swap(): return lax.ppermute(value, 'ctx', [(0, 1), (1, 0)])  5.49 us
    pallas_call x9, Pallas kernels, local_call(): pl.pallas_call(kernel, out_shape=outs, in_specs=[pl.BlockSpec(memory_spac...  5.27 us
    ppermute x5, waiting for transfers between devices, swap(): return lax.ppermute(value, 'ctx', [(0, 1), (1, 0)])  1.55 us
    unnamed x12, local copies, waits for them, and re-layouts  0.83 us
    ppermute x1, starting transfers between devices, body(): lax.ppermute(near, BOTH, [(device * 2 + 1, (device ^ count // 2) * 2 + 1)...  0.67 us
  transfers between devices with their start and end apart: 12, of which 8 were waited for; matrix products, arithmetic and copies ran while one was open for 0% of the time, Pallas kernels for 14%

profile of v7, /device:TPU:0, one launch (start us, length us, event | category | flops | bytes accessed | tf_op | source)
XLA Modules:
  0.0 33.1 jit_solution(7557563117842446166)
XLA Ops:
  0.6 0.0 copy-start.5
  0.6 0.0 copy-start.4
  0.7 0.0 copy-start.3
  0.7 0.0 copy-start.2
  0.7 0.0 copy-start
  0.7 0.7 %copy-done.5 = bf16[1,128,128]{2,1,0:T(8,128)(2,1)S(1)} copy-done((bf16[1,128,128]{2,1,0:T(8,128)(2,1)S(1)}, bf16[1,128,128]{2,1,0:T(8,128)(2,1)}, u32[]{:S(2)}) %copy-start.5) | copy-done | bytes 32792
  1.4 0.0 copy-done.4
  1.4 0.0 copy-done.3
  1.4 0.1 copy-done.2
  1.6 0.5 %collective-permute-start.1 = (f32[4,128,128]{2,1,0:T(8,128)S(1)}, f32[4,128,128]{2,1,0:T(8,128)S(1)}, u32[]{:S(2)}, u32[]{:S(2)}) collective-permute-start(f32[4,128,128]{2,1,0:T(8,128)S(1)} %pad_maximum_fusion.own_ref.packed_ref), channel_id=1, source_target_pairs={{0,1},{1,0},{2,3},{3,2},{4,5},{5,4},{6,7},{7,6},{8,9},{9,8},{10,11... | collective-permute-start | bytes 786440 | tf_op jit(solution)/shard_map/ppermute | solution.py:153
  2.1 0.0 copy-done
  2.1 0.6 %turn.1 = (bf16[2560,128]{1,0:T(8,128)(2,1)S(1)}, f32[1280,128]{1,0:T(8,128)S(1)}, f32[1280,128]{1,0:T(8,128)S(1)}) custom-call(bf16[1,128,5120]{2,1,0:T(8,128)(2,1)S(1)} %copy-done), custom_call_target="tpu_custom_call" | custom-call | flops 13421772800 | bytes 3276800 | tf_op jit(solution)/shard_map/turn/pallas_call | solution.py:141
  2.6 0.5 %collective-permute-start = (f32[1280,128]{1,0:T(8,128)S(1)}, f32[1280,128]{1,0:T(8,128)S(1)}, u32[]{:S(2)}, u32[]{:S(2)}) collective-permute-start(f32[1280,128]{1,0:T(8,128)S(1)} %get-tuple-element.40), channel_id=1, source_target_pairs={{0,1},{1,0},{2,3},{3,2},{4,5},{5,4},{6,7},{7,6},{8,9},{9,8},{10,11... | collective-permute-start | bytes 1966088 | tf_op jit(solution)/shard_map/ppermute | solution.py:153
  3.1 0.1 collective-permute-done.1.other_ref
  3.2 0.7 %joint.1 = (f32[128,128]{1,0:T(8,128)S(1)}, f32[128,128]{1,0:T(8,128)S(1)}, f32[128,128]{1,0:T(8,128)S(1)}, f32[128,128]{1,0:T(8,128)S(1)}, f32[128,128]{1,0:T(8,128)S(1)}, /*index=5*/bf16[256,128]{1,0:T(8,128)(2,1)S(1)}) custom-call(f32[4,128,128]{2,1,0:T(8,128)S(1)} %pad_maximum_fusion.own_ref.packed_ref, ...), custom_call_target="tpu_custom_call" | custom-call | flops 26843545600 | bytes 950272 | tf_op jit(solution)/shard_map/joint/pallas_call | solution.py:141
  4.0 0.0 copy-start.1
  4.0 0.4 %collective-permute-start.3 = (f32[1280,128]{1,0:T(8,128)S(1)}, f32[1280,128]{1,0:T(8,128)S(1)}, u32[]{:S(2)}, u32[]{:S(2)}) collective-permute-start(f32[1280,128]{1,0:T(8,128)S(1)} %get-tuple-element.60), channel_id=1, source_target_pairs={{0,1},{1,0},{2,3},{3,2},{4,5},{5,4},{6,7},{7,6},{8,9},{9,8},{10,11... | collective-permute-start | bytes 1966088 | tf_op jit(solution)/shard_map/ppermute | solution.py:153
  4.4 0.4 %collective-permute-done.received_ref = f32[1280,128]{1,0:T(8,128)S(1)} collective-permute-done((f32[1280,128]{1,0:T(8,128)S(1)}, f32[1280,128]{1,0:T(8,128)S(1)}, u32[]{:S(2)}, u32[]{:S(2)}) %collective-permute-start) | collective-permute-done | bytes 655392 | tf_op jit(solution)/shard_map/ppermute | solution.py:153
  4.9 0.3 sent_shares.1
  5.2 2.9 %collective-permute-start.4 = (f32[640,128]{1,0:T(8,128)S(1)}, f32[640,128]{1,0:T(8,128)S(1)}, u32[]{:S(2)}, u32[]{:S(2)}) collective-permute-start(f32[640,128]{1,0:T(8,128)S(1)} %get-tuple-element.62), channel_id=1, source_target_pairs={{0,2},{1,5},{2,0},{3,7},{4,6},{5,1},{6,4},{7,3},{8,10},{9,13},{10,... | collective-permute-start | bytes 983048 | tf_op jit(solution)/shard_map/ppermute | solution.py:270
  8.1 0.1 collective-permute-start.2
  8.2 0.0 copy-done.1
  8.2 1.6 %grads.1 = (bf16[1,128,128]{2,1,0:T(8,128)(2,1)}, f32[128,128]{1,0:T(8,128)S(1)}, f32[128,128]{1,0:T(8,128)S(1)}, f32[128,128]{1,0:T(8,128)S(1)}, f32[136,128]{1,0:T(8,128)S(1)}) custom-call(f32[4,128,128]{2,1,0:T(8,128)S(1)} %pad_maximum_fusion.own_ref.packed_ref, f32[128,128]{1,0:T(8,128)S(1)} %get-tuple-element.50.cumul_ref, ...), custom_call_target="tpu_custom_call" | custom-call | flops 1342177280 | bytes 3510272 | tf_op jit(solution)/shard_map/grads/pallas_call | solution.py:141
  9.8 1.1 %collective-permute-start.7 = (f32[136,128]{1,0:T(8,128)S(1)}, f32[136,128]{1,0:T(8,128)S(1)}, u32[]{:S(2)}, u32[]{:S(2)}) collective-permute-start(f32[136,128]{1,0:T(8,128)S(1)} %get-tuple-element.63), channel_id=1, source_target_pairs={{0,1},{1,0},{2,3},{3,2},{4,5},{5,4},{6,7},{7,6},{8,9},{9,8},{10,11... | collective-permute-start | bytes 208904 | tf_op jit(solution)/shard_map/ppermute | solution.py:153
  10.9 0.0 collective-permute-done.3.received_ref
  10.9 0.3 kept_shares.1
  11.2 2.0 %collective-permute-done.4 = f32[640,128]{1,0:T(8,128)S(1)} collective-permute-done((f32[640,128]{1,0:T(8,128)S(1)}, f32[640,128]{1,0:T(8,128)S(1)}, u32[]{:S(2)}, u32[]{:S(2)}) %collective-permute-start.4) | collective-permute-done | bytes 327712 | tf_op jit(solution)/shard_map/ppermute | solution.py:270
  13.2 2.2 %collective-permute-start.5 = (f32[320,128]{1,0:T(8,128)S(1)}, f32[320,128]{1,0:T(8,128)S(1)}, u32[]{:S(2)}, u32[]{:S(2)}) collective-permute-start(f32[320,128]{1,0:T(8,128)S(1)} %get-tuple-element.76), channel_id=1, source_target_pairs={{0,8},{1,9},{2,10},{3,11},{4,12},{5,13},{6,14},{7,15},{8,0},{9,1},... | collective-permute-start | bytes 491528 | tf_op jit(solution)/shard_map/ppermute | solution.py:270
  15.4 1.3 %collective-permute-done.2 = f32[640,128]{1,0:T(8,128)S(1)} collective-permute-done((f32[640,128]{1,0:T(8,128)S(1)}, f32[640,128]{1,0:T(8,128)S(1)}, u32[]{:S(2)}, u32[]{:S(2)}) %collective-permute-start.2) | collective-permute-done | bytes 327712 | tf_op jit(solution)/shard_map/ppermute | solution.py:270
  16.7 2.1 %collective-permute-start.8 = (f32[320,128]{1,0:T(8,128)S(1)}, f32[320,128]{1,0:T(8,128)S(1)}, u32[]{:S(2)}, u32[]{:S(2)}) collective-permute-start(f32[320,128]{1,0:T(8,128)S(1)} %get-tuple-element.74), channel_id=1, source_target_pairs={{0,4},{1,5},{2,6},{3,7},{4,0},{5,1},{6,2},{7,3},{8,12},{9,13},{10,... | collective-permute-start | bytes 491528 | tf_op jit(solution)/shard_map/ppermute | solution.py:270
  18.8 0.2 collective-permute-done.5
  19.0 1.7 %collective-permute-start.6 = (f32[160,128]{1,0:T(8,128)S(1)}, f32[160,128]{1,0:T(8,128)S(1)}, u32[]{:S(2)}, u32[]{:S(2)}) collective-permute-start(f32[160,128]{1,0:T(8,128)S(1)} %slice_add_fusion.7), channel_id=1, source_target_pairs={{0,4},{1,3},{2,6},{3,1},{4,0},{5,7},{6,2},{7,5},{8,12},{9,11},{10,... | collective-permute-start | bytes 245768 | tf_op jit(solution)/shard_map/ppermute | solution.py:270
  20.8 1.3 %collective-permute-done.8 = f32[320,128]{1,0:T(8,128)S(1)} collective-permute-done((f32[320,128]{1,0:T(8,128)S(1)}, f32[320,128]{1,0:T(8,128)S(1)}, u32[]{:S(2)}, u32[]{:S(2)}) %collective-permute-start.8) | collective-permute-done | bytes 163872 | tf_op jit(solution)/shard_map/ppermute | solution.py:270
  22.1 2.1 %collective-permute-start.9 = (f32[160,128]{1,0:T(8,128)S(1)}, f32[160,128]{1,0:T(8,128)S(1)}, u32[]{:S(2)}, u32[]{:S(2)}) collective-permute-start(f32[160,128]{1,0:T(8,128)S(1)} %slice_add_fusion.4), channel_id=1, source_target_pairs={{0,8},{1,3},{2,10},{3,1},{4,12},{5,7},{6,14},{7,5},{8,0},{9,11},{1... | collective-permute-start | bytes 245768 | tf_op jit(solution)/shard_map/ppermute | solution.py:270
  24.3 0.0 collective-permute-done.7.later_ref
  24.3 0.0 collective-permute-done.6
  24.3 2.4 %collective-permute-done.9 = f32[160,128]{1,0:T(8,128)S(1)} collective-permute-done((f32[160,128]{1,0:T(8,128)S(1)}, f32[160,128]{1,0:T(8,128)S(1)}, u32[]{:S(2)}, u32[]{:S(2)}) %collective-permute-start.9) | collective-permute-done | bytes 81952 | tf_op jit(solution)/shard_map/ppermute | solution.py:270
  26.7 0.7 %collective-permute-start.10 = (f32[320,128]{1,0:T(8,128)S(1)}, f32[320,128]{1,0:T(8,128)S(1)}, u32[]{:S(2)}, u32[]{:S(2)}) collective-permute-start(f32[320,128]{1,0:T(8,128)S(1)} %pad_maximum_fusion.1.near_ref), channel_id=1, source_target_pairs={{1,17},{3,19},{5,21},{7,23},{9,25},{11,27},{13,29},{15,31},{17,1},... | collective-permute-start | bytes 491528 | tf_op jit(solution)/shard_map/ppermute | solution.py:419
  27.4 1.0 %finish.1 = (bf16[1,128,128]{2,1,0:T(8,128)(2,1)}, bf16[1,128,128]{2,1,0:T(8,128)(2,1)}, f32[1,128,128]{2,1,0:T(8,128)}) custom-call(f32[4,128,128]{2,1,0:T(8,128)S(1)} %pad_maximum_fusion.own_ref.packed_ref, f32[128,128]{1,0:T(8,128)S(1)} %get-tuple-element.50.cumul_ref, f32[128,128]{1,0:T(8,128)S(1)} %get-tuple-element.57.grad_key_ref, ...), custom_call_target="tpu_custom_call" | custom-call | flops 671088640 | bytes 724992 | tf_op jit(solution)/shard_map/finish/pallas_call | solution.py:141
  28.4 0.0 collective-permute-done.10.far_ref
  28.5 2.9 %collective-permute-start.11 = (f32[320,128]{1,0:T(8,128)S(1)}, f32[320,128]{1,0:T(8,128)S(1)}, u32[]{:S(2)}, u32[]{:S(2)}) collective-permute-start(f32[320,128]{1,0:T(8,128)S(1)} %pick.1.mine_ref), channel_id=1, source_target_pairs={{0,1},{1,0},{2,3},{3,2},{4,5},{5,4},{6,7},{7,6},{8,9},{9,8},{10,11... | collective-permute-start | bytes 491528 | tf_op jit(solution)/shard_map/ppermute | solution.py:153
  31.4 1.0 %collective-permute-done.11.theirs_ref = f32[320,128]{1,0:T(8,128)S(1)} collective-permute-done((f32[320,128]{1,0:T(8,128)S(1)}, f32[320,128]{1,0:T(8,128)S(1)}, u32[]{:S(2)}, u32[]{:S(2)}) %collective-permute-start.11) | collective-permute-done | bytes 163872 | tf_op jit(solution)/shard_map/ppermute | solution.py:153
  32.4 0.7 %add.55 = f32[320,128]{1,0:T(8,128)} custom-call(f32[320,128]{1,0:T(8,128)S(1)} %pick.1.mine_ref, f32[320,128]{1,0:T(8,128)S(1)} %collective-permute-done.11.theirs_ref), custom_call_target="tpu_custom_call" | custom-call | flops 167772160 | bytes 491520 | tf_op jit(solution)/shard_map/add/pallas_call | solution.py:141
  (11 shorter events, 0.2 us)
Async XLA Ops:
  0.6 0.8 %copy-start.5 = (bf16[1,128,128]{2,1,0:T(8,128)(2,1)S(1)}, bf16[1,128,128]{2,1,0:T(8,128)(2,1)}, u32[]{:S(2)}) copy-start(bf16[1,128,128]{2,1,0:T(8,128)(2,1)} %param.6) | copy-start | bytes 98308
  0.6 0.8 %copy-start.4 = (bf16[1,128,128]{2,1,0:T(8,128)(2,1)S(1)}, bf16[1,128,128]{2,1,0:T(8,128)(2,1)}, u32[]{:S(2)}) copy-start(bf16[1,128,128]{2,1,0:T(8,128)(2,1)} %param.7) | copy-start | bytes 98308
  0.7 0.8 %copy-start.3 = (bf16[1,128,128]{2,1,0:T(8,128)(2,1)S(1)}, bf16[1,128,128]{2,1,0:T(8,128)(2,1)}, u32[]{:S(2)}) copy-start(bf16[1,128,128]{2,1,0:T(8,128)(2,1)} %param.8) | copy-start | bytes 98308
  0.7 0.9 %copy-start.2 = (f32[1,128,128]{2,1,0:T(8,128)S(1)}, f32[1,128,128]{2,1,0:T(8,128)}, u32[]{:S(2)}) copy-start(f32[1,128,128]{2,1,0:T(8,128)} %param.9) | copy-start | bytes 196612
  0.7 1.4 %copy-start = (bf16[1,128,5120]{2,1,0:T(8,128)(2,1)S(1)}, bf16[1,128,5120]{2,1,0:T(8,128)(2,1)}, u32[]{:S(2)}) copy-start(bf16[1,128,5120]{2,1,0:T(8,128)(2,1)} %upstream_ref.3) | copy-start | bytes 3932164
  1.6 1.7 %collective-permute-start.1 = (f32[4,128,128]{2,1,0:T(8,128)S(1)}, f32[4,128,128]{2,1,0:T(8,128)S(1)}, u32[]{:S(2)}, u32[]{:S(2)}) collective-permute-start(f32[4,128,128]{2,1,0:T(8,128)S(1)} %pad_maximum_fusion.own_ref.packed_ref), channel_id=1, source_target_pairs={{0,1},{1,0},{2,3},{3,2},{4,5},{5,4},{6,7},{7,6},{8,9},{9,8},{10,11... | collective-permute-start | bytes 786440 | tf_op jit(solution)/shard_map/ppermute | solution.py:153
  2.6 2.2 %collective-permute-start = (f32[1280,128]{1,0:T(8,128)S(1)}, f32[1280,128]{1,0:T(8,128)S(1)}, u32[]{:S(2)}, u32[]{:S(2)}) collective-permute-start(f32[1280,128]{1,0:T(8,128)S(1)} %get-tuple-element.40), channel_id=1, source_target_pairs={{0,1},{1,0},{2,3},{3,2},{4,5},{5,4},{6,7},{7,6},{8,9},{9,8},{10,11... | collective-permute-start | bytes 1966088 | tf_op jit(solution)/shard_map/ppermute | solution.py:153
  4.0 4.2 %copy-start.1 = (bf16[5120,128]{1,0:T(8,128)(2,1)S(1)}, bf16[5120,128]{1,0:T(8,128)(2,1)}, u32[]{:S(2)}) copy-start(bf16[5120,128]{1,0:T(8,128)(2,1)} %weight_ref.1) | copy-start | bytes 3932164
  4.0 6.9 %collective-permute-start.3 = (f32[1280,128]{1,0:T(8,128)S(1)}, f32[1280,128]{1,0:T(8,128)S(1)}, u32[]{:S(2)}, u32[]{:S(2)}) collective-permute-start(f32[1280,128]{1,0:T(8,128)S(1)} %get-tuple-element.60), channel_id=1, source_target_pairs={{0,1},{1,0},{2,3},{3,2},{4,5},{5,4},{6,7},{7,6},{8,9},{9,8},{10,11... | collective-permute-start | bytes 1966088 | tf_op jit(solution)/shard_map/ppermute | solution.py:153
  5.2 8.0 %collective-permute-start.4 = (f32[640,128]{1,0:T(8,128)S(1)}, f32[640,128]{1,0:T(8,128)S(1)}, u32[]{:S(2)}, u32[]{:S(2)}) collective-permute-start(f32[640,128]{1,0:T(8,128)S(1)} %get-tuple-element.62), channel_id=1, source_target_pairs={{0,2},{1,5},{2,0},{3,7},{4,6},{5,1},{6,4},{7,3},{8,10},{9,13},{10,... | collective-permute-start | bytes 983048 | tf_op jit(solution)/shard_map/ppermute | solution.py:270
  8.1 8.6 %collective-permute-start.2 = (f32[640,128]{1,0:T(8,128)S(1)}, f32[640,128]{1,0:T(8,128)S(1)}, u32[]{:S(2)}, u32[]{:S(2)}) collective-permute-start(f32[640,128]{1,0:T(8,128)S(1)} %get-tuple-element.49), channel_id=1, source_target_pairs={{0,2},{1,9},{2,0},{3,11},{4,6},{5,13},{6,4},{7,15},{8,10},{9,1},{1... | collective-permute-start | bytes 983048 | tf_op jit(solution)/shard_map/ppermute | solution.py:270
  9.8 14.5 %collective-permute-start.7 = (f32[136,128]{1,0:T(8,128)S(1)}, f32[136,128]{1,0:T(8,128)S(1)}, u32[]{:S(2)}, u32[]{:S(2)}) collective-permute-start(f32[136,128]{1,0:T(8,128)S(1)} %get-tuple-element.63), channel_id=1, source_target_pairs={{0,1},{1,0},{2,3},{3,2},{4,5},{5,4},{6,7},{7,6},{8,9},{9,8},{10,11... | collective-permute-start | bytes 208904 | tf_op jit(solution)/shard_map/ppermute | solution.py:153
  13.2 5.8 %collective-permute-start.5 = (f32[320,128]{1,0:T(8,128)S(1)}, f32[320,128]{1,0:T(8,128)S(1)}, u32[]{:S(2)}, u32[]{:S(2)}) collective-permute-start(f32[320,128]{1,0:T(8,128)S(1)} %get-tuple-element.76), channel_id=1, source_target_pairs={{0,8},{1,9},{2,10},{3,11},{4,12},{5,13},{6,14},{7,15},{8,0},{9,1},... | collective-permute-start | bytes 491528 | tf_op jit(solution)/shard_map/ppermute | solution.py:270
  16.7 5.4 %collective-permute-start.8 = (f32[320,128]{1,0:T(8,128)S(1)}, f32[320,128]{1,0:T(8,128)S(1)}, u32[]{:S(2)}, u32[]{:S(2)}) collective-permute-start(f32[320,128]{1,0:T(8,128)S(1)} %get-tuple-element.74), channel_id=1, source_target_pairs={{0,4},{1,5},{2,6},{3,7},{4,0},{5,1},{6,2},{7,3},{8,12},{9,13},{10,... | collective-permute-start | bytes 491528 | tf_op jit(solution)/shard_map/ppermute | solution.py:270
  19.0 5.2 %collective-permute-start.6 = (f32[160,128]{1,0:T(8,128)S(1)}, f32[160,128]{1,0:T(8,128)S(1)}, u32[]{:S(2)}, u32[]{:S(2)}) collective-permute-start(f32[160,128]{1,0:T(8,128)S(1)} %slice_add_fusion.7), channel_id=1, source_target_pairs={{0,4},{1,3},{2,6},{3,1},{4,0},{5,7},{6,2},{7,5},{8,12},{9,11},{10,... | collective-permute-start | bytes 245768 | tf_op jit(solution)/shard_map/ppermute | solution.py:270
  22.1 4.6 %collective-permute-start.9 = (f32[160,128]{1,0:T(8,128)S(1)}, f32[160,128]{1,0:T(8,128)S(1)}, u32[]{:S(2)}, u32[]{:S(2)}) collective-permute-start(f32[160,128]{1,0:T(8,128)S(1)} %slice_add_fusion.4), channel_id=1, source_target_pairs={{0,8},{1,3},{2,10},{3,1},{4,12},{5,7},{6,14},{7,5},{8,0},{9,11},{1... | collective-permute-start | bytes 245768 | tf_op jit(solution)/shard_map/ppermute | solution.py:270
  26.7 1.7 %collective-permute-start.10 = (f32[320,128]{1,0:T(8,128)S(1)}, f32[320,128]{1,0:T(8,128)S(1)}, u32[]{:S(2)}, u32[]{:S(2)}) collective-permute-start(f32[320,128]{1,0:T(8,128)S(1)} %pad_maximum_fusion.1.near_ref), channel_id=1, source_target_pairs={{1,17},{3,19},{5,21},{7,23},{9,25},{11,27},{13,29},{15,31},{17,1},... | collective-permute-start | bytes 491528 | tf_op jit(solution)/shard_map/ppermute | solution.py:419
  28.5 4.0 %collective-permute-start.11 = (f32[320,128]{1,0:T(8,128)S(1)}, f32[320,128]{1,0:T(8,128)S(1)}, u32[]{:S(2)}, u32[]{:S(2)}) collective-permute-start(f32[320,128]{1,0:T(8,128)S(1)} %pick.1.mine_ref), channel_id=1, source_target_pairs={{0,1},{1,0},{2,3},{3,2},{4,5},{5,4},{6,7},{7,6},{8,9},{9,8},{10,11... | collective-permute-start | bytes 491528 | tf_op jit(solution)/shard_map/ppermute | solution.py:153

commit v8 on v6

--- a/solution.py
+++ b/solution.py
@@ -172,29 +172,43 @@
     lower_ref[...] = lower_mask(lower_ref.shape[0]).astype(F32).astype(BF16)
 
 
-def turn_kernel(count, plan, upstream_ref, own_ref, first_ref, second_ref, turned):
+def rows_of(count, plan, me, core, part, share):
+    half = share // 2
+    offset = 0
+    for rows, orders in plan:
+        for place in part:
+            masks = [relative(place, order) for order in orders]
+            owner = me ^ (masks[0] + core * (masks[1] - masks[0]))
+            yield pl.multiple_of(owner * share + core * half + offset, 16), rows
+        offset += rows
+
+
+def turn_kernel(count, plan, upstream_ref, turned_ref, first_ref):
     me, core = lax.axis_index("dp"), lax.axis_index("ctx")
-    model = turned.shape[0]
+    model = turned_ref.shape[0]
     lanes = 128
     for start in range(0, model, lanes):
-        turned[start:start + lanes] = jnp.transpose(upstream_ref[0, :, start:start + lanes].astype(F32))
-    share = model // count
-    half = share // 2
+        turned_ref[start:start + lanes] = jnp.transpose(
+            upstream_ref[0, :, start:start + lanes].astype(F32)
+        )
     at = 0
-    for ref, places in ((first_ref, range(count // 2, count)), (second_ref, range(count // 2))):
-        offset = sent = 0
-        for rows, orders in plan:
-            for place in places:
-                masks = [relative(place, order) for order in orders]
-                mine = me ^ (masks[0] + core * (masks[1] - masks[0]))
-                other = me ^ (masks[1] + core * (masks[0] - masks[1]))
-                begin = pl.multiple_of(mine * share + core * half + offset, 16)
-                own_ref[at:at + rows] = turned[pl.ds(begin, rows)].astype(BF16)
-                begin = pl.multiple_of(other * share + (1 - core) * half + offset, 16)
-                ref[sent:sent + rows] = turned[pl.ds(begin, rows)]
-                at += rows
-                sent += rows
-            offset += rows
+    for begin, rows in rows_of(count, plan, me, 1 - core, range(count // 2, count), model // count):
+        first_ref[at:at + rows] = turned_ref[pl.ds(begin, rows)]
+        at += rows
+
+
+def rest_kernel(count, plan, turned_ref, own_ref, second_ref):
+    me, core = lax.axis_index("dp"), lax.axis_index("ctx")
+    share = turned_ref.shape[0] // count
+    at = 0
+    for part in (range(count // 2, count), range(count // 2)):
+        for begin, rows in rows_of(count, plan, me, core, part, share):
+            own_ref[at:at + rows] = turned_ref[pl.ds(begin, rows)].astype(BF16)
+            at += rows
+    at = 0
+    for begin, rows in rows_of(count, plan, me, 1 - core, range(count // 2), share):
+        second_ref[at:at + rows] = turned_ref[pl.ds(begin, rows)]
+        at += rows
 
 
 def joined(pairs, left_axis, right_axis):
@@ -329,12 +343,17 @@
     if paired:
         plan = halving_plan(count, rows)
         part_rows = rows * count // 2
-        own, send_first, send_second = local_call(
+        turned, send_first = local_call(
             functools.partial(turn_kernel, count, plan),
-            [((2 * part_rows, length), BF16), ((part_rows, length), F32), ((part_rows, length), F32)],
+            [((model, length), F32), ((part_rows, length), F32)],
             cotangent,
             name="turn", flops=20 * flops,
-            scratch=[pltpu.VMEM((model, length), F32)],
+        )
+        own, send_second = local_call(
+            functools.partial(rest_kernel, count, plan),
+            [((2 * part_rows, length), BF16), ((part_rows, length), F32)],
+            turned,
+            name="rest", flops=flops,
         )
         others = swap(packed)
         received_first = swap(send_first)
@@ -406,7 +425,7 @@
 
         def beside_first(arrived):
             large, small = arrived
-            small, held["query"] = lax.optimization_barrier((small, grad_query))
+            large, held["query"] = lax.optimization_barrier((large, grad_query))
             return [large, small]
 
         def beside_third(arrived):

time: 32.9 us -> 32.8 us (level)
    pallas_call x8 -> x9, Pallas kernels: 5.25 us -> 5.24 us  [local_call(): pl.pallas_call(kernel, out_shape=outs, in_specs=[pl.BlockSpec(memory_spac...]
where the time goes in v8:
time: 32.8 us; the launch traced here: 32.7 us
  starting transfers between devices  16.1 us (49%)
  waiting for transfers between devices  9.56 us (29%)
  Pallas kernels  5.24 us (16%)
  local copies, waits for them, and re-layouts  0.83 us (3%)
  between operations  0.77 us (2%)
    ppermute x7, starting transfers between devices, exchanged(): return lax.ppermute(value, BOTH, pairs)  14.6 us
    ppermute x7, waiting for transfers between devices, exchanged(): return lax.ppermute(value, BOTH, pairs)  7.88 us
    pallas_call x9, Pallas kernels, local_call(): pl.pallas_call(kernel, out_shape=outs, in_specs=[pl.BlockSpec(memory_spac...  5.24 us
    ppermute x5, waiting for transfers between devices, swap(): return lax.ppermute(value, 'ctx', [(0, 1), (1, 0)])  1.68 us
    ppermute x5, starting transfers between devices, swap(): return lax.ppermute(value, 'ctx', [(0, 1), (1, 0)])  1.52 us
    unnamed x12, local copies, waits for them, and re-layouts  0.83 us
  transfers between devices with their start and end apart: 12, of which 8 were waited for; matrix products, arithmetic and copies ran while one was open for 0% of the time, Pallas kernels for 14%

profile of v8, /device:TPU:0, one launch (start us, length us, event | category | flops | bytes accessed | tf_op | source)
XLA Modules:
  0.0 32.7 jit_solution(8629102135652075448)
XLA Ops:
  0.6 0.0 copy-start.5
  0.6 0.0 copy-start.4
  0.7 0.0 copy-start.3
  0.7 0.0 copy-start.2
  0.7 0.0 copy-start
  0.7 0.7 %copy-done.5 = bf16[1,128,128]{2,1,0:T(8,128)(2,1)S(1)} copy-done((bf16[1,128,128]{2,1,0:T(8,128)(2,1)S(1)}, bf16[1,128,128]{2,1,0:T(8,128)(2,1)}, u32[]{:S(2)}) %copy-start.5) | copy-done | bytes 32792
  1.4 0.0 copy-done.4
  1.4 0.0 copy-done.3
  1.4 0.1 copy-done.2
  1.6 0.5 %collective-permute-start.1 = (f32[4,128,128]{2,1,0:T(8,128)S(1)}, f32[4,128,128]{2,1,0:T(8,128)S(1)}, u32[]{:S(2)}, u32[]{:S(2)}) collective-permute-start(f32[4,128,128]{2,1,0:T(8,128)S(1)} %pad_maximum_fusion.own_ref.packed_ref), channel_id=1, source_target_pairs={{0,1},{1,0},{2,3},{3,2},{4,5},{5,4},{6,7},{7,6},{8,9},{9,8},{10,11... | collective-permute-start | bytes 786440 | tf_op jit(solution)/shard_map/ppermute | solution.py:153
  2.1 0.0 copy-done
  2.1 0.4 %turn.1 = (f32[5120,128]{1,0:T(8,128)S(1)}, f32[1280,128]{1,0:T(8,128)S(1)}) custom-call(bf16[1,128,5120]{2,1,0:T(8,128)(2,1)S(1)} %copy-done), custom_call_target="tpu_custom_call" | custom-call | flops 13421772800 | bytes 4587520 | tf_op jit(solution)/shard_map/turn/pallas_call | solution.py:141
  2.5 0.5 %collective-permute-start = (f32[1280,128]{1,0:T(8,128)S(1)}, f32[1280,128]{1,0:T(8,128)S(1)}, u32[]{:S(2)}, u32[]{:S(2)}) collective-permute-start(f32[1280,128]{1,0:T(8,128)S(1)} %get-tuple-element.42), channel_id=1, source_target_pairs={{0,1},{1,0},{2,3},{3,2},{4,5},{5,4},{6,7},{7,6},{8,9},{9,8},{10,11... | collective-permute-start | bytes 1966088 | tf_op jit(solution)/shard_map/ppermute | solution.py:153
  3.0 0.1 rest.1
  3.1 0.1 collective-permute-done.1.other_ref
  3.2 0.7 %joint.1 = (f32[128,128]{1,0:T(8,128)S(1)}, f32[128,128]{1,0:T(8,128)S(1)}, f32[128,128]{1,0:T(8,128)S(1)}, f32[128,128]{1,0:T(8,128)S(1)}, f32[128,128]{1,0:T(8,128)S(1)}, /*index=5*/bf16[256,128]{1,0:T(8,128)(2,1)S(1)}) custom-call(f32[4,128,128]{2,1,0:T(8,128)S(1)} %pad_maximum_fusion.own_ref.packed_ref, ...), custom_call_target="tpu_custom_call" | custom-call | flops 26843545600 | bytes 950272 | tf_op jit(solution)/shard_map/joint/pallas_call | solution.py:141
  4.0 0.0 copy-start.1
  4.0 0.4 %collective-permute-start.3 = (f32[1280,128]{1,0:T(8,128)S(1)}, f32[1280,128]{1,0:T(8,128)S(1)}, u32[]{:S(2)}, u32[]{:S(2)}) collective-permute-start(f32[1280,128]{1,0:T(8,128)S(1)} %get-tuple-element.62), channel_id=1, source_target_pairs={{0,1},{1,0},{2,3},{3,2},{4,5},{5,4},{6,7},{7,6},{8,9},{9,8},{10,11... | collective-permute-start | bytes 1966088 | tf_op jit(solution)/shard_map/ppermute | solution.py:153
  4.4 0.3 collective-permute-done.received_ref
  4.7 0.3 sent_shares.1
  5.1 2.9 %collective-permute-start.2 = (f32[640,128]{1,0:T(8,128)S(1)}, f32[640,128]{1,0:T(8,128)S(1)}, u32[]{:S(2)}, u32[]{:S(2)}) collective-permute-start(f32[640,128]{1,0:T(8,128)S(1)} %get-tuple-element.51), channel_id=1, source_target_pairs={{0,2},{1,5},{2,0},{3,7},{4,6},{5,1},{6,4},{7,3},{8,10},{9,13},{10,... | collective-permute-start | bytes 983048 | tf_op jit(solution)/shard_map/ppermute | solution.py:285
  8.0 1.6 %collective-permute-start.7 = (f32[640,128]{1,0:T(8,128)S(1)}, f32[640,128]{1,0:T(8,128)S(1)}, u32[]{:S(2)}, u32[]{:S(2)}) collective-permute-start(f32[640,128]{1,0:T(8,128)S(1)} %get-tuple-element.71), channel_id=1, source_target_pairs={{0,8},{1,5},{2,10},{3,7},{4,12},{5,1},{6,14},{7,3},{8,0},{9,13},{1... | collective-permute-start | bytes 983048 | tf_op jit(solution)/shard_map/ppermute | solution.py:285
  9.6 0.0 copy-done.1
  9.6 1.6 %grads.1 = (bf16[1,128,128]{2,1,0:T(8,128)(2,1)}, f32[128,128]{1,0:T(8,128)S(1)}, f32[128,128]{1,0:T(8,128)S(1)}, f32[128,128]{1,0:T(8,128)S(1)}, f32[136,128]{1,0:T(8,128)S(1)}) custom-call(f32[4,128,128]{2,1,0:T(8,128)S(1)} %pad_maximum_fusion.own_ref.packed_ref, f32[128,128]{1,0:T(8,128)S(1)} %get-tuple-element.52.cumul_ref, ...), custom_call_target="tpu_custom_call" | custom-call | flops 1342177280 | bytes 3510272 | tf_op jit(solution)/shard_map/grads/pallas_call | solution.py:141
  11.2 0.0 collective-permute-start.6
  11.2 0.0 collective-permute-done.3.received_ref
  11.2 0.3 kept_shares.1
  11.5 1.5 %collective-permute-done.2 = f32[640,128]{1,0:T(8,128)S(1)} collective-permute-done((f32[640,128]{1,0:T(8,128)S(1)}, f32[640,128]{1,0:T(8,128)S(1)}, u32[]{:S(2)}, u32[]{:S(2)}) %collective-permute-start.2) | collective-permute-done | bytes 327712 | tf_op jit(solution)/shard_map/ppermute | solution.py:285
  13.1 0.1 slice_add_fusion.3
  13.1 2.1 %collective-permute-start.4 = (f32[320,128]{1,0:T(8,128)S(1)}, f32[320,128]{1,0:T(8,128)S(1)}, u32[]{:S(2)}, u32[]{:S(2)}) collective-permute-start(f32[320,128]{1,0:T(8,128)S(1)} %get-tuple-element.78), channel_id=1, source_target_pairs={{0,4},{1,3},{2,6},{3,1},{4,0},{5,7},{6,2},{7,5},{8,12},{9,11},{10,... | collective-permute-start | bytes 491528 | tf_op jit(solution)/shard_map/ppermute | solution.py:285
  15.2 0.0 collective-permute-done.7
  15.2 0.1 slice_add_fusion.1
  15.3 1.6 %collective-permute-start.8 = (f32[320,128]{1,0:T(8,128)S(1)}, f32[320,128]{1,0:T(8,128)S(1)}, u32[]{:S(2)}, u32[]{:S(2)}) collective-permute-start(f32[320,128]{1,0:T(8,128)S(1)} %get-tuple-element.76), channel_id=1, source_target_pairs={{0,2},{1,9},{2,0},{3,11},{4,6},{5,13},{6,4},{7,15},{8,10},{9,1},{1... | collective-permute-start | bytes 491528 | tf_op jit(solution)/shard_map/ppermute | solution.py:285
  16.8 1.7 %collective-permute-done.4 = f32[320,128]{1,0:T(8,128)S(1)} collective-permute-done((f32[320,128]{1,0:T(8,128)S(1)}, f32[320,128]{1,0:T(8,128)S(1)}, u32[]{:S(2)}, u32[]{:S(2)}) %collective-permute-start.4) | collective-permute-done | bytes 163872 | tf_op jit(solution)/shard_map/ppermute | solution.py:285
  18.5 2.1 %collective-permute-start.5 = (f32[160,128]{1,0:T(8,128)S(1)}, f32[160,128]{1,0:T(8,128)S(1)}, u32[]{:S(2)}, u32[]{:S(2)}) collective-permute-start(f32[160,128]{1,0:T(8,128)S(1)} %get-tuple-element.80), channel_id=1, source_target_pairs={{0,8},{1,9},{2,10},{3,11},{4,12},{5,13},{6,14},{7,15},{8,0},{9,1},... | collective-permute-start | bytes 245768 | tf_op jit(solution)/shard_map/ppermute | solution.py:285
  20.7 0.0 collective-permute-done.8
  20.7 1.6 %collective-permute-start.9 = (f32[160,128]{1,0:T(8,128)S(1)}, f32[160,128]{1,0:T(8,128)S(1)}, u32[]{:S(2)}, u32[]{:S(2)}) collective-permute-start(f32[160,128]{1,0:T(8,128)S(1)} %get-tuple-element.82), channel_id=1, source_target_pairs={{0,4},{1,3},{2,6},{3,1},{4,0},{5,7},{6,2},{7,5},{8,12},{9,11},{10,... | collective-permute-start | bytes 245768 | tf_op jit(solution)/shard_map/ppermute | solution.py:285
  22.3 0.0 collective-permute-done.6.later_ref
  22.3 0.8 %collective-permute-done.5 = f32[160,128]{1,0:T(8,128)S(1)} collective-permute-done((f32[160,128]{1,0:T(8,128)S(1)}, f32[160,128]{1,0:T(8,128)S(1)}, u32[]{:S(2)}, u32[]{:S(2)}) %collective-permute-start.5) | collective-permute-done | bytes 81952 | tf_op jit(solution)/shard_map/ppermute | solution.py:285
  23.1 2.1 %collective-permute-done.9 = f32[160,128]{1,0:T(8,128)S(1)} collective-permute-done((f32[160,128]{1,0:T(8,128)S(1)}, f32[160,128]{1,0:T(8,128)S(1)}, u32[]{:S(2)}, u32[]{:S(2)}) %collective-permute-start.9) | collective-permute-done | bytes 81952 | tf_op jit(solution)/shard_map/ppermute | solution.py:285
  25.2 2.7 %collective-permute-start.10 = (f32[160,128]{1,0:T(8,128)S(1)}, f32[160,128]{1,0:T(8,128)S(1)}, u32[]{:S(2)}, u32[]{:S(2)}) collective-permute-start(f32[160,128]{1,0:T(8,128)S(1)} %pad_maximum_fusion.1), channel_id=1, source_target_pairs={{0,16},{1,17},{2,18},{3,19},{4,20},{5,21},{6,22},{7,23},{8,24},{9,... | collective-permute-start | bytes 245768 | tf_op jit(solution)/shard_map/ppermute | solution.py:285
  27.9 1.0 %finish.1 = (bf16[1,128,128]{2,1,0:T(8,128)(2,1)}, bf16[1,128,128]{2,1,0:T(8,128)(2,1)}, f32[1,128,128]{2,1,0:T(8,128)}) custom-call(f32[4,128,128]{2,1,0:T(8,128)S(1)} %pad_maximum_fusion.own_ref.packed_ref, f32[128,128]{1,0:T(8,128)S(1)} %get-tuple-element.52.cumul_ref, f32[128,128]{1,0:T(8,128)S(1)} %get-tuple-element.59.grad_key_ref, ...), custom_call_target="tpu_custom_call" | custom-call | flops 671088640 | bytes 724992 | tf_op jit(solution)/shard_map/finish/pallas_call | solution.py:141
  28.9 1.7 %collective-permute-done.10 = f32[160,128]{1,0:T(8,128)S(1)} collective-permute-done((f32[160,128]{1,0:T(8,128)S(1)}, f32[160,128]{1,0:T(8,128)S(1)}, u32[]{:S(2)}, u32[]{:S(2)}) %collective-permute-start.10) | collective-permute-done | bytes 81952 | tf_op jit(solution)/shard_map/ppermute | solution.py:285
  30.7 0.1 collective-permute-start.11
  30.7 1.3 %collective-permute-done.11.theirs_ref = f32[160,128]{1,0:T(8,128)S(1)} collective-permute-done((f32[160,128]{1,0:T(8,128)S(1)}, f32[160,128]{1,0:T(8,128)S(1)}, u32[]{:S(2)}, u32[]{:S(2)}) %collective-permute-start.11) | collective-permute-done | bytes 81952 | tf_op jit(solution)/shard_map/ppermute | solution.py:153
  32.0 0.7 %assemble.1 = f32[320,128]{1,0:T(8,128)} custom-call(f32[160,128]{1,0:T(8,128)S(1)} %pad_maximum_fusion.2.mine_ref, f32[160,128]{1,0:T(8,128)S(1)} %collective-permute-done.11.theirs_ref), custom_call_target="tpu_custom_call" | custom-call | flops 167772160 | bytes 327680 | tf_op jit(solution)/shard_map/assemble/pallas_call | solution.py:141
  (10 shorter events, 0.1 us)
Async XLA Ops:
  0.6 0.8 %copy-start.5 = (bf16[1,128,128]{2,1,0:T(8,128)(2,1)S(1)}, bf16[1,128,128]{2,1,0:T(8,128)(2,1)}, u32[]{:S(2)}) copy-start(bf16[1,128,128]{2,1,0:T(8,128)(2,1)} %param.6) | copy-start | bytes 98308
  0.6 0.8 %copy-start.4 = (bf16[1,128,128]{2,1,0:T(8,128)(2,1)S(1)}, bf16[1,128,128]{2,1,0:T(8,128)(2,1)}, u32[]{:S(2)}) copy-start(bf16[1,128,128]{2,1,0:T(8,128)(2,1)} %param.7) | copy-start | bytes 98308
  0.7 0.8 %copy-start.3 = (bf16[1,128,128]{2,1,0:T(8,128)(2,1)S(1)}, bf16[1,128,128]{2,1,0:T(8,128)(2,1)}, u32[]{:S(2)}) copy-start(bf16[1,128,128]{2,1,0:T(8,128)(2,1)} %param.8) | copy-start | bytes 98308
  0.7 0.9 %copy-start.2 = (f32[1,128,128]{2,1,0:T(8,128)S(1)}, f32[1,128,128]{2,1,0:T(8,128)}, u32[]{:S(2)}) copy-start(f32[1,128,128]{2,1,0:T(8,128)} %param.9) | copy-start | bytes 196612
  0.7 1.4 %copy-start = (bf16[1,128,5120]{2,1,0:T(8,128)(2,1)S(1)}, bf16[1,128,5120]{2,1,0:T(8,128)(2,1)}, u32[]{:S(2)}) copy-start(bf16[1,128,5120]{2,1,0:T(8,128)(2,1)} %upstream_ref.3) | copy-start | bytes 3932164
  1.6 1.7 %collective-permute-start.1 = (f32[4,128,128]{2,1,0:T(8,128)S(1)}, f32[4,128,128]{2,1,0:T(8,128)S(1)}, u32[]{:S(2)}, u32[]{:S(2)}) collective-permute-start(f32[4,128,128]{2,1,0:T(8,128)S(1)} %pad_maximum_fusion.own_ref.packed_ref), channel_id=1, source_target_pairs={{0,1},{1,0},{2,3},{3,2},{4,5},{5,4},{6,7},{7,6},{8,9},{9,8},{10,11... | collective-permute-start | bytes 786440 | tf_op jit(solution)/shard_map/ppermute | solution.py:153
  2.5 2.2 %collective-permute-start = (f32[1280,128]{1,0:T(8,128)S(1)}, f32[1280,128]{1,0:T(8,128)S(1)}, u32[]{:S(2)}, u32[]{:S(2)}) collective-permute-start(f32[1280,128]{1,0:T(8,128)S(1)} %get-tuple-element.42), channel_id=1, source_target_pairs={{0,1},{1,0},{2,3},{3,2},{4,5},{5,4},{6,7},{7,6},{8,9},{9,8},{10,11... | collective-permute-start | bytes 1966088 | tf_op jit(solution)/shard_map/ppermute | solution.py:153
  4.0 5.6 %copy-start.1 = (bf16[5120,128]{1,0:T(8,128)(2,1)S(1)}, bf16[5120,128]{1,0:T(8,128)(2,1)}, u32[]{:S(2)}) copy-start(bf16[5120,128]{1,0:T(8,128)(2,1)} %weight_ref.1) | copy-start | bytes 3932164
  4.0 7.2 %collective-permute-start.3 = (f32[1280,128]{1,0:T(8,128)S(1)}, f32[1280,128]{1,0:T(8,128)S(1)}, u32[]{:S(2)}, u32[]{:S(2)}) collective-permute-start(f32[1280,128]{1,0:T(8,128)S(1)} %get-tuple-element.62), channel_id=1, source_target_pairs={{0,1},{1,0},{2,3},{3,2},{4,5},{5,4},{6,7},{7,6},{8,9},{9,8},{10,11... | collective-permute-start | bytes 1966088 | tf_op jit(solution)/shard_map/ppermute | solution.py:153
  5.1 8.0 %collective-permute-start.2 = (f32[640,128]{1,0:T(8,128)S(1)}, f32[640,128]{1,0:T(8,128)S(1)}, u32[]{:S(2)}, u32[]{:S(2)}) collective-permute-start(f32[640,128]{1,0:T(8,128)S(1)} %get-tuple-element.51), channel_id=1, source_target_pairs={{0,2},{1,5},{2,0},{3,7},{4,6},{5,1},{6,4},{7,3},{8,10},{9,13},{10,... | collective-permute-start | bytes 983048 | tf_op jit(solution)/shard_map/ppermute | solution.py:285
  8.0 7.2 %collective-permute-start.7 = (f32[640,128]{1,0:T(8,128)S(1)}, f32[640,128]{1,0:T(8,128)S(1)}, u32[]{:S(2)}, u32[]{:S(2)}) collective-permute-start(f32[640,128]{1,0:T(8,128)S(1)} %get-tuple-element.71), channel_id=1, source_target_pairs={{0,8},{1,5},{2,10},{3,7},{4,12},{5,1},{6,14},{7,3},{8,0},{9,13},{1... | collective-permute-start | bytes 983048 | tf_op jit(solution)/shard_map/ppermute | solution.py:285
  11.2 11.1 %collective-permute-start.6 = (f32[136,128]{1,0:T(8,128)S(1)}, f32[136,128]{1,0:T(8,128)S(1)}, u32[]{:S(2)}, u32[]{:S(2)}) collective-permute-start(f32[136,128]{1,0:T(8,128)S(1)} %get-tuple-element.65), channel_id=1, source_target_pairs={{0,1},{1,0},{2,3},{3,2},{4,5},{5,4},{6,7},{7,6},{8,9},{9,8},{10,11... | collective-permute-start | bytes 208904 | tf_op jit(solution)/shard_map/ppermute | solution.py:153
  13.1 5.4 %collective-permute-start.4 = (f32[320,128]{1,0:T(8,128)S(1)}, f32[320,128]{1,0:T(8,128)S(1)}, u32[]{:S(2)}, u32[]{:S(2)}) collective-permute-start(f32[320,128]{1,0:T(8,128)S(1)} %get-tuple-element.78), channel_id=1, source_target_pairs={{0,4},{1,3},{2,6},{3,1},{4,0},{5,7},{6,2},{7,5},{8,12},{9,11},{10,... | collective-permute-start | bytes 491528 | tf_op jit(solution)/shard_map/ppermute | solution.py:285
  15.3 5.4 %collective-permute-start.8 = (f32[320,128]{1,0:T(8,128)S(1)}, f32[320,128]{1,0:T(8,128)S(1)}, u32[]{:S(2)}, u32[]{:S(2)}) collective-permute-start(f32[320,128]{1,0:T(8,128)S(1)} %get-tuple-element.76), channel_id=1, source_target_pairs={{0,2},{1,9},{2,0},{3,11},{4,6},{5,13},{6,4},{7,15},{8,10},{9,1},{1... | collective-permute-start | bytes 491528 | tf_op jit(solution)/shard_map/ppermute | solution.py:285
  18.5 4.6 %collective-permute-start.5 = (f32[160,128]{1,0:T(8,128)S(1)}, f32[160,128]{1,0:T(8,128)S(1)}, u32[]{:S(2)}, u32[]{:S(2)}) collective-permute-start(f32[160,128]{1,0:T(8,128)S(1)} %get-tuple-element.80), channel_id=1, source_target_pairs={{0,8},{1,9},{2,10},{3,11},{4,12},{5,13},{6,14},{7,15},{8,0},{9,1},... | collective-permute-start | bytes 245768 | tf_op jit(solution)/shard_map/ppermute | solution.py:285
  20.7 4.5 %collective-permute-start.9 = (f32[160,128]{1,0:T(8,128)S(1)}, f32[160,128]{1,0:T(8,128)S(1)}, u32[]{:S(2)}, u32[]{:S(2)}) collective-permute-start(f32[160,128]{1,0:T(8,128)S(1)} %get-tuple-element.82), channel_id=1, source_target_pairs={{0,4},{1,3},{2,6},{3,1},{4,0},{5,7},{6,2},{7,5},{8,12},{9,11},{10,... | collective-permute-start | bytes 245768 | tf_op jit(solution)/shard_map/ppermute | solution.py:285
  25.2 5.4 %collective-permute-start.10 = (f32[160,128]{1,0:T(8,128)S(1)}, f32[160,128]{1,0:T(8,128)S(1)}, u32[]{:S(2)}, u32[]{:S(2)}) collective-permute-start(f32[160,128]{1,0:T(8,128)S(1)} %pad_maximum_fusion.1), channel_id=1, source_target_pairs={{0,16},{1,17},{2,18},{3,19},{4,20},{5,21},{6,22},{7,23},{8,24},{9,... | collective-permute-start | bytes 245768 | tf_op jit(solution)/shard_map/ppermute | solution.py:285
  30.7 1.3 %collective-permute-start.11 = (f32[160,128]{1,0:T(8,128)S(1)}, f32[160,128]{1,0:T(8,128)S(1)}, u32[]{:S(2)}, u32[]{:S(2)}) collective-permute-start(f32[160,128]{1,0:T(8,128)S(1)} %pad_maximum_fusion.2.mine_ref), channel_id=1, source_target_pairs={{0,1},{1,0},{2,3},{3,2},{4,5},{5,4},{6,7},{7,6},{8,9},{9,8},{10,11... | collective-permute-start | bytes 245768 | tf_op jit(solution)/shard_map/ppermute | solution.py:153

commit v9 on v8

--- a/solution.py
+++ b/solution.py
@@ -273,6 +273,27 @@
             [own_ref[begin + at:begin + at + rows], received_ref[at:at + rows].astype(BF16)], axis=1
         )
         out[...] = jnp.dot(left, rounded_ref[...], preferred_element_type=F32)
+        at += rows
+
+
+def own_part_kernel(own_ref, rounded_ref, *outs):
+    at = 0
+    for out in outs:
+        rows = out.shape[0]
+        out[...] = jnp.dot(
+            own_ref[at:at + rows], rounded_ref[: rounded_ref.shape[0] // 2], preferred_element_type=F32
+        )
+        at += rows
+
+
+def add_part_kernel(received_ref, rounded_ref, *refs):
+    at = 0
+    for part, out in zip(refs[: len(refs) // 2], refs[len(refs) // 2:]):
+        rows = out.shape[0]
+        out[...] = part[...] + jnp.dot(
+            received_ref[at:at + rows].astype(BF16), rounded_ref[rounded_ref.shape[0] // 2:],
+            preferred_element_type=F32,
+        )
         at += rows
 
 
@@ -368,10 +389,12 @@
         )
         rounded, send_second = lax.optimization_barrier((rounded, send_second))
         received_second = swap(send_second)
+        part_shapes = [((count // 2 * part, width), F32) for part, _ in plan]
+        own_part = local_call(
+            own_part_kernel, part_shapes, own, rounded, name="own_part", flops=flops // 4
+        )
         sent = local_call(
-            functools.partial(share_kernel, 0),
-            [((count // 2 * part, width), F32) for part, _ in plan],
-            own, received_first, rounded,
+            add_part_kernel, part_shapes, received_first, rounded, *own_part,
             name="sent_shares", flops=flops // 4,
         )
         kept = local_call(

time: 32.8 us -> 32.7 us (level)
    pallas_call x9 -> x10, Pallas kernels: 5.24 us -> 5.37 us  [local_call(): pl.pallas_call(kernel, out_shape=outs, in_specs=[pl.BlockSpec(memory_spac...]
where the time goes in v9:
time: 32.7 us; the launch traced here: 32.6 us
  starting transfers between devices  16.1 us (49%)
  waiting for transfers between devices  9.34 us (29%)
  Pallas kernels  5.37 us (16%)
  local copies, waits for them, and re-layouts  0.83 us (3%)
  between operations  0.79 us (2%)
    ppermute x7, starting transfers between devices, exchanged(): return lax.ppermute(value, BOTH, pairs)  14.6 us
    ppermute x7, waiting for transfers between devices, exchanged(): return lax.ppermute(value, BOTH, pairs)  7.89 us
    pallas_call x10, Pallas kernels, local_call(): pl.pallas_call(kernel, out_shape=outs, in_specs=[pl.BlockSpec(memory_spac...  5.37 us
    ppermute x5, starting transfers between devices, swap(): return lax.ppermute(value, 'ctx', [(0, 1), (1, 0)])  1.52 us
    ppermute x5, waiting for transfers between devices, swap(): return lax.ppermute(value, 'ctx', [(0, 1), (1, 0)])  1.45 us
    unnamed x12, local copies, waits for them, and re-layouts  0.83 us
  transfers between devices with their start and end apart: 12, of which 8 were waited for; matrix products, arithmetic and copies ran while one was open for 0% of the time, Pallas kernels for 14%

profile of v9, /device:TPU:0, one launch (start us, length us, event | category | flops | bytes accessed | tf_op | source)
XLA Modules:
  0.0 32.6 jit_solution(5636856939151196071)
XLA Ops:
  0.6 0.0 copy-start.5
  0.6 0.0 copy-start.4
  0.7 0.0 copy-start.3
  0.7 0.0 copy-start.2
  0.7 0.0 copy-start
  0.7 0.7 %copy-done.5 = bf16[1,128,128]{2,1,0:T(8,128)(2,1)S(1)} copy-done((bf16[1,128,128]{2,1,0:T(8,128)(2,1)S(1)}, bf16[1,128,128]{2,1,0:T(8,128)(2,1)}, u32[]{:S(2)}) %copy-start.5) | copy-done | bytes 32792
  1.4 0.0 copy-done.4
  1.4 0.0 copy-done.3
  1.4 0.1 copy-done.2
  1.6 0.5 %collective-permute-start.1 = (f32[4,128,128]{2,1,0:T(8,128)S(1)}, f32[4,128,128]{2,1,0:T(8,128)S(1)}, u32[]{:S(2)}, u32[]{:S(2)}) collective-permute-start(f32[4,128,128]{2,1,0:T(8,128)S(1)} %pad_maximum_fusion.own_ref.packed_ref), channel_id=1, source_target_pairs={{0,1},{1,0},{2,3},{3,2},{4,5},{5,4},{6,7},{7,6},{8,9},{9,8},{10,11... | collective-permute-start | bytes 786440 | tf_op jit(solution)/shard_map/ppermute | solution.py:153
  2.1 0.0 copy-done
  2.1 0.4 %turn.1 = (f32[5120,128]{1,0:T(8,128)S(1)}, f32[1280,128]{1,0:T(8,128)S(1)}) custom-call(bf16[1,128,5120]{2,1,0:T(8,128)(2,1)S(1)} %copy-done), custom_call_target="tpu_custom_call" | custom-call | flops 13421772800 | bytes 4587520 | tf_op jit(solution)/shard_map/turn/pallas_call | solution.py:141
  2.5 0.5 %collective-permute-start = (f32[1280,128]{1,0:T(8,128)S(1)}, f32[1280,128]{1,0:T(8,128)S(1)}, u32[]{:S(2)}, u32[]{:S(2)}) collective-permute-start(f32[1280,128]{1,0:T(8,128)S(1)} %get-tuple-element.42), channel_id=1, source_target_pairs={{0,1},{1,0},{2,3},{3,2},{4,5},{5,4},{6,7},{7,6},{8,9},{9,8},{10,11... | collective-permute-start | bytes 1966088 | tf_op jit(solution)/shard_map/ppermute | solution.py:153
  3.0 0.1 rest.1
  3.1 0.1 collective-permute-done.1.other_ref
  3.2 0.7 %joint.1 = (f32[128,128]{1,0:T(8,128)S(1)}, f32[128,128]{1,0:T(8,128)S(1)}, f32[128,128]{1,0:T(8,128)S(1)}, f32[128,128]{1,0:T(8,128)S(1)}, f32[128,128]{1,0:T(8,128)S(1)}, /*index=5*/bf16[256,128]{1,0:T(8,128)(2,1)S(1)}) custom-call(f32[4,128,128]{2,1,0:T(8,128)S(1)} %pad_maximum_fusion.own_ref.packed_ref, ...), custom_call_target="tpu_custom_call" | custom-call | flops 26843545600 | bytes 950272 | tf_op jit(solution)/shard_map/joint/pallas_call | solution.py:141
  4.0 0.0 copy-start.1
  4.0 0.4 %collective-permute-start.3 = (f32[1280,128]{1,0:T(8,128)S(1)}, f32[1280,128]{1,0:T(8,128)S(1)}, u32[]{:S(2)}, u32[]{:S(2)}) collective-permute-start(f32[1280,128]{1,0:T(8,128)S(1)} %get-tuple-element.66), channel_id=1, source_target_pairs={{0,1},{1,0},{2,3},{3,2},{4,5},{5,4},{6,7},{7,6},{8,9},{9,8},{10,11... | collective-permute-start | bytes 1966088 | tf_op jit(solution)/shard_map/ppermute | solution.py:153
  4.4 0.2 own_part.1
  4.7 0.1 collective-permute-done.received_ref
  4.7 0.2 sent_shares.1
  5.0 2.9 %collective-permute-start.2 = (f32[640,128]{1,0:T(8,128)S(1)}, f32[640,128]{1,0:T(8,128)S(1)}, u32[]{:S(2)}, u32[]{:S(2)}) collective-permute-start(f32[640,128]{1,0:T(8,128)S(1)} %get-tuple-element.55), channel_id=1, source_target_pairs={{0,2},{1,5},{2,0},{3,7},{4,6},{5,1},{6,4},{7,3},{8,10},{9,13},{10,... | collective-permute-start | bytes 983048 | tf_op jit(solution)/shard_map/ppermute | solution.py:306
  7.9 1.6 %collective-permute-start.7 = (f32[640,128]{1,0:T(8,128)S(1)}, f32[640,128]{1,0:T(8,128)S(1)}, u32[]{:S(2)}, u32[]{:S(2)}) collective-permute-start(f32[640,128]{1,0:T(8,128)S(1)} %get-tuple-element.75), channel_id=1, source_target_pairs={{0,8},{1,5},{2,10},{3,7},{4,12},{5,1},{6,14},{7,3},{8,0},{9,13},{1... | collective-permute-start | bytes 983048 | tf_op jit(solution)/shard_map/ppermute | solution.py:306
  9.5 0.0 copy-done.1
  9.5 1.6 %grads.1 = (bf16[1,128,128]{2,1,0:T(8,128)(2,1)}, f32[128,128]{1,0:T(8,128)S(1)}, f32[128,128]{1,0:T(8,128)S(1)}, f32[128,128]{1,0:T(8,128)S(1)}, f32[136,128]{1,0:T(8,128)S(1)}) custom-call(f32[4,128,128]{2,1,0:T(8,128)S(1)} %pad_maximum_fusion.own_ref.packed_ref, f32[128,128]{1,0:T(8,128)S(1)} %get-tuple-element.56.cumul_ref, ...), custom_call_target="tpu_custom_call" | custom-call | flops 1342177280 | bytes 3510272 | tf_op jit(solution)/shard_map/grads/pallas_call | solution.py:141
  11.1 0.0 collective-permute-start.6
  11.1 0.0 collective-permute-done.3.received_ref
  11.1 0.3 kept_shares.1
  11.4 1.6 %collective-permute-done.2 = f32[640,128]{1,0:T(8,128)S(1)} collective-permute-done((f32[640,128]{1,0:T(8,128)S(1)}, f32[640,128]{1,0:T(8,128)S(1)}, u32[]{:S(2)}, u32[]{:S(2)}) %collective-permute-start.2) | collective-permute-done | bytes 327712 | tf_op jit(solution)/shard_map/ppermute | solution.py:306
  13.0 2.1 %collective-permute-start.4 = (f32[320,128]{1,0:T(8,128)S(1)}, f32[320,128]{1,0:T(8,128)S(1)}, u32[]{:S(2)}, u32[]{:S(2)}) collective-permute-start(f32[320,128]{1,0:T(8,128)S(1)} %get-tuple-element.82), channel_id=1, source_target_pairs={{0,4},{1,3},{2,6},{3,1},{4,0},{5,7},{6,2},{7,5},{8,12},{9,11},{10,... | collective-permute-start | bytes 491528 | tf_op jit(solution)/shard_map/ppermute | solution.py:306
  15.1 0.0 collective-permute-done.7
  15.2 1.6 %collective-permute-start.8 = (f32[320,128]{1,0:T(8,128)S(1)}, f32[320,128]{1,0:T(8,128)S(1)}, u32[]{:S(2)}, u32[]{:S(2)}) collective-permute-start(f32[320,128]{1,0:T(8,128)S(1)} %get-tuple-element.80), channel_id=1, source_target_pairs={{0,2},{1,9},{2,0},{3,11},{4,6},{5,13},{6,4},{7,15},{8,10},{9,1},{1... | collective-permute-start | bytes 491528 | tf_op jit(solution)/shard_map/ppermute | solution.py:306
  16.7 1.7 %collective-permute-done.4 = f32[320,128]{1,0:T(8,128)S(1)} collective-permute-done((f32[320,128]{1,0:T(8,128)S(1)}, f32[320,128]{1,0:T(8,128)S(1)}, u32[]{:S(2)}, u32[]{:S(2)}) %collective-permute-start.4) | collective-permute-done | bytes 163872 | tf_op jit(solution)/shard_map/ppermute | solution.py:306
  18.4 2.1 %collective-permute-start.5 = (f32[160,128]{1,0:T(8,128)S(1)}, f32[160,128]{1,0:T(8,128)S(1)}, u32[]{:S(2)}, u32[]{:S(2)}) collective-permute-start(f32[160,128]{1,0:T(8,128)S(1)} %get-tuple-element.84), channel_id=1, source_target_pairs={{0,8},{1,9},{2,10},{3,11},{4,12},{5,13},{6,14},{7,15},{8,0},{9,1},... | collective-permute-start | bytes 245768 | tf_op jit(solution)/shard_map/ppermute | solution.py:306
  20.6 0.0 collective-permute-done.8
  20.6 1.6 %collective-permute-start.9 = (f32[160,128]{1,0:T(8,128)S(1)}, f32[160,128]{1,0:T(8,128)S(1)}, u32[]{:S(2)}, u32[]{:S(2)}) collective-permute-start(f32[160,128]{1,0:T(8,128)S(1)} %get-tuple-element.86), channel_id=1, source_target_pairs={{0,4},{1,3},{2,6},{3,1},{4,0},{5,7},{6,2},{7,5},{8,12},{9,11},{10,... | collective-permute-start | bytes 245768 | tf_op jit(solution)/shard_map/ppermute | solution.py:306
  22.2 0.0 collective-permute-done.6.later_ref
  22.2 0.8 %collective-permute-done.5 = f32[160,128]{1,0:T(8,128)S(1)} collective-permute-done((f32[160,128]{1,0:T(8,128)S(1)}, f32[160,128]{1,0:T(8,128)S(1)}, u32[]{:S(2)}, u32[]{:S(2)}) %collective-permute-start.5) | collective-permute-done | bytes 81952 | tf_op jit(solution)/shard_map/ppermute | solution.py:306
  23.0 2.1 %collective-permute-done.9 = f32[160,128]{1,0:T(8,128)S(1)} collective-permute-done((f32[160,128]{1,0:T(8,128)S(1)}, f32[160,128]{1,0:T(8,128)S(1)}, u32[]{:S(2)}, u32[]{:S(2)}) %collective-permute-start.9) | collective-permute-done | bytes 81952 | tf_op jit(solution)/shard_map/ppermute | solution.py:306
  25.1 2.7 %collective-permute-start.10 = (f32[160,128]{1,0:T(8,128)S(1)}, f32[160,128]{1,0:T(8,128)S(1)}, u32[]{:S(2)}, u32[]{:S(2)}) collective-permute-start(f32[160,128]{1,0:T(8,128)S(1)} %pad_maximum_fusion.1), channel_id=1, source_target_pairs={{0,16},{1,17},{2,18},{3,19},{4,20},{5,21},{6,22},{7,23},{8,24},{9,... | collective-permute-start | bytes 245768 | tf_op jit(solution)/shard_map/ppermute | solution.py:306
  27.8 1.0 %finish.1 = (bf16[1,128,128]{2,1,0:T(8,128)(2,1)}, bf16[1,128,128]{2,1,0:T(8,128)(2,1)}, f32[1,128,128]{2,1,0:T(8,128)}) custom-call(f32[4,128,128]{2,1,0:T(8,128)S(1)} %pad_maximum_fusion.own_ref.packed_ref, f32[128,128]{1,0:T(8,128)S(1)} %get-tuple-element.56.cumul_ref, f32[128,128]{1,0:T(8,128)S(1)} %get-tuple-element.63.grad_key_ref, ...), custom_call_target="tpu_custom_call" | custom-call | flops 671088640 | bytes 724992 | tf_op jit(solution)/shard_map/finish/pallas_call | solution.py:141
  28.8 1.7 %collective-permute-done.10 = f32[160,128]{1,0:T(8,128)S(1)} collective-permute-done((f32[160,128]{1,0:T(8,128)S(1)}, f32[160,128]{1,0:T(8,128)S(1)}, u32[]{:S(2)}, u32[]{:S(2)}) %collective-permute-start.10) | collective-permute-done | bytes 81952 | tf_op jit(solution)/shard_map/ppermute | solution.py:306
  30.6 0.1 collective-permute-start.11
  30.6 1.3 %collective-permute-done.11.theirs_ref = f32[160,128]{1,0:T(8,128)S(1)} collective-permute-done((f32[160,128]{1,0:T(8,128)S(1)}, f32[160,128]{1,0:T(8,128)S(1)}, u32[]{:S(2)}, u32[]{:S(2)}) %collective-permute-start.11) | collective-permute-done | bytes 81952 | tf_op jit(solution)/shard_map/ppermute | solution.py:153
  31.9 0.7 %assemble.1 = f32[320,128]{1,0:T(8,128)} custom-call(f32[160,128]{1,0:T(8,128)S(1)} %pad_maximum_fusion.2.mine_ref, f32[160,128]{1,0:T(8,128)S(1)} %collective-permute-done.11.theirs_ref), custom_call_target="tpu_custom_call" | custom-call | flops 167772160 | bytes 327680 | tf_op jit(solution)/shard_map/assemble/pallas_call | solution.py:141
  (12 shorter events, 0.2 us)
Async XLA Ops:
  0.6 0.8 %copy-start.5 = (bf16[1,128,128]{2,1,0:T(8,128)(2,1)S(1)}, bf16[1,128,128]{2,1,0:T(8,128)(2,1)}, u32[]{:S(2)}) copy-start(bf16[1,128,128]{2,1,0:T(8,128)(2,1)} %param.6) | copy-start | bytes 98308
  0.6 0.8 %copy-start.4 = (bf16[1,128,128]{2,1,0:T(8,128)(2,1)S(1)}, bf16[1,128,128]{2,1,0:T(8,128)(2,1)}, u32[]{:S(2)}) copy-start(bf16[1,128,128]{2,1,0:T(8,128)(2,1)} %param.7) | copy-start | bytes 98308
  0.7 0.8 %copy-start.3 = (bf16[1,128,128]{2,1,0:T(8,128)(2,1)S(1)}, bf16[1,128,128]{2,1,0:T(8,128)(2,1)}, u32[]{:S(2)}) copy-start(bf16[1,128,128]{2,1,0:T(8,128)(2,1)} %param.8) | copy-start | bytes 98308
  0.7 0.9 %copy-start.2 = (f32[1,128,128]{2,1,0:T(8,128)S(1)}, f32[1,128,128]{2,1,0:T(8,128)}, u32[]{:S(2)}) copy-start(f32[1,128,128]{2,1,0:T(8,128)} %param.9) | copy-start | bytes 196612
  0.7 1.4 %copy-start = (bf16[1,128,5120]{2,1,0:T(8,128)(2,1)S(1)}, bf16[1,128,5120]{2,1,0:T(8,128)(2,1)}, u32[]{:S(2)}) copy-start(bf16[1,128,5120]{2,1,0:T(8,128)(2,1)} %upstream_ref.3) | copy-start | bytes 3932164
  1.6 1.7 %collective-permute-start.1 = (f32[4,128,128]{2,1,0:T(8,128)S(1)}, f32[4,128,128]{2,1,0:T(8,128)S(1)}, u32[]{:S(2)}, u32[]{:S(2)}) collective-permute-start(f32[4,128,128]{2,1,0:T(8,128)S(1)} %pad_maximum_fusion.own_ref.packed_ref), channel_id=1, source_target_pairs={{0,1},{1,0},{2,3},{3,2},{4,5},{5,4},{6,7},{7,6},{8,9},{9,8},{10,11... | collective-permute-start | bytes 786440 | tf_op jit(solution)/shard_map/ppermute | solution.py:153
  2.5 2.2 %collective-permute-start = (f32[1280,128]{1,0:T(8,128)S(1)}, f32[1280,128]{1,0:T(8,128)S(1)}, u32[]{:S(2)}, u32[]{:S(2)}) collective-permute-start(f32[1280,128]{1,0:T(8,128)S(1)} %get-tuple-element.42), channel_id=1, source_target_pairs={{0,1},{1,0},{2,3},{3,2},{4,5},{5,4},{6,7},{7,6},{8,9},{9,8},{10,11... | collective-permute-start | bytes 1966088 | tf_op jit(solution)/shard_map/ppermute | solution.py:153
  4.0 5.5 %copy-start.1 = (bf16[5120,128]{1,0:T(8,128)(2,1)S(1)}, bf16[5120,128]{1,0:T(8,128)(2,1)}, u32[]{:S(2)}) copy-start(bf16[5120,128]{1,0:T(8,128)(2,1)} %weight_ref.1) | copy-start | bytes 3932164
  4.0 7.1 %collective-permute-start.3 = (f32[1280,128]{1,0:T(8,128)S(1)}, f32[1280,128]{1,0:T(8,128)S(1)}, u32[]{:S(2)}, u32[]{:S(2)}) collective-permute-start(f32[1280,128]{1,0:T(8,128)S(1)} %get-tuple-element.66), channel_id=1, source_target_pairs={{0,1},{1,0},{2,3},{3,2},{4,5},{5,4},{6,7},{7,6},{8,9},{9,8},{10,11... | collective-permute-start | bytes 1966088 | tf_op jit(solution)/shard_map/ppermute | solution.py:153
  5.0 8.0 %collective-permute-start.2 = (f32[640,128]{1,0:T(8,128)S(1)}, f32[640,128]{1,0:T(8,128)S(1)}, u32[]{:S(2)}, u32[]{:S(2)}) collective-permute-start(f32[640,128]{1,0:T(8,128)S(1)} %get-tuple-element.55), channel_id=1, source_target_pairs={{0,2},{1,5},{2,0},{3,7},{4,6},{5,1},{6,4},{7,3},{8,10},{9,13},{10,... | collective-permute-start | bytes 983048 | tf_op jit(solution)/shard_map/ppermute | solution.py:306
  7.9 7.2 %collective-permute-start.7 = (f32[640,128]{1,0:T(8,128)S(1)}, f32[640,128]{1,0:T(8,128)S(1)}, u32[]{:S(2)}, u32[]{:S(2)}) collective-permute-start(f32[640,128]{1,0:T(8,128)S(1)} %get-tuple-element.75), channel_id=1, source_target_pairs={{0,8},{1,5},{2,10},{3,7},{4,12},{5,1},{6,14},{7,3},{8,0},{9,13},{1... | collective-permute-start | bytes 983048 | tf_op jit(solution)/shard_map/ppermute | solution.py:306
  11.1 11.1 %collective-permute-start.6 = (f32[136,128]{1,0:T(8,128)S(1)}, f32[136,128]{1,0:T(8,128)S(1)}, u32[]{:S(2)}, u32[]{:S(2)}) collective-permute-start(f32[136,128]{1,0:T(8,128)S(1)} %get-tuple-element.69), channel_id=1, source_target_pairs={{0,1},{1,0},{2,3},{3,2},{4,5},{5,4},{6,7},{7,6},{8,9},{9,8},{10,11... | collective-permute-start | bytes 208904 | tf_op jit(solution)/shard_map/ppermute | solution.py:153
  13.0 5.4 %collective-permute-start.4 = (f32[320,128]{1,0:T(8,128)S(1)}, f32[320,128]{1,0:T(8,128)S(1)}, u32[]{:S(2)}, u32[]{:S(2)}) collective-permute-start(f32[320,128]{1,0:T(8,128)S(1)} %get-tuple-element.82), channel_id=1, source_target_pairs={{0,4},{1,3},{2,6},{3,1},{4,0},{5,7},{6,2},{7,5},{8,12},{9,11},{10,... | collective-permute-start | bytes 491528 | tf_op jit(solution)/shard_map/ppermute | solution.py:306
  15.2 5.4 %collective-permute-start.8 = (f32[320,128]{1,0:T(8,128)S(1)}, f32[320,128]{1,0:T(8,128)S(1)}, u32[]{:S(2)}, u32[]{:S(2)}) collective-permute-start(f32[320,128]{1,0:T(8,128)S(1)} %get-tuple-element.80), channel_id=1, source_target_pairs={{0,2},{1,9},{2,0},{3,11},{4,6},{5,13},{6,4},{7,15},{8,10},{9,1},{1... | collective-permute-start | bytes 491528 | tf_op jit(solution)/shard_map/ppermute | solution.py:306
  18.4 4.6 %collective-permute-start.5 = (f32[160,128]{1,0:T(8,128)S(1)}, f32[160,128]{1,0:T(8,128)S(1)}, u32[]{:S(2)}, u32[]{:S(2)}) collective-permute-start(f32[160,128]{1,0:T(8,128)S(1)} %get-tuple-element.84), channel_id=1, source_target_pairs={{0,8},{1,9},{2,10},{3,11},{4,12},{5,13},{6,14},{7,15},{8,0},{9,1},... | collective-permute-start | bytes 245768 | tf_op jit(solution)/shard_map/ppermute | solution.py:306
  20.6 4.5 %collective-permute-start.9 = (f32[160,128]{1,0:T(8,128)S(1)}, f32[160,128]{1,0:T(8,128)S(1)}, u32[]{:S(2)}, u32[]{:S(2)}) collective-permute-start(f32[160,128]{1,0:T(8,128)S(1)} %get-tuple-element.86), channel_id=1, source_target_pairs={{0,4},{1,3},{2,6},{3,1},{4,0},{5,7},{6,2},{7,5},{8,12},{9,11},{10,... | collective-permute-start | bytes 245768 | tf_op jit(solution)/shard_map/ppermute | solution.py:306
  25.1 5.4 %collective-permute-start.10 = (f32[160,128]{1,0:T(8,128)S(1)}, f32[160,128]{1,0:T(8,128)S(1)}, u32[]{:S(2)}, u32[]{:S(2)}) collective-permute-start(f32[160,128]{1,0:T(8,128)S(1)} %pad_maximum_fusion.1), channel_id=1, source_target_pairs={{0,16},{1,17},{2,18},{3,19},{4,20},{5,21},{6,22},{7,23},{8,24},{9,... | collective-permute-start | bytes 245768 | tf_op jit(solution)/shard_map/ppermute | solution.py:306
  30.6 1.3 %collective-permute-start.11 = (f32[160,128]{1,0:T(8,128)S(1)}, f32[160,128]{1,0:T(8,128)S(1)}, u32[]{:S(2)}, u32[]{:S(2)}) collective-permute-start(f32[160,128]{1,0:T(8,128)S(1)} %pad_maximum_fusion.2.mine_ref), channel_id=1, source_target_pairs={{0,1},{1,0},{2,3},{3,2},{4,5},{5,4},{6,7},{7,6},{8,9},{9,8},{10,11... | collective-permute-start | bytes 245768 | tf_op jit(solution)/shard_map/ppermute | solution.py:153

commit v10 on v9

--- a/solution.py
+++ b/solution.py
@@ -286,8 +286,8 @@
         at += rows
 
 
-def add_part_kernel(received_ref, rounded_ref, *refs):
-    at = 0
+def add_part_kernel(begin, received_ref, rounded_ref, *refs):
+    at = begin
     for part, out in zip(refs[: len(refs) // 2], refs[len(refs) // 2:]):
         rows = out.shape[0]
         out[...] = part[...] + jnp.dot(
@@ -393,10 +393,14 @@
         own_part = local_call(
             own_part_kernel, part_shapes, own, rounded, name="own_part", flops=flops // 4
         )
-        sent = local_call(
-            add_part_kernel, part_shapes, received_first, rounded, *own_part,
-            name="sent_shares", flops=flops // 4,
-        )
+        sent = []
+        begin = 0
+        for part, shape in zip(own_part, part_shapes):
+            sent += local_call(
+                functools.partial(add_part_kernel, begin), [shape], received_first, rounded, part,
+                name="sent_share", flops=flops // 4,
+            )
+            begin += shape[0][0]
         kept = local_call(
             functools.partial(share_kernel, part_rows),
             [((count // 2 * part, width), F32) for part, _ in plan],

time: 32.7 us -> 32.8 us (level)
    pallas_call x10 -> x11, Pallas kernels: 5.37 us -> 5.51 us  [local_call(): pl.pallas_call(kernel, out_shape=outs, in_specs=[pl.BlockSpec(memory_spac...]
  transfers between devices with their start and end apart: 12 -> 12, of which waited for: 8 -> 10; matrix products, arithmetic and copies ran while one was open for 0% -> 0% of each run, Pallas kernels for 14% -> 15%
where the time goes in v10:
time: 32.8 us; the launch traced here: 32.6 us
  starting transfers between devices  16 us (49%)
  waiting for transfers between devices  9.28 us (28%)
  Pallas kernels  5.51 us (17%)
  local copies, waits for them, and re-layouts  0.82 us (2%)
  between operations  0.77 us (2%)
    ppermute x7, starting transfers between devices, exchanged(): return lax.ppermute(value, BOTH, pairs)  14.5 us
    ppermute x7, waiting for transfers between devices, exchanged(): return lax.ppermute(value, BOTH, pairs)  7.82 us
    pallas_call x11, Pallas kernels, local_call(): pl.pallas_call(kernel, out_shape=outs, in_specs=[pl.BlockSpec(memory_spac...  5.51 us
    ppermute x5, starting transfers between devices, swap(): return lax.ppermute(value, 'ctx', [(0, 1), (1, 0)])  1.52 us
    ppermute x5, waiting for transfers between devices, swap(): return lax.ppermute(value, 'ctx', [(0, 1), (1, 0)])  1.47 us
    unnamed x12, local copies, waits for them, and re-layouts  0.82 us
  transfers between devices with their start and end apart: 12, of which 10 were waited for; matrix products, arithmetic and copies ran while one was open for 0% of the time, Pallas kernels for 15%

profile of v10, /device:TPU:0, one launch (start us, length us, event | category | flops | bytes accessed | tf_op | source)
XLA Modules:
  0.0 32.6 jit_solution(10327334649830079043)
XLA Ops:
  0.6 0.0 copy-start.5
  0.6 0.0 copy-start.4
  0.7 0.0 copy-start.3
  0.7 0.0 copy-start.2
  0.7 0.0 copy-start
  0.7 0.7 %copy-done.5 = bf16[1,128,128]{2,1,0:T(8,128)(2,1)S(1)} copy-done((bf16[1,128,128]{2,1,0:T(8,128)(2,1)S(1)}, bf16[1,128,128]{2,1,0:T(8,128)(2,1)}, u32[]{:S(2)}) %copy-start.5) | copy-done | bytes 32792
  1.4 0.0 copy-done.4
  1.4 0.0 copy-done.3
  1.4 0.1 copy-done.2
  1.6 0.5 %collective-permute-start.1 = (f32[4,128,128]{2,1,0:T(8,128)S(1)}, f32[4,128,128]{2,1,0:T(8,128)S(1)}, u32[]{:S(2)}, u32[]{:S(2)}) collective-permute-start(f32[4,128,128]{2,1,0:T(8,128)S(1)} %pad_maximum_fusion.own_ref.packed_ref), channel_id=1, source_target_pairs={{0,1},{1,0},{2,3},{3,2},{4,5},{5,4},{6,7},{7,6},{8,9},{9,8},{10,11... | collective-permute-start | bytes 786440 | tf_op jit(solution)/shard_map/ppermute | solution.py:153
  2.1 0.0 copy-done
  2.1 0.4 %turn.1 = (f32[5120,128]{1,0:T(8,128)S(1)}, f32[1280,128]{1,0:T(8,128)S(1)}) custom-call(bf16[1,128,5120]{2,1,0:T(8,128)(2,1)S(1)} %copy-done), custom_call_target="tpu_custom_call" | custom-call | flops 13421772800 | bytes 4587520 | tf_op jit(solution)/shard_map/turn/pallas_call | solution.py:141
  2.5 0.5 %collective-permute-start = (f32[1280,128]{1,0:T(8,128)S(1)}, f32[1280,128]{1,0:T(8,128)S(1)}, u32[]{:S(2)}, u32[]{:S(2)}) collective-permute-start(f32[1280,128]{1,0:T(8,128)S(1)} %get-tuple-element.40), channel_id=1, source_target_pairs={{0,1},{1,0},{2,3},{3,2},{4,5},{5,4},{6,7},{7,6},{8,9},{9,8},{10,11... | collective-permute-start | bytes 1966088 | tf_op jit(solution)/shard_map/ppermute | solution.py:153
  3.0 0.1 rest.1
  3.1 0.1 collective-permute-done.1.other_ref
  3.2 0.7 %joint.1 = (f32[128,128]{1,0:T(8,128)S(1)}, f32[128,128]{1,0:T(8,128)S(1)}, f32[128,128]{1,0:T(8,128)S(1)}, f32[128,128]{1,0:T(8,128)S(1)}, f32[128,128]{1,0:T(8,128)S(1)}, /*index=5*/bf16[256,128]{1,0:T(8,128)(2,1)S(1)}) custom-call(f32[4,128,128]{2,1,0:T(8,128)S(1)} %pad_maximum_fusion.own_ref.packed_ref, ...), custom_call_target="tpu_custom_call" | custom-call | flops 26843545600 | bytes 950272 | tf_op jit(solution)/shard_map/joint/pallas_call | solution.py:141
  4.0 0.4 %collective-permute-start.3 = (f32[1280,128]{1,0:T(8,128)S(1)}, f32[1280,128]{1,0:T(8,128)S(1)}, u32[]{:S(2)}, u32[]{:S(2)}) collective-permute-start(f32[1280,128]{1,0:T(8,128)S(1)} %get-tuple-element.62), channel_id=1, source_target_pairs={{0,1},{1,0},{2,3},{3,2},{4,5},{5,4},{6,7},{7,6},{8,9},{9,8},{10,11... | collective-permute-start | bytes 1966088 | tf_op jit(solution)/shard_map/ppermute | solution.py:153
  4.4 0.2 own_part.1
  4.6 0.1 collective-permute-done.received_ref
  4.7 0.0 copy-start.1
  4.7 0.2 sent_share.2
  4.9 2.9 %collective-permute-start.2 = (f32[640,128]{1,0:T(8,128)S(1)}, f32[640,128]{1,0:T(8,128)S(1)}, u32[]{:S(2)}, u32[]{:S(2)}) collective-permute-start(f32[640,128]{1,0:T(8,128)S(1)} %sent_share.2), channel_id=1, source_target_pairs={{0,2},{1,5},{2,0},{3,7},{4,6},{5,1},{6,4},{7,3},{8,10},{9,13},{10,... | collective-permute-start | bytes 983048 | tf_op jit(solution)/shard_map/ppermute | solution.py:306
  7.9 0.2 sent_share.3
  8.0 1.6 %collective-permute-start.7 = (f32[640,128]{1,0:T(8,128)S(1)}, f32[640,128]{1,0:T(8,128)S(1)}, u32[]{:S(2)}, u32[]{:S(2)}) collective-permute-start(f32[640,128]{1,0:T(8,128)S(1)} %sent_share.3), channel_id=1, source_target_pairs={{0,8},{1,5},{2,10},{3,7},{4,12},{5,1},{6,14},{7,3},{8,0},{9,13},{1... | collective-permute-start | bytes 983048 | tf_op jit(solution)/shard_map/ppermute | solution.py:306
  9.7 0.0 copy-done.1
  9.7 1.6 %grads.1 = (bf16[1,128,128]{2,1,0:T(8,128)(2,1)}, f32[128,128]{1,0:T(8,128)S(1)}, f32[128,128]{1,0:T(8,128)S(1)}, f32[128,128]{1,0:T(8,128)S(1)}, f32[136,128]{1,0:T(8,128)S(1)}) custom-call(f32[4,128,128]{2,1,0:T(8,128)S(1)} %pad_maximum_fusion.own_ref.packed_ref, f32[128,128]{1,0:T(8,128)S(1)} %get-tuple-element.52.cumul_ref, ...), custom_call_target="tpu_custom_call" | custom-call | flops 1342177280 | bytes 3510272 | tf_op jit(solution)/shard_map/grads/pallas_call | solution.py:141
  11.3 0.0 collective-permute-start.6
  11.3 0.0 collective-permute-done.3.received_ref
  11.3 0.3 kept_shares.1
  11.6 1.3 %collective-permute-done.2 = f32[640,128]{1,0:T(8,128)S(1)} collective-permute-done((f32[640,128]{1,0:T(8,128)S(1)}, f32[640,128]{1,0:T(8,128)S(1)}, u32[]{:S(2)}, u32[]{:S(2)}) %collective-permute-start.2) | collective-permute-done | bytes 327712 | tf_op jit(solution)/shard_map/ppermute | solution.py:306
  12.9 0.1 slice_add_fusion.3
  13.0 2.1 %collective-permute-start.4 = (f32[320,128]{1,0:T(8,128)S(1)}, f32[320,128]{1,0:T(8,128)S(1)}, u32[]{:S(2)}, u32[]{:S(2)}) collective-permute-start(f32[320,128]{1,0:T(8,128)S(1)} %get-tuple-element.78), channel_id=1, source_target_pairs={{0,4},{1,3},{2,6},{3,1},{4,0},{5,7},{6,2},{7,5},{8,12},{9,11},{10,... | collective-permute-start | bytes 491528 | tf_op jit(solution)/shard_map/ppermute | solution.py:306
  15.1 0.1 collective-permute-done.7
  15.2 1.5 %collective-permute-start.8 = (f32[320,128]{1,0:T(8,128)S(1)}, f32[320,128]{1,0:T(8,128)S(1)}, u32[]{:S(2)}, u32[]{:S(2)}) collective-permute-start(f32[320,128]{1,0:T(8,128)S(1)} %get-tuple-element.76), channel_id=1, source_target_pairs={{0,2},{1,9},{2,0},{3,11},{4,6},{5,13},{6,4},{7,15},{8,10},{9,1},{1... | collective-permute-start | bytes 491528 | tf_op jit(solution)/shard_map/ppermute | solution.py:306
  16.7 1.7 %collective-permute-done.4 = f32[320,128]{1,0:T(8,128)S(1)} collective-permute-done((f32[320,128]{1,0:T(8,128)S(1)}, f32[320,128]{1,0:T(8,128)S(1)}, u32[]{:S(2)}, u32[]{:S(2)}) %collective-permute-start.4) | collective-permute-done | bytes 163872 | tf_op jit(solution)/shard_map/ppermute | solution.py:306
  18.4 2.1 %collective-permute-start.5 = (f32[160,128]{1,0:T(8,128)S(1)}, f32[160,128]{1,0:T(8,128)S(1)}, u32[]{:S(2)}, u32[]{:S(2)}) collective-permute-start(f32[160,128]{1,0:T(8,128)S(1)} %get-tuple-element.80), channel_id=1, source_target_pairs={{0,8},{1,9},{2,10},{3,11},{4,12},{5,13},{6,14},{7,15},{8,0},{9,1},... | collective-permute-start | bytes 245768 | tf_op jit(solution)/shard_map/ppermute | solution.py:306
  20.5 0.1 collective-permute-done.8
  20.6 1.6 %collective-permute-start.9 = (f32[160,128]{1,0:T(8,128)S(1)}, f32[160,128]{1,0:T(8,128)S(1)}, u32[]{:S(2)}, u32[]{:S(2)}) collective-permute-start(f32[160,128]{1,0:T(8,128)S(1)} %get-tuple-element.82), channel_id=1, source_target_pairs={{0,4},{1,3},{2,6},{3,1},{4,0},{5,7},{6,2},{7,5},{8,12},{9,11},{10,... | collective-permute-start | bytes 245768 | tf_op jit(solution)/shard_map/ppermute | solution.py:306
  22.2 0.0 collective-permute-done.6.later_ref
  22.2 0.7 %collective-permute-done.5 = f32[160,128]{1,0:T(8,128)S(1)} collective-permute-done((f32[160,128]{1,0:T(8,128)S(1)}, f32[160,128]{1,0:T(8,128)S(1)}, u32[]{:S(2)}, u32[]{:S(2)}) %collective-permute-start.5) | collective-permute-done | bytes 81952 | tf_op jit(solution)/shard_map/ppermute | solution.py:306
  23.0 2.2 %collective-permute-done.9 = f32[160,128]{1,0:T(8,128)S(1)} collective-permute-done((f32[160,128]{1,0:T(8,128)S(1)}, f32[160,128]{1,0:T(8,128)S(1)}, u32[]{:S(2)}, u32[]{:S(2)}) %collective-permute-start.9) | collective-permute-done | bytes 81952 | tf_op jit(solution)/shard_map/ppermute | solution.py:306
  25.2 2.7 %collective-permute-start.10 = (f32[160,128]{1,0:T(8,128)S(1)}, f32[160,128]{1,0:T(8,128)S(1)}, u32[]{:S(2)}, u32[]{:S(2)}) collective-permute-start(f32[160,128]{1,0:T(8,128)S(1)} %pad_maximum_fusion.1), channel_id=1, source_target_pairs={{0,16},{1,17},{2,18},{3,19},{4,20},{5,21},{6,22},{7,23},{8,24},{9,... | collective-permute-start | bytes 245768 | tf_op jit(solution)/shard_map/ppermute | solution.py:306
  27.8 1.0 %finish.1 = (bf16[1,128,128]{2,1,0:T(8,128)(2,1)}, bf16[1,128,128]{2,1,0:T(8,128)(2,1)}, f32[1,128,128]{2,1,0:T(8,128)}) custom-call(f32[4,128,128]{2,1,0:T(8,128)S(1)} %pad_maximum_fusion.own_ref.packed_ref, f32[128,128]{1,0:T(8,128)S(1)} %get-tuple-element.52.cumul_ref, f32[128,128]{1,0:T(8,128)S(1)} %get-tuple-element.59.grad_key_ref, ...), custom_call_target="tpu_custom_call" | custom-call | flops 671088640 | bytes 724992 | tf_op jit(solution)/shard_map/finish/pallas_call | solution.py:141
  28.8 1.7 %collective-permute-done.10 = f32[160,128]{1,0:T(8,128)S(1)} collective-permute-done((f32[160,128]{1,0:T(8,128)S(1)}, f32[160,128]{1,0:T(8,128)S(1)}, u32[]{:S(2)}, u32[]{:S(2)}) %collective-permute-start.10) | collective-permute-done | bytes 81952 | tf_op jit(solution)/shard_map/ppermute | solution.py:306
  30.6 0.1 collective-permute-start.11
  30.7 1.3 %collective-permute-done.11.theirs_ref = f32[160,128]{1,0:T(8,128)S(1)} collective-permute-done((f32[160,128]{1,0:T(8,128)S(1)}, f32[160,128]{1,0:T(8,128)S(1)}, u32[]{:S(2)}, u32[]{:S(2)}) %collective-permute-start.11) | collective-permute-done | bytes 81952 | tf_op jit(solution)/shard_map/ppermute | solution.py:153
  31.9 0.7 %assemble.1 = f32[320,128]{1,0:T(8,128)} custom-call(f32[160,128]{1,0:T(8,128)S(1)} %pad_maximum_fusion.2.mine_ref, f32[160,128]{1,0:T(8,128)S(1)} %collective-permute-done.11.theirs_ref), custom_call_target="tpu_custom_call" | custom-call | flops 167772160 | bytes 327680 | tf_op jit(solution)/shard_map/assemble/pallas_call | solution.py:141
  (11 shorter events, 0.2 us)
Async XLA Ops:
  0.6 0.8 %copy-start.5 = (bf16[1,128,128]{2,1,0:T(8,128)(2,1)S(1)}, bf16[1,128,128]{2,1,0:T(8,128)(2,1)}, u32[]{:S(2)}) copy-start(bf16[1,128,128]{2,1,0:T(8,128)(2,1)} %param.6) | copy-start | bytes 98308
  0.6 0.8 %copy-start.4 = (bf16[1,128,128]{2,1,0:T(8,128)(2,1)S(1)}, bf16[1,128,128]{2,1,0:T(8,128)(2,1)}, u32[]{:S(2)}) copy-start(bf16[1,128,128]{2,1,0:T(8,128)(2,1)} %param.7) | copy-start | bytes 98308
  0.7 0.8 %copy-start.3 = (bf16[1,128,128]{2,1,0:T(8,128)(2,1)S(1)}, bf16[1,128,128]{2,1,0:T(8,128)(2,1)}, u32[]{:S(2)}) copy-start(bf16[1,128,128]{2,1,0:T(8,128)(2,1)} %param.8) | copy-start | bytes 98308
  0.7 0.9 %copy-start.2 = (f32[1,128,128]{2,1,0:T(8,128)S(1)}, f32[1,128,128]{2,1,0:T(8,128)}, u32[]{:S(2)}) copy-start(f32[1,128,128]{2,1,0:T(8,128)} %param.9) | copy-start | bytes 196612
  0.7 1.4 %copy-start = (bf16[1,128,5120]{2,1,0:T(8,128)(2,1)S(1)}, bf16[1,128,5120]{2,1,0:T(8,128)(2,1)}, u32[]{:S(2)}) copy-start(bf16[1,128,5120]{2,1,0:T(8,128)(2,1)} %upstream_ref.3) | copy-start | bytes 3932164
  1.6 1.7 %collective-permute-start.1 = (f32[4,128,128]{2,1,0:T(8,128)S(1)}, f32[4,128,128]{2,1,0:T(8,128)S(1)}, u32[]{:S(2)}, u32[]{:S(2)}) collective-permute-start(f32[4,128,128]{2,1,0:T(8,128)S(1)} %pad_maximum_fusion.own_ref.packed_ref), channel_id=1, source_target_pairs={{0,1},{1,0},{2,3},{3,2},{4,5},{5,4},{6,7},{7,6},{8,9},{9,8},{10,11... | collective-permute-start | bytes 786440 | tf_op jit(solution)/shard_map/ppermute | solution.py:153
  2.5 2.2 %collective-permute-start = (f32[1280,128]{1,0:T(8,128)S(1)}, f32[1280,128]{1,0:T(8,128)S(1)}, u32[]{:S(2)}, u32[]{:S(2)}) collective-permute-start(f32[1280,128]{1,0:T(8,128)S(1)} %get-tuple-element.40), channel_id=1, source_target_pairs={{0,1},{1,0},{2,3},{3,2},{4,5},{5,4},{6,7},{7,6},{8,9},{9,8},{10,11... | collective-permute-start | bytes 1966088 | tf_op jit(solution)/shard_map/ppermute | solution.py:153
  4.0 7.3 %collective-permute-start.3 = (f32[1280,128]{1,0:T(8,128)S(1)}, f32[1280,128]{1,0:T(8,128)S(1)}, u32[]{:S(2)}, u32[]{:S(2)}) collective-permute-start(f32[1280,128]{1,0:T(8,128)S(1)} %get-tuple-element.62), channel_id=1, source_target_pairs={{0,1},{1,0},{2,3},{3,2},{4,5},{5,4},{6,7},{7,6},{8,9},{9,8},{10,11... | collective-permute-start | bytes 1966088 | tf_op jit(solution)/shard_map/ppermute | solution.py:153
  4.7 4.9 %copy-start.1 = (bf16[5120,128]{1,0:T(8,128)(2,1)S(1)}, bf16[5120,128]{1,0:T(8,128)(2,1)}, u32[]{:S(2)}) copy-start(bf16[5120,128]{1,0:T(8,128)(2,1)} %weight_ref.1) | copy-start | bytes 3932164
  4.9 8.0 %collective-permute-start.2 = (f32[640,128]{1,0:T(8,128)S(1)}, f32[640,128]{1,0:T(8,128)S(1)}, u32[]{:S(2)}, u32[]{:S(2)}) collective-permute-start(f32[640,128]{1,0:T(8,128)S(1)} %sent_share.2), channel_id=1, source_target_pairs={{0,2},{1,5},{2,0},{3,7},{4,6},{5,1},{6,4},{7,3},{8,10},{9,13},{10,... | collective-permute-start | bytes 983048 | tf_op jit(solution)/shard_map/ppermute | solution.py:306
  8.0 7.1 %collective-permute-start.7 = (f32[640,128]{1,0:T(8,128)S(1)}, f32[640,128]{1,0:T(8,128)S(1)}, u32[]{:S(2)}, u32[]{:S(2)}) collective-permute-start(f32[640,128]{1,0:T(8,128)S(1)} %sent_share.3), channel_id=1, source_target_pairs={{0,8},{1,5},{2,10},{3,7},{4,12},{5,1},{6,14},{7,3},{8,0},{9,13},{1... | collective-permute-start | bytes 983048 | tf_op jit(solution)/shard_map/ppermute | solution.py:306
  11.3 10.9 %collective-permute-start.6 = (f32[136,128]{1,0:T(8,128)S(1)}, f32[136,128]{1,0:T(8,128)S(1)}, u32[]{:S(2)}, u32[]{:S(2)}) collective-permute-start(f32[136,128]{1,0:T(8,128)S(1)} %get-tuple-element.65), channel_id=1, source_target_pairs={{0,1},{1,0},{2,3},{3,2},{4,5},{5,4},{6,7},{7,6},{8,9},{9,8},{10,11... | collective-permute-start | bytes 208904 | tf_op jit(solution)/shard_map/ppermute | solution.py:153
  13.0 5.4 %collective-permute-start.4 = (f32[320,128]{1,0:T(8,128)S(1)}, f32[320,128]{1,0:T(8,128)S(1)}, u32[]{:S(2)}, u32[]{:S(2)}) collective-permute-start(f32[320,128]{1,0:T(8,128)S(1)} %get-tuple-element.78), channel_id=1, source_target_pairs={{0,4},{1,3},{2,6},{3,1},{4,0},{5,7},{6,2},{7,5},{8,12},{9,11},{10,... | collective-permute-start | bytes 491528 | tf_op jit(solution)/shard_map/ppermute | solution.py:306
  15.2 5.4 %collective-permute-start.8 = (f32[320,128]{1,0:T(8,128)S(1)}, f32[320,128]{1,0:T(8,128)S(1)}, u32[]{:S(2)}, u32[]{:S(2)}) collective-permute-start(f32[320,128]{1,0:T(8,128)S(1)} %get-tuple-element.76), channel_id=1, source_target_pairs={{0,2},{1,9},{2,0},{3,11},{4,6},{5,13},{6,4},{7,15},{8,10},{9,1},{1... | collective-permute-start | bytes 491528 | tf_op jit(solution)/shard_map/ppermute | solution.py:306
  18.4 4.6 %collective-permute-start.5 = (f32[160,128]{1,0:T(8,128)S(1)}, f32[160,128]{1,0:T(8,128)S(1)}, u32[]{:S(2)}, u32[]{:S(2)}) collective-permute-start(f32[160,128]{1,0:T(8,128)S(1)} %get-tuple-element.80), channel_id=1, source_target_pairs={{0,8},{1,9},{2,10},{3,11},{4,12},{5,13},{6,14},{7,15},{8,0},{9,1},... | collective-permute-start | bytes 245768 | tf_op jit(solution)/shard_map/ppermute | solution.py:306
  20.6 4.5 %collective-permute-start.9 = (f32[160,128]{1,0:T(8,128)S(1)}, f32[160,128]{1,0:T(8,128)S(1)}, u32[]{:S(2)}, u32[]{:S(2)}) collective-permute-start(f32[160,128]{1,0:T(8,128)S(1)} %get-tuple-element.82), channel_id=1, source_target_pairs={{0,4},{1,3},{2,6},{3,1},{4,0},{5,7},{6,2},{7,5},{8,12},{9,11},{10,... | collective-permute-start | bytes 245768 | tf_op jit(solution)/shard_map/ppermute | solution.py:306
  25.2 5.4 %collective-permute-start.10 = (f32[160,128]{1,0:T(8,128)S(1)}, f32[160,128]{1,0:T(8,128)S(1)}, u32[]{:S(2)}, u32[]{:S(2)}) collective-permute-start(f32[160,128]{1,0:T(8,128)S(1)} %pad_maximum_fusion.1), channel_id=1, source_target_pairs={{0,16},{1,17},{2,18},{3,19},{4,20},{5,21},{6,22},{7,23},{8,24},{9,... | collective-permute-start | bytes 245768 | tf_op jit(solution)/shard_map/ppermute | solution.py:306
  30.6 1.3 %collective-permute-start.11 = (f32[160,128]{1,0:T(8,128)S(1)}, f32[160,128]{1,0:T(8,128)S(1)}, u32[]{:S(2)}, u32[]{:S(2)}) collective-permute-start(f32[160,128]{1,0:T(8,128)S(1)} %pad_maximum_fusion.2.mine_ref), channel_id=1, source_target_pairs={{0,1},{1,0},{2,3},{3,2},{4,5},{5,4},{6,7},{7,6},{8,9},{9,8},{10,11... | collective-permute-start | bytes 245768 | tf_op jit(solution)/shard_map/ppermute | solution.py:153

commit v11 on v9

--- a/solution.py
+++ b/solution.py
@@ -54,7 +54,7 @@
     cumul = cumulate(decay_ref[0])
     to_end = jnp.exp(cumul[-1:] - cumul)
     key_to_end = key_ref[0].astype(F32) * to_end
-    state_ref[...] = product(split(key_to_end, 2), [value_ref[0]], 0, 0)
+    state_ref[...] = product(split(key_to_end, 3), [value_ref[0]], 0, 0)
 
 
 def within_kernel(query_ref, key_ref, value_ref, decay_ref, within_ref, scores_ref, cumul_ref):
@@ -62,15 +62,15 @@
     cumul_ref[...] = cumul
     query_scaled = query_ref[0].astype(F32) * jnp.exp(cumul)
     key_scaled = key_ref[0].astype(F32) * jnp.exp(-cumul)
-    scores = product(split(query_scaled, 2), split(key_scaled, 2), 1, 1)
+    scores = product(split(query_scaled, 3), split(key_scaled, 3), 1, 1)
     scores = jnp.where(lower_mask(cumul.shape[0]), scores, 0.0)
     scores_ref[...] = scores
-    within_ref[...] = product(split(scores, 2), [value_ref[0]], 1, 0)
+    within_ref[...] = product(split(scores, 3), [value_ref[0]], 1, 0)
 
 
 def normed_kernel(query_ref, cumul_ref, within_ref, state_ref, normed_ref, scale_ref, rounded_ref):
     query_scaled = query_ref[0].astype(F32) * jnp.exp(cumul_ref[...])
-    output = within_ref[...] + product(split(query_scaled, 2), split(state_ref[...], 2), 1, 0)
+    output = within_ref[...] + product(split(query_scaled, 3), split(state_ref[...], 3), 1, 0)
     scale_inv = lax.rsqrt(jnp.mean(output * output, axis=-1, keepdims=True) + EPSILON)
     normed = output * scale_inv
     normed_ref[...] = normed
@@ -94,18 +94,18 @@
     grad_output = scale_ref[...] * (
         grad_normed - normed * jnp.mean(grad_normed * normed, axis=-1, keepdims=True)
     )
-    grad_output = split(grad_output, 2)
-    query_scaled = split(query * rising, 2)
-    key_scaled = split(key * falling, 2)
+    grad_output = split(grad_output, 3)
+    query_scaled = split(query * rising, 3)
+    key_scaled = split(key * falling, 3)
     pairs = product(grad_output, [value], 1, 1)
-    pairs = split(jnp.where(lower_mask(cumul.shape[0]), pairs, 0.0), 2)
+    pairs = split(jnp.where(lower_mask(cumul.shape[0]), pairs, 0.0), 3)
     grad_query = rising * (
-        product(pairs, key_scaled, 1, 0) + product(grad_output, split(state_ref[...], 2), 1, 1)
+        product(pairs, key_scaled, 1, 0) + product(grad_output, split(state_ref[...], 3), 1, 1)
     )
     grad_query_ref[0] = grad_query.astype(BF16)
     grad_key = falling * product(pairs, query_scaled, 0, 0)
     grad_key_ref[...] = grad_key
-    grad_value_ref[...] = product(split(scores_ref[...], 2), grad_output, 0, 0)
+    grad_value_ref[...] = product(split(scores_ref[...], 3), grad_output, 0, 0)
     gate = query * grad_query - key * grad_key
     gate_ref[...] = gate
     width = query.shape[1]
@@ -125,10 +125,10 @@
     to_end = jnp.exp(cumul[-1:] - cumul)
     last = lax.axis_index("ctx") == lax.axis_size("ctx") - 1
     later = jnp.where(last, 0.0, later_ref[...])
-    grad_in = split(later[:width], 2)
+    grad_in = split(later[:width], 3)
     extra = to_end * product([packed_ref[2].astype(BF16)], grad_in, 1, 1)
     key_out_ref[0] = (grad_key_ref[...] + extra).astype(BF16)
-    grad_value = grad_value_ref[...] + product(split(key * to_end, 2), grad_in, 1, 0)
+    grad_value = grad_value_ref[...] + product(split(key * to_end, 3), grad_in, 1, 0)
     value_out_ref[0] = grad_value.astype(BF16)
     gate = gate_ref[...] - key * extra
     lower = lower_mask(cumul.shape[0]).astype(F32).astype(BF16)
@@ -249,13 +249,13 @@
     cumul = [cumuls[:, :width], cumuls[:, width:]]
     scaled = [q * jnp.exp(c) for q, c in zip(query, cumul)]
     scores = [
-        jnp.where(lower, joined([(q, 2, k * jnp.exp(-c), 2)], 1, 1), 0.0)
+        jnp.where(lower, joined([(q, 3, k * jnp.exp(-c), 3)], 1, 1), 0.0)
         for q, k, c in zip(scaled, key, cumul)
     ]
     to_end = jnp.exp(cumul[0][-1:] - cumul[0])
-    state = joined([(key[0] * to_end, 2, value[0], 1)], 0, 0)
-    early = normalized(joined([(scores[0], 2, value[0], 1)], 1, 0))
-    late = normalized(joined([(scores[1], 2, value[1], 1), (scaled[1], 2, state, 2)], 1, 0))
+    state = joined([(key[0] * to_end, 3, value[0], 1)], 0, 0)
+    early = normalized(joined([(scores[0], 3, value[0], 1)], 1, 0))
+    late = normalized(joined([(scores[1], 3, value[1], 1), (scaled[1], 3, state, 3)], 1, 0))
     rounded_ref[:length] = jnp.where(first, early[2], late[2])
     rounded_ref[length:] = jnp.where(first, late[2], early[2])
     cumul_ref[...] = jnp.where(first, cumul[0], cumul[1])

time: 32.7 us -> 32.7 us (level)
  Pallas kernels: 5.37 us -> 5.74 us
  waiting for transfers between devices: 9.34 us -> 9 us
    pallas_call x10, Pallas kernels: 5.37 us -> 5.74 us  [local_call(): pl.pallas_call(kernel, out_shape=outs, in_specs=[pl.BlockSpec(memory_spac...]
  transfers between devices with their start and end apart: 12 -> 12, of which waited for: 8 -> 7; matrix products, arithmetic and copies ran while one was open for 0% -> 0% of each run, Pallas kernels for 14% -> 15%
where the time goes in v11:
time: 32.7 us; the launch traced here: 32.6 us
  starting transfers between devices  16 us (49%)
  waiting for transfers between devices  9 us (28%)
  Pallas kernels  5.74 us (18%)
  local copies, waits for them, and re-layouts  0.83 us (3%)
  between operations  0.79 us (2%)
    ppermute x7, starting transfers between devices, exchanged(): return lax.ppermute(value, BOTH, pairs)  14.5 us
    ppermute x7, waiting for transfers between devices, exchanged(): return lax.ppermute(value, BOTH, pairs)  7.62 us
    pallas_call x10, Pallas kernels, local_call(): pl.pallas_call(kernel, out_shape=outs, in_specs=[pl.BlockSpec(memory_spac...  5.74 us
    ppermute x5, starting transfers between devices, swap(): return lax.ppermute(value, 'ctx', [(0, 1), (1, 0)])  1.52 us
    ppermute x5, waiting for transfers between devices, swap(): return lax.ppermute(value, 'ctx', [(0, 1), (1, 0)])  1.38 us
    unnamed x12, local copies, waits for them, and re-layouts  0.83 us
  transfers between devices with their start and end apart: 12, of which 7 were waited for; matrix products, arithmetic and copies ran while one was open for 0% of the time, Pallas kernels for 15%

profile of v11, /device:TPU:0, one launch (start us, length us, event | category | flops | bytes accessed | tf_op | source)
XLA Modules:
  0.0 32.6 jit_solution(14051498891294865086)
XLA Ops:
  0.6 0.0 copy-start.5
  0.6 0.0 copy-start.4
  0.7 0.0 copy-start.3
  0.7 0.0 copy-start.2
  0.7 0.0 copy-start
  0.7 0.7 %copy-done.5 = bf16[1,128,128]{2,1,0:T(8,128)(2,1)S(1)} copy-done((bf16[1,128,128]{2,1,0:T(8,128)(2,1)S(1)}, bf16[1,128,128]{2,1,0:T(8,128)(2,1)}, u32[]{:S(2)}) %copy-start.5) | copy-done | bytes 32792
  1.4 0.0 copy-done.4
  1.4 0.0 copy-done.3
  1.4 0.1 copy-done.2
  1.6 0.5 %collective-permute-start.1 = (f32[4,128,128]{2,1,0:T(8,128)S(1)}, f32[4,128,128]{2,1,0:T(8,128)S(1)}, u32[]{:S(2)}, u32[]{:S(2)}) collective-permute-start(f32[4,128,128]{2,1,0:T(8,128)S(1)} %pad_maximum_fusion.own_ref.packed_ref), channel_id=1, source_target_pairs={{0,1},{1,0},{2,3},{3,2},{4,5},{5,4},{6,7},{7,6},{8,9},{9,8},{10,11... | collective-permute-start | bytes 786440 | tf_op jit(solution)/shard_map/ppermute | solution.py:153
  2.1 0.0 copy-done
  2.1 0.4 %turn.1 = (f32[5120,128]{1,0:T(8,128)S(1)}, f32[1280,128]{1,0:T(8,128)S(1)}) custom-call(bf16[1,128,5120]{2,1,0:T(8,128)(2,1)S(1)} %copy-done), custom_call_target="tpu_custom_call" | custom-call | flops 13421772800 | bytes 4587520 | tf_op jit(solution)/shard_map/turn/pallas_call | solution.py:141
  2.5 0.5 %collective-permute-start = (f32[1280,128]{1,0:T(8,128)S(1)}, f32[1280,128]{1,0:T(8,128)S(1)}, u32[]{:S(2)}, u32[]{:S(2)}) collective-permute-start(f32[1280,128]{1,0:T(8,128)S(1)} %get-tuple-element.42), channel_id=1, source_target_pairs={{0,1},{1,0},{2,3},{3,2},{4,5},{5,4},{6,7},{7,6},{8,9},{9,8},{10,11... | collective-permute-start | bytes 1966088 | tf_op jit(solution)/shard_map/ppermute | solution.py:153
  3.0 0.1 rest.1
  3.1 0.1 collective-permute-done.1.other_ref
  3.2 0.9 %joint.1 = (f32[128,128]{1,0:T(8,128)S(1)}, f32[128,128]{1,0:T(8,128)S(1)}, f32[128,128]{1,0:T(8,128)S(1)}, f32[128,128]{1,0:T(8,128)S(1)}, f32[128,128]{1,0:T(8,128)S(1)}, /*index=5*/bf16[256,128]{1,0:T(8,128)(2,1)S(1)}) custom-call(f32[4,128,128]{2,1,0:T(8,128)S(1)} %pad_maximum_fusion.own_ref.packed_ref, ...), custom_call_target="tpu_custom_call" | custom-call | flops 26843545600 | bytes 950272 | tf_op jit(solution)/shard_map/joint/pallas_call | solution.py:141
  4.1 0.0 copy-start.1
  4.1 0.4 %collective-permute-start.3 = (f32[1280,128]{1,0:T(8,128)S(1)}, f32[1280,128]{1,0:T(8,128)S(1)}, u32[]{:S(2)}, u32[]{:S(2)}) collective-permute-start(f32[1280,128]{1,0:T(8,128)S(1)} %get-tuple-element.66), channel_id=1, source_target_pairs={{0,1},{1,0},{2,3},{3,2},{4,5},{5,4},{6,7},{7,6},{8,9},{9,8},{10,11... | collective-permute-start | bytes 1966088 | tf_op jit(solution)/shard_map/ppermute | solution.py:153
  4.5 0.2 own_part.1
  4.8 0.0 collective-permute-done.received_ref
  4.8 0.2 sent_shares.1
  5.0 2.9 %collective-permute-start.2 = (f32[640,128]{1,0:T(8,128)S(1)}, f32[640,128]{1,0:T(8,128)S(1)}, u32[]{:S(2)}, u32[]{:S(2)}) collective-permute-start(f32[640,128]{1,0:T(8,128)S(1)} %get-tuple-element.55), channel_id=1, source_target_pairs={{0,2},{1,5},{2,0},{3,7},{4,6},{5,1},{6,4},{7,3},{8,10},{9,13},{10,... | collective-permute-start | bytes 983048 | tf_op jit(solution)/shard_map/ppermute | solution.py:306
  7.9 1.6 %collective-permute-start.7 = (f32[640,128]{1,0:T(8,128)S(1)}, f32[640,128]{1,0:T(8,128)S(1)}, u32[]{:S(2)}, u32[]{:S(2)}) collective-permute-start(f32[640,128]{1,0:T(8,128)S(1)} %get-tuple-element.75), channel_id=1, source_target_pairs={{0,8},{1,5},{2,10},{3,7},{4,12},{5,1},{6,14},{7,3},{8,0},{9,13},{1... | collective-permute-start | bytes 983048 | tf_op jit(solution)/shard_map/ppermute | solution.py:306
  9.5 0.0 copy-done.1
  9.5 1.8 %grads.1 = (bf16[1,128,128]{2,1,0:T(8,128)(2,1)}, f32[128,128]{1,0:T(8,128)S(1)}, f32[128,128]{1,0:T(8,128)S(1)}, f32[128,128]{1,0:T(8,128)S(1)}, f32[136,128]{1,0:T(8,128)S(1)}) custom-call(f32[4,128,128]{2,1,0:T(8,128)S(1)} %pad_maximum_fusion.own_ref.packed_ref, f32[128,128]{1,0:T(8,128)S(1)} %get-tuple-element.56.cumul_ref, ...), custom_call_target="tpu_custom_call" | custom-call | flops 1342177280 | bytes 3510272 | tf_op jit(solution)/shard_map/grads/pallas_call | solution.py:141
  11.3 0.0 collective-permute-start.6
  11.3 0.0 collective-permute-done.3.received_ref
  11.3 0.3 kept_shares.1
  11.7 1.3 %collective-permute-done.2 = f32[640,128]{1,0:T(8,128)S(1)} collective-permute-done((f32[640,128]{1,0:T(8,128)S(1)}, f32[640,128]{1,0:T(8,128)S(1)}, u32[]{:S(2)}, u32[]{:S(2)}) %collective-permute-start.2) | collective-permute-done | bytes 327712 | tf_op jit(solution)/shard_map/ppermute | solution.py:306
  13.0 2.1 %collective-permute-start.4 = (f32[320,128]{1,0:T(8,128)S(1)}, f32[320,128]{1,0:T(8,128)S(1)}, u32[]{:S(2)}, u32[]{:S(2)}) collective-permute-start(f32[320,128]{1,0:T(8,128)S(1)} %get-tuple-element.82), channel_id=1, source_target_pairs={{0,4},{1,3},{2,6},{3,1},{4,0},{5,7},{6,2},{7,5},{8,12},{9,11},{10,... | collective-permute-start | bytes 491528 | tf_op jit(solution)/shard_map/ppermute | solution.py:306
  15.1 0.0 collective-permute-done.7
  15.2 1.6 %collective-permute-start.8 = (f32[320,128]{1,0:T(8,128)S(1)}, f32[320,128]{1,0:T(8,128)S(1)}, u32[]{:S(2)}, u32[]{:S(2)}) collective-permute-start(f32[320,128]{1,0:T(8,128)S(1)} %get-tuple-element.80), channel_id=1, source_target_pairs={{0,2},{1,9},{2,0},{3,11},{4,6},{5,13},{6,4},{7,15},{8,10},{9,1},{1... | collective-permute-start | bytes 491528 | tf_op jit(solution)/shard_map/ppermute | solution.py:306
  16.7 1.7 %collective-permute-done.4 = f32[320,128]{1,0:T(8,128)S(1)} collective-permute-done((f32[320,128]{1,0:T(8,128)S(1)}, f32[320,128]{1,0:T(8,128)S(1)}, u32[]{:S(2)}, u32[]{:S(2)}) %collective-permute-start.4) | collective-permute-done | bytes 163872 | tf_op jit(solution)/shard_map/ppermute | solution.py:306
  18.4 2.1 %collective-permute-start.5 = (f32[160,128]{1,0:T(8,128)S(1)}, f32[160,128]{1,0:T(8,128)S(1)}, u32[]{:S(2)}, u32[]{:S(2)}) collective-permute-start(f32[160,128]{1,0:T(8,128)S(1)} %get-tuple-element.84), channel_id=1, source_target_pairs={{0,8},{1,9},{2,10},{3,11},{4,12},{5,13},{6,14},{7,15},{8,0},{9,1},... | collective-permute-start | bytes 245768 | tf_op jit(solution)/shard_map/ppermute | solution.py:306
  20.6 0.0 collective-permute-done.8
  20.6 1.6 %collective-permute-start.9 = (f32[160,128]{1,0:T(8,128)S(1)}, f32[160,128]{1,0:T(8,128)S(1)}, u32[]{:S(2)}, u32[]{:S(2)}) collective-permute-start(f32[160,128]{1,0:T(8,128)S(1)} %get-tuple-element.86), channel_id=1, source_target_pairs={{0,4},{1,3},{2,6},{3,1},{4,0},{5,7},{6,2},{7,5},{8,12},{9,11},{10,... | collective-permute-start | bytes 245768 | tf_op jit(solution)/shard_map/ppermute | solution.py:306
  22.2 0.0 collective-permute-done.6.later_ref
  22.2 0.8 %collective-permute-done.5 = f32[160,128]{1,0:T(8,128)S(1)} collective-permute-done((f32[160,128]{1,0:T(8,128)S(1)}, f32[160,128]{1,0:T(8,128)S(1)}, u32[]{:S(2)}, u32[]{:S(2)}) %collective-permute-start.5) | collective-permute-done | bytes 81952 | tf_op jit(solution)/shard_map/ppermute | solution.py:306
  23.0 2.1 %collective-permute-done.9 = f32[160,128]{1,0:T(8,128)S(1)} collective-permute-done((f32[160,128]{1,0:T(8,128)S(1)}, f32[160,128]{1,0:T(8,128)S(1)}, u32[]{:S(2)}, u32[]{:S(2)}) %collective-permute-start.9) | collective-permute-done | bytes 81952 | tf_op jit(solution)/shard_map/ppermute | solution.py:306
  25.1 2.7 %collective-permute-start.10 = (f32[160,128]{1,0:T(8,128)S(1)}, f32[160,128]{1,0:T(8,128)S(1)}, u32[]{:S(2)}, u32[]{:S(2)}) collective-permute-start(f32[160,128]{1,0:T(8,128)S(1)} %pad_maximum_fusion.1), channel_id=1, source_target_pairs={{0,16},{1,17},{2,18},{3,19},{4,20},{5,21},{6,22},{7,23},{8,24},{9,... | collective-permute-start | bytes 245768 | tf_op jit(solution)/shard_map/ppermute | solution.py:306
  27.8 1.0 %finish.1 = (bf16[1,128,128]{2,1,0:T(8,128)(2,1)}, bf16[1,128,128]{2,1,0:T(8,128)(2,1)}, f32[1,128,128]{2,1,0:T(8,128)}) custom-call(f32[4,128,128]{2,1,0:T(8,128)S(1)} %pad_maximum_fusion.own_ref.packed_ref, f32[128,128]{1,0:T(8,128)S(1)} %get-tuple-element.56.cumul_ref, f32[128,128]{1,0:T(8,128)S(1)} %get-tuple-element.63.grad_key_ref, ...), custom_call_target="tpu_custom_call" | custom-call | flops 671088640 | bytes 724992 | tf_op jit(solution)/shard_map/finish/pallas_call | solution.py:141
  28.8 1.7 %collective-permute-done.10 = f32[160,128]{1,0:T(8,128)S(1)} collective-permute-done((f32[160,128]{1,0:T(8,128)S(1)}, f32[160,128]{1,0:T(8,128)S(1)}, u32[]{:S(2)}, u32[]{:S(2)}) %collective-permute-start.10) | collective-permute-done | bytes 81952 | tf_op jit(solution)/shard_map/ppermute | solution.py:306
  30.6 0.1 collective-permute-start.11
  30.6 1.3 %collective-permute-done.11.theirs_ref = f32[160,128]{1,0:T(8,128)S(1)} collective-permute-done((f32[160,128]{1,0:T(8,128)S(1)}, f32[160,128]{1,0:T(8,128)S(1)}, u32[]{:S(2)}, u32[]{:S(2)}) %collective-permute-start.11) | collective-permute-done | bytes 81952 | tf_op jit(solution)/shard_map/ppermute | solution.py:153
  31.9 0.7 %assemble.1 = f32[320,128]{1,0:T(8,128)} custom-call(f32[160,128]{1,0:T(8,128)S(1)} %pad_maximum_fusion.2.mine_ref, f32[160,128]{1,0:T(8,128)S(1)} %collective-permute-done.11.theirs_ref), custom_call_target="tpu_custom_call" | custom-call | flops 167772160 | bytes 327680 | tf_op jit(solution)/shard_map/assemble/pallas_call | solution.py:141
  (12 shorter events, 0.2 us)
Async XLA Ops:
  0.6 0.8 %copy-start.5 = (bf16[1,128,128]{2,1,0:T(8,128)(2,1)S(1)}, bf16[1,128,128]{2,1,0:T(8,128)(2,1)}, u32[]{:S(2)}) copy-start(bf16[1,128,128]{2,1,0:T(8,128)(2,1)} %param.6) | copy-start | bytes 98308
  0.6 0.8 %copy-start.4 = (bf16[1,128,128]{2,1,0:T(8,128)(2,1)S(1)}, bf16[1,128,128]{2,1,0:T(8,128)(2,1)}, u32[]{:S(2)}) copy-start(bf16[1,128,128]{2,1,0:T(8,128)(2,1)} %param.7) | copy-start | bytes 98308
  0.7 0.8 %copy-start.3 = (bf16[1,128,128]{2,1,0:T(8,128)(2,1)S(1)}, bf16[1,128,128]{2,1,0:T(8,128)(2,1)}, u32[]{:S(2)}) copy-start(bf16[1,128,128]{2,1,0:T(8,128)(2,1)} %param.8) | copy-start | bytes 98308
  0.7 0.9 %copy-start.2 = (f32[1,128,128]{2,1,0:T(8,128)S(1)}, f32[1,128,128]{2,1,0:T(8,128)}, u32[]{:S(2)}) copy-start(f32[1,128,128]{2,1,0:T(8,128)} %param.9) | copy-start | bytes 196612
  0.7 1.4 %copy-start = (bf16[1,128,5120]{2,1,0:T(8,128)(2,1)S(1)}, bf16[1,128,5120]{2,1,0:T(8,128)(2,1)}, u32[]{:S(2)}) copy-start(bf16[1,128,5120]{2,1,0:T(8,128)(2,1)} %upstream_ref.3) | copy-start | bytes 3932164
  1.6 1.7 %collective-permute-start.1 = (f32[4,128,128]{2,1,0:T(8,128)S(1)}, f32[4,128,128]{2,1,0:T(8,128)S(1)}, u32[]{:S(2)}, u32[]{:S(2)}) collective-permute-start(f32[4,128,128]{2,1,0:T(8,128)S(1)} %pad_maximum_fusion.own_ref.packed_ref), channel_id=1, source_target_pairs={{0,1},{1,0},{2,3},{3,2},{4,5},{5,4},{6,7},{7,6},{8,9},{9,8},{10,11... | collective-permute-start | bytes 786440 | tf_op jit(solution)/shard_map/ppermute | solution.py:153
  2.5 2.2 %collective-permute-start = (f32[1280,128]{1,0:T(8,128)S(1)}, f32[1280,128]{1,0:T(8,128)S(1)}, u32[]{:S(2)}, u32[]{:S(2)}) collective-permute-start(f32[1280,128]{1,0:T(8,128)S(1)} %get-tuple-element.42), channel_id=1, source_target_pairs={{0,1},{1,0},{2,3},{3,2},{4,5},{5,4},{6,7},{7,6},{8,9},{9,8},{10,11... | collective-permute-start | bytes 1966088 | tf_op jit(solution)/shard_map/ppermute | solution.py:153
  4.1 5.4 %copy-start.1 = (bf16[5120,128]{1,0:T(8,128)(2,1)S(1)}, bf16[5120,128]{1,0:T(8,128)(2,1)}, u32[]{:S(2)}) copy-start(bf16[5120,128]{1,0:T(8,128)(2,1)} %weight_ref.1) | copy-start | bytes 3932164
  4.1 7.2 %collective-permute-start.3 = (f32[1280,128]{1,0:T(8,128)S(1)}, f32[1280,128]{1,0:T(8,128)S(1)}, u32[]{:S(2)}, u32[]{:S(2)}) collective-permute-start(f32[1280,128]{1,0:T(8,128)S(1)} %get-tuple-element.66), channel_id=1, source_target_pairs={{0,1},{1,0},{2,3},{3,2},{4,5},{5,4},{6,7},{7,6},{8,9},{9,8},{10,11... | collective-permute-start | bytes 1966088 | tf_op jit(solution)/shard_map/ppermute | solution.py:153
  5.0 7.9 %collective-permute-start.2 = (f32[640,128]{1,0:T(8,128)S(1)}, f32[640,128]{1,0:T(8,128)S(1)}, u32[]{:S(2)}, u32[]{:S(2)}) collective-permute-start(f32[640,128]{1,0:T(8,128)S(1)} %get-tuple-element.55), channel_id=1, source_target_pairs={{0,2},{1,5},{2,0},{3,7},{4,6},{5,1},{6,4},{7,3},{8,10},{9,13},{10,... | collective-permute-start | bytes 983048 | tf_op jit(solution)/shard_map/ppermute | solution.py:306
  7.9 7.2 %collective-permute-start.7 = (f32[640,128]{1,0:T(8,128)S(1)}, f32[640,128]{1,0:T(8,128)S(1)}, u32[]{:S(2)}, u32[]{:S(2)}) collective-permute-start(f32[640,128]{1,0:T(8,128)S(1)} %get-tuple-element.75), channel_id=1, source_target_pairs={{0,8},{1,5},{2,10},{3,7},{4,12},{5,1},{6,14},{7,3},{8,0},{9,13},{1... | collective-permute-start | bytes 983048 | tf_op jit(solution)/shard_map/ppermute | solution.py:306
  11.3 10.9 %collective-permute-start.6 = (f32[136,128]{1,0:T(8,128)S(1)}, f32[136,128]{1,0:T(8,128)S(1)}, u32[]{:S(2)}, u32[]{:S(2)}) collective-permute-start(f32[136,128]{1,0:T(8,128)S(1)} %get-tuple-element.69), channel_id=1, source_target_pairs={{0,1},{1,0},{2,3},{3,2},{4,5},{5,4},{6,7},{7,6},{8,9},{9,8},{10,11... | collective-permute-start | bytes 208904 | tf_op jit(solution)/shard_map/ppermute | solution.py:153
  13.0 5.4 %collective-permute-start.4 = (f32[320,128]{1,0:T(8,128)S(1)}, f32[320,128]{1,0:T(8,128)S(1)}, u32[]{:S(2)}, u32[]{:S(2)}) collective-permute-start(f32[320,128]{1,0:T(8,128)S(1)} %get-tuple-element.82), channel_id=1, source_target_pairs={{0,4},{1,3},{2,6},{3,1},{4,0},{5,7},{6,2},{7,5},{8,12},{9,11},{10,... | collective-permute-start | bytes 491528 | tf_op jit(solution)/shard_map/ppermute | solution.py:306
  15.2 5.4 %collective-permute-start.8 = (f32[320,128]{1,0:T(8,128)S(1)}, f32[320,128]{1,0:T(8,128)S(1)}, u32[]{:S(2)}, u32[]{:S(2)}) collective-permute-start(f32[320,128]{1,0:T(8,128)S(1)} %get-tuple-element.80), channel_id=1, source_target_pairs={{0,2},{1,9},{2,0},{3,11},{4,6},{5,13},{6,4},{7,15},{8,10},{9,1},{1... | collective-permute-start | bytes 491528 | tf_op jit(solution)/shard_map/ppermute | solution.py:306
  18.4 4.6 %collective-permute-start.5 = (f32[160,128]{1,0:T(8,128)S(1)}, f32[160,128]{1,0:T(8,128)S(1)}, u32[]{:S(2)}, u32[]{:S(2)}) collective-permute-start(f32[160,128]{1,0:T(8,128)S(1)} %get-tuple-element.84), channel_id=1, source_target_pairs={{0,8},{1,9},{2,10},{3,11},{4,12},{5,13},{6,14},{7,15},{8,0},{9,1},... | collective-permute-start | bytes 245768 | tf_op jit(solution)/shard_map/ppermute | solution.py:306
  20.6 4.5 %collective-permute-start.9 = (f32[160,128]{1,0:T(8,128)S(1)}, f32[160,128]{1,0:T(8,128)S(1)}, u32[]{:S(2)}, u32[]{:S(2)}) collective-permute-start(f32[160,128]{1,0:T(8,128)S(1)} %get-tuple-element.86), channel_id=1, source_target_pairs={{0,4},{1,3},{2,6},{3,1},{4,0},{5,7},{6,2},{7,5},{8,12},{9,11},{10,... | collective-permute-start | bytes 245768 | tf_op jit(solution)/shard_map/ppermute | solution.py:306
  25.1 5.4 %collective-permute-start.10 = (f32[160,128]{1,0:T(8,128)S(1)}, f32[160,128]{1,0:T(8,128)S(1)}, u32[]{:S(2)}, u32[]{:S(2)}) collective-permute-start(f32[160,128]{1,0:T(8,128)S(1)} %pad_maximum_fusion.1), channel_id=1, source_target_pairs={{0,16},{1,17},{2,18},{3,19},{4,20},{5,21},{6,22},{7,23},{8,24},{9,... | collective-permute-start | bytes 245768 | tf_op jit(solution)/shard_map/ppermute | solution.py:306
  30.6 1.3 %collective-permute-start.11 = (f32[160,128]{1,0:T(8,128)S(1)}, f32[160,128]{1,0:T(8,128)S(1)}, u32[]{:S(2)}, u32[]{:S(2)}) collective-permute-start(f32[160,128]{1,0:T(8,128)S(1)} %pad_maximum_fusion.2.mine_ref), channel_id=1, source_target_pairs={{0,1},{1,0},{2,3},{3,2},{4,5},{5,4},{6,7},{7,6},{8,9},{9,8},{10,11... | collective-permute-start | bytes 245768 | tf_op jit(solution)/shard_map/ppermute | solution.py:153
